TPU v7x, 32 devices: a whole 2x2x4 slice. The times are simulated.
32 devices in a mesh: seq: 16 (over z, y, core), head: 2 (over x).
Axes of the slice: x: 2, y: 2, z: 4, core: 2. Of those that a mesh axis runs over, the one named last changes fastest.
Arguments:
- inputs: bfloat16 [6, 2048, 768], P(None, 'seq'), may hold values from -6 to 6
- attend_weight: bfloat16 [3, 768, 768], P(None, 'seq', 'head'), may hold values from -0.21875 to 0.21875
- merge_weight: bfloat16 [768, 768], P('head', 'seq'), may hold values from -0.21875 to 0.21875
- expand_weight: bfloat16 [768, 3072], P('seq', 'head'), may hold values from -0.21875 to 0.21875
- reduce_weight: bfloat16 [3072, 768], P('head', 'seq'), may hold values from -0.109375 to 0.109375
- gain_first: float32 [768], replicated, may hold values from 0.1 to 1.9
- gain_heads: float32 [768], P('head'), may hold values from 0.1 to 1.9
- gain_second: float32 [768], replicated, may hold values from 0.1 to 1.9
- gain_hidden: float32 [3072], P('head'), may hold values from 0.1 to 1.9
- cotangent: bfloat16 [6, 2048, 768], P(None, 'seq'), may hold values from -6 to 6
- lengths: int32 [6], replicated, may hold values from 1024 to 2048, as said below
- local_span: int32 [6], replicated, may hold values from 32 to 128, as said below
- dilation: int32 [6], replicated, may hold values from 8 to 16, as said below
Outputs:
- block_out: bfloat16 [6, 2048, 768], P(None, 'seq')
- grad_inputs: bfloat16 [6, 2048, 768], P(None, 'seq')
- grad_attend: float32 [3, 768, 768], P(None, 'seq', 'head')
- grad_merge: float32 [768, 768], P('head', 'seq')
- grad_expand: float32 [768, 3072], P('seq', 'head')
- grad_reduce: float32 [3072, 768], P('head', 'seq')
- grad_first: float32 [768], replicated
- grad_heads: float32 [768], P('head')
- grad_second: float32 [768], replicated
- grad_hidden: float32 [3072], P('head')
Inputs may be any that keep to these rules, and one draw needn't show every extreme that they name: `lengths`: some row is full, 2048 tokens long. `local_span`: each value divides 128; 128, 64 and 32 each occur. `dilation`: each value is 8 or 16; both occur.
All inputs are finite; a program needn't handle non-finite values.
Results may differ from a plain program's by a relative error of at most 0.02.
Values may be sent and summed in bfloat16 or wider, within the bound.
No kernel may reach another device: no remote copies, remote signals or barrier semaphores. Data moves between devices by JAX's collectives and lax.ppermute only.
A program may use at most 192 MiB of HBM per device.

v0:
```python
from functools import partial

import jax
import jax.numpy as jnp
from jax import lax
from jax.sharding import PartitionSpec as P

HD = 64
DILATION_SMALL = 8


NORM_EPSILON = 1e-05
MASKED_SCORE = -1e30
PRECISE = lax.Precision.HIGHEST


def row_norm(values):
    center = jnp.mean(values, axis=-1, keepdims=True)
    spread = jnp.mean(values * values, axis=-1, keepdims=True) - center * center
    inverse = lax.rsqrt(spread + NORM_EPSILON)
    return ((values - center) * inverse, inverse)


def row_norm_back(incoming, normal, inverse, gain_row):
    scaled = incoming * gain_row
    first_mean = jnp.mean(scaled, axis=-1, keepdims=True)
    second_mean = jnp.mean(scaled * normal, axis=-1, keepdims=True)
    return inverse * (scaled - first_mean - normal * second_mean)


def feature_totals(first_term, second_term):
    return lax.psum((first_term, second_term), "head")


def head_norm(values, feature_count):
    total_one, total_two = feature_totals(
        jnp.sum(values, axis=-1), jnp.sum(values * values, axis=-1)
    )
    center = (total_one / feature_count)[:, None]
    spread = (total_two / feature_count)[:, None] - center * center
    inverse = lax.rsqrt(spread + NORM_EPSILON)
    return ((values - center) * inverse, inverse)


def head_norm_back(incoming, normal, inverse, gain_row, feature_count):
    scaled = incoming * gain_row
    total_one, total_two = feature_totals(
        jnp.sum(scaled, axis=-1), jnp.sum(scaled * normal, axis=-1)
    )
    return inverse * (
        scaled
        - (total_one / feature_count)[:, None]
        - normal * (total_two / feature_count)[:, None]
    )


def head_total(partial_sum):
    return lax.psum(partial_sum.astype(jnp.bfloat16), "head").astype(jnp.float32)


def causal_pairs(active_count, query_dev, query_slot, key_dev, key_slot):
    query_live = query_slot[None, :, None] < active_count[:, None, None]
    key_live = key_slot[None, None, :] < active_count[:, None, None]
    earlier = (key_dev[None, :] < query_dev[:, None]) | (key_dev[None, :] == query_dev[:, None]) & (
        key_slot[None, :] <= query_slot[:, None]
    )
    return query_live & key_live & earlier[None]


def at_slots(tensor, slot_clamp):
    indices = slot_clamp.reshape(slot_clamp.shape + (1,) * (tensor.ndim - 3))
    return jnp.take_along_axis(tensor, indices, axis=2)


def per_device(
    inputs,
    attend_weight,
    merge_weight,
    expand_weight,
    reduce_weight,
    gain_first,
    gain_heads,
    gain_second,
    gain_hidden,
    cotangent,
    lengths,
    local_span,
    dilation,
):
    row_count, for_each_row, model_width = inputs.shape
    tokens = row_count * for_each_row
    heads_here = attend_weight.shape[2] // HD
    hidden_width = expand_weight.shape[1] * lax.axis_size("head")
    attend_width = heads_here * HD * lax.axis_size("head")
    slot_number_count = for_each_row // DILATION_SMALL
    score_scale = HD ** (-0.5)
    seq_index = lax.axis_index("seq")
    full_weights = (
        lax.all_gather(attend_weight, "seq", axis=1, tiled=True),
        lax.all_gather(merge_weight, "seq", axis=1, tiled=True),
        lax.all_gather(expand_weight, "seq", axis=0, tiled=True),
        lax.all_gather(reduce_weight, "seq", axis=1, tiled=True),
    )
    attend_all, merge_all, expand_all, reduce_all = full_weights
    flat_in = inputs.reshape(tokens, model_width).astype(jnp.float32)
    normal_one, inverse_one = row_norm(flat_in)
    first_in = (normal_one * gain_first).astype(jnp.bfloat16)
    projected = jnp.einsum(
        "td,edf->etf", first_in, attend_all, preferred_element_type=jnp.float32
    ).astype(jnp.bfloat16)
    by_head = projected.reshape(3, row_count, for_each_row, heads_here, HD).transpose(0, 1, 3, 2, 4)
    queries, keys_here, values_here = (by_head[0], by_head[1], by_head[2])
    places = jnp.arange(for_each_row)
    span_block = places[None, :] // local_span[:, None]
    within = (span_block[:, :, None] == span_block[:, None, :]) & (
        places[None, :] <= places[:, None]
    )[None]

    def near_scores():
        raw_score = (
            jnp.einsum("rhid,rhjd->rhij", queries, keys_here, preferred_element_type=jnp.float32)
            * score_scale
        )
        return jnp.where(within[:, None], raw_score, MASKED_SCORE)

    score_near = near_scores()
    peak_near = jnp.max(score_near, axis=-1)
    expo_near = jnp.exp(score_near - peak_near[..., None])
    total_near = jnp.sum(expo_near, axis=-1)
    accum_near = jnp.einsum(
        "rhij,rhjd->rhid",
        expo_near.astype(jnp.bfloat16),
        values_here,
        preferred_element_type=jnp.float32,
    )
    head_ids = lax.axis_index("head") * heads_here + jnp.arange(heads_here)
    slot_index = jnp.arange(slot_number_count)
    slot_place = (head_ids[None, :] % dilation[:, None])[..., None] + dilation[
        :, None, None
    ] * slot_index
    active_count = for_each_row // dilation
    slot_clamp = jnp.minimum(slot_place, for_each_row - 1)
    slot_table = (
        (slot_clamp[..., None] == places)
        & (slot_index[None, :] < active_count[:, None])[:, None, :, None]
    ).astype(jnp.float32)
    query_slot = at_slots(queries, slot_clamp)
    key_slot = at_slots(keys_here, slot_clamp)
    value_slot = at_slots(values_here, slot_clamp)
    pairs_send = jnp.concatenate([key_slot, value_slot], axis=-1).transpose(2, 0, 1, 3)
    own_dev = jnp.full((slot_number_count,), seq_index)
    key_piece = lax.all_gather(pairs_send, "seq", axis=0, tiled=True)
    peak_run = at_slots(peak_near, slot_clamp)
    total_run = at_slots(total_near, slot_clamp)
    accum_run = at_slots(accum_near, slot_clamp)
    key_order = jnp.arange(key_piece.shape[0])
    allowed = causal_pairs(
        active_count,
        own_dev,
        slot_index,
        key_order // slot_number_count,
        key_order % slot_number_count,
    )
    raw_score = (
        jnp.einsum(
            "rhad,prhd->rhap", query_slot, key_piece[..., :HD], preferred_element_type=jnp.float32
        )
        * score_scale
    )
    raw_score = jnp.where(allowed[:, None], raw_score, MASKED_SCORE)
    peak_new = jnp.maximum(peak_run, jnp.max(raw_score, axis=-1))
    expo_far = jnp.exp(raw_score - peak_new[..., None])
    factor = jnp.exp(peak_run - peak_new)
    total_new = total_run * factor + jnp.sum(expo_far, axis=-1)
    accum_new = accum_run * factor[..., None] + jnp.einsum(
        "rhap,prhd->rhad",
        expo_far.astype(jnp.bfloat16),
        key_piece[..., HD:],
        preferred_element_type=jnp.float32,
    )
    log_near = peak_near + jnp.log(total_near)
    log_far = peak_new + jnp.log(total_new)
    chosen = jnp.sum(slot_table, axis=2) > 0
    log_all = jnp.where(
        chosen, jnp.einsum("rhsc,rhs->rhc", slot_table, log_far, precision=PRECISE), log_near
    )
    mixed_out = jnp.where(
        chosen[..., None],
        jnp.einsum(
            "rhsc,rhsd->rhcd", slot_table, accum_new / total_new[..., None], precision=PRECISE
        ),
        accum_near / total_near[..., None],
    )
    attended = mixed_out.transpose(0, 2, 1, 3).reshape(tokens, heads_here * HD)
    normal_heads, inverse_heads = head_norm(attended, attend_width)
    heads_in = (normal_heads * gain_heads).astype(jnp.bfloat16)
    residual = flat_in + head_total(
        jnp.dot(heads_in, merge_all, preferred_element_type=jnp.float32)
    )
    normal_two, inverse_two = row_norm(residual)
    second_in = (normal_two * gain_second).astype(jnp.bfloat16)
    hidden_pre = jnp.dot(second_in, expand_all, preferred_element_type=jnp.float32)
    activated, gelu_back = jax.vjp(partial(jax.nn.gelu, approximate=False), hidden_pre)
    normal_hidden, inverse_hidden = head_norm(activated, hidden_width)
    hidden_in = (normal_hidden * gain_hidden).astype(jnp.bfloat16)
    block_out = residual + head_total(
        jnp.dot(hidden_in, reduce_all, preferred_element_type=jnp.float32)
    )
    attend_back, merge_back, expand_back, reduce_back = full_weights
    in_length = (seq_index * for_each_row + places)[None, :] < lengths[:, None]
    seed_grad = jnp.where(in_length[..., None], cotangent, jnp.zeros((), jnp.bfloat16)).reshape(
        tokens, model_width
    )
    grad_reduce = jnp.einsum("tf,td->fd", hidden_in, seed_grad, preferred_element_type=jnp.float32)
    grad_hidden_in = jnp.einsum(
        "td,fd->tf", seed_grad, reduce_back, preferred_element_type=jnp.float32
    )
    grad_hidden = jnp.sum(grad_hidden_in * normal_hidden, axis=0)
    grad_activated = head_norm_back(
        grad_hidden_in, normal_hidden, inverse_hidden, gain_hidden, hidden_width
    )
    grad_pre = gelu_back(grad_activated)[0].astype(jnp.bfloat16)
    grad_expand = jnp.einsum("td,tf->df", second_in, grad_pre, preferred_element_type=jnp.float32)
    grad_second_in = head_total(
        jnp.einsum("tf,df->td", grad_pre, expand_back, preferred_element_type=jnp.float32)
    )
    grad_second = jnp.sum(grad_second_in * normal_two, axis=0)
    grad_resid = seed_grad.astype(jnp.float32) + row_norm_back(
        grad_second_in, normal_two, inverse_two, gain_second
    )
    resid_low = grad_resid.astype(jnp.bfloat16)
    grad_merge = jnp.einsum("tf,td->fd", heads_in, resid_low, preferred_element_type=jnp.float32)
    grad_heads_in = jnp.einsum(
        "td,fd->tf", resid_low, merge_back, preferred_element_type=jnp.float32
    )
    grad_heads = jnp.sum(grad_heads_in * normal_heads, axis=0)
    grad_attended = head_norm_back(
        grad_heads_in, normal_heads, inverse_heads, gain_heads, attend_width
    )
    grad_mixed = (
        grad_attended.astype(jnp.bfloat16)
        .reshape(row_count, for_each_row, heads_here, HD)
        .transpose(0, 2, 1, 3)
    )
    row_dot = jnp.sum(grad_mixed.astype(jnp.float32) * mixed_out, axis=-1)
    weight_near = jnp.exp(near_scores() - log_all[..., None])
    grad_weight = jnp.einsum(
        "rhid,rhjd->rhij", grad_mixed, values_here, preferred_element_type=jnp.float32
    )
    grad_score = (weight_near * (grad_weight - row_dot[..., None])).astype(jnp.bfloat16)
    grad_queries = (
        jnp.einsum("rhij,rhjd->rhid", grad_score, keys_here, preferred_element_type=jnp.float32)
        * score_scale
    )
    grad_keys = (
        jnp.einsum("rhij,rhid->rhjd", grad_score, queries, preferred_element_type=jnp.float32)
        * score_scale
    )
    grad_values = jnp.einsum(
        "rhij,rhid->rhjd",
        weight_near.astype(jnp.bfloat16),
        grad_mixed,
        preferred_element_type=jnp.float32,
    )
    grad_slot = at_slots(grad_mixed, slot_clamp)
    log_slot = at_slots(log_all, slot_clamp)
    dot_slot = at_slots(row_dot, slot_clamp)
    pairs_all = lax.all_gather(pairs_send, "seq", axis=0, tiled=True)
    key_order = jnp.arange(pairs_all.shape[0])
    allowed_all = causal_pairs(
        active_count,
        own_dev,
        slot_index,
        key_order // slot_number_count,
        key_order % slot_number_count,
    )
    raw_far = (
        jnp.einsum(
            "rhad,prhd->rhap", query_slot, pairs_all[..., :HD], preferred_element_type=jnp.float32
        )
        * score_scale
    )
    weight_far = jnp.exp(
        jnp.where(allowed_all[:, None], raw_far - log_slot[..., None], MASKED_SCORE)
    )
    grad_weight_far = jnp.einsum(
        "rhad,prhd->rhap", grad_slot, pairs_all[..., HD:], preferred_element_type=jnp.float32
    )
    grad_score_far = (weight_far * (grad_weight_far - dot_slot[..., None])).astype(jnp.bfloat16)
    grad_query_slot = (
        jnp.einsum(
            "rhap,prhd->rhad",
            grad_score_far,
            pairs_all[..., :HD],
            preferred_element_type=jnp.float32,
        )
        * score_scale
    )
    log_every, dot_every = (
        lax.all_gather(log_slot.transpose(2, 0, 1), "seq", axis=0, tiled=True),
        lax.all_gather(dot_slot.transpose(2, 0, 1), "seq", axis=0, tiled=True),
    )
    query_pairs = jnp.concatenate([query_slot, grad_slot], axis=-1).transpose(2, 0, 1, 3)
    query_piece = lax.all_gather(query_pairs, "seq", axis=0, tiled=True)
    row_total = query_piece.shape[0]
    query_order = jnp.arange(row_total)
    log_piece = log_every.transpose(1, 2, 0)
    dot_piece = dot_every.transpose(1, 2, 0)
    allowed = causal_pairs(
        active_count,
        query_order // slot_number_count,
        query_order % slot_number_count,
        own_dev,
        slot_index,
    )
    raw_score = (
        jnp.einsum(
            "prhd,rhbd->rhpb", query_piece[..., :HD], key_slot, preferred_element_type=jnp.float32
        )
        * score_scale
    )
    weight_here = jnp.exp(
        jnp.where(allowed[:, None], raw_score - log_piece[..., None], MASKED_SCORE)
    )
    grad_here = jnp.einsum(
        "prhd,rhbd->rhpb", query_piece[..., HD:], value_slot, preferred_element_type=jnp.float32
    )
    score_here = (weight_here * (grad_here - dot_piece[..., None])).astype(jnp.bfloat16)
    key_portion = (
        jnp.einsum(
            "rhpb,prhd->brhd", score_here, query_piece[..., :HD], preferred_element_type=jnp.float32
        )
        * score_scale
    )
    value_part = jnp.einsum(
        "rhpb,prhd->brhd",
        weight_here.astype(jnp.bfloat16),
        query_piece[..., HD:],
        preferred_element_type=jnp.float32,
    )
    pair_grads = jnp.concatenate([key_portion, value_part], axis=-1)
    pair_grads_t = pair_grads.transpose(1, 2, 0, 3)
    grad_queries = grad_queries + jnp.einsum(
        "rhsc,rhsd->rhcd", slot_table, grad_query_slot, precision=PRECISE
    )
    grad_keys = grad_keys + jnp.einsum(
        "rhsc,rhsd->rhcd", slot_table, pair_grads_t[..., :HD], precision=PRECISE
    )
    grad_values = grad_values + jnp.einsum(
        "rhsc,rhsd->rhcd", slot_table, pair_grads_t[..., HD:], precision=PRECISE
    )
    grad_project = (
        jnp.stack([grad_queries, grad_keys, grad_values])
        .astype(jnp.bfloat16)
        .transpose(0, 1, 3, 2, 4)
        .reshape(3, tokens, heads_here * HD)
    )
    grad_attend = jnp.einsum(
        "td,etf->edf", first_in, grad_project, preferred_element_type=jnp.float32
    )
    grad_first_in = head_total(
        jnp.einsum("etf,edf->td", grad_project, attend_back, preferred_element_type=jnp.float32)
    )
    grad_first = jnp.sum(grad_first_in * normal_one, axis=0)
    grad_inputs = grad_resid + row_norm_back(grad_first_in, normal_one, inverse_one, gain_first)
    weight_grads = (
        lax.psum_scatter(grad_attend, "seq", scatter_dimension=1, tiled=True),
        lax.psum_scatter(grad_merge, "seq", scatter_dimension=1, tiled=True),
        lax.psum_scatter(grad_expand, "seq", scatter_dimension=0, tiled=True),
        lax.psum_scatter(grad_reduce, "seq", scatter_dimension=1, tiled=True),
    )
    gain_grads = lax.psum((grad_first, grad_heads, grad_second, grad_hidden), "seq")
    return (
        block_out.reshape(row_count, for_each_row, model_width).astype(jnp.bfloat16),
        grad_inputs.reshape(row_count, for_each_row, model_width).astype(jnp.bfloat16),
        weight_grads[0],
        weight_grads[1],
        weight_grads[2],
        weight_grads[3],
        gain_grads[0],
        gain_grads[1],
        gain_grads[2],
        gain_grads[3],
    )


def solution(mesh):
    placed = (
        P(None, "seq", None),
        P(None, "seq", "head"),
        P("head", "seq"),
        P("seq", "head"),
        P("head", "seq"),
        P(),
        P("head"),
        P(),
        P("head"),
        P(None, "seq", None),
        P(),
        P(),
        P(),
    )
    return jax.shard_map(
        per_device,
        mesh=mesh,
        in_specs=placed,
        out_specs=(
            P(None, "seq", None),
            P(None, "seq", None),
            P(None, "seq", "head"),
            P("head", "seq"),
            P("seq", "head"),
            P("head", "seq"),
            P(),
            P("head"),
            P(),
            P("head"),
        ),
        check_vma=False,
    )
```

profile of v0, /device:TPU:0, one launch (start us, length us, event | category | flops | bytes accessed | tf_op | source)
XLA Modules:
  0.0 924.3 jit_solution(15141655809107991478)
XLA Ops:
  14.6 38.8 %all-gather.6.cloned.1.call-done = bf16[3,768,384]{2,1,0:T(8,128)(2,1)} async-done(((bf16[3,48,384]{2,1,0:T(8,128)(2,1)}), bf16[3,768,384]{2,1,0:T(8,128)(2,1)}) %all-gather.6.cloned.1.call-update) | async-done | bytes 1769488 | tf_op jit(solution)/shard_map/all_gather | solution.py:99
  53.5 3.2 convert_bitcast_fusion
  56.7 4.7 reshape.866
  61.4 4.9 copy.98
  71.5 8.6 gather_fusion.2
  80.1 11.7 %gather_fusion.3 = bf16[576,64]{1,0:T(8,128)(2,1)S(1)} fusion(bf16[6,6,128,64]{3,2,1,0:T(8,128)(2,1)} %copy.102, s32[576]{0:T(1024)S(1)} %reshape.799), kind=kCustom, calls=%fused_computation.5.clone | custom fusion | bytes 154368 | tf_op jit(solution)/shard_map/jit(take_along_axis)/gather | solution.py:72
  93.5 10.3 %gather_fusion.4 = bf16[576,64]{1,0:T(8,128)(2,1)} fusion(bf16[6,6,128,64]{3,2,1,0:T(8,128)(2,1)S(1)} %copy.103, s32[576]{0:T(1024)S(1)} %reshape.799), kind=kCustom, calls=%fused_computation.6.clone | custom fusion | bytes 154368 | tf_op jit(solution)/shard_map/jit(take_along_axis)/gather | solution.py:72
  107.5 27.3 %all_gather.27 = bf16[384,768]{0,1:T(8,128)(2,1)S(1)} all-gather(bf16[384,48]{0,1:T(8,128)(2,1)S(1)} %copy-done.49), channel_id=1, replica_groups=mesh['seq'=16,'head'=2] {'seq'}, dimensions={1}, use_global_device_ids=true | all-gather | bytes 626688 | tf_op jit(solution)/shard_map/all_gather | solution.py:100
  136.9 3.7 gather_fusion.1
  142.9 3.7 gather_fusion.5
  146.7 3.2 fusion.97
  149.8 2.9 copy.100
  152.7 8.8 gather_fusion
  169.4 5.0 all-reduce.5
  180.8 40.7 %all-reduce.12.cloned.1.call-done = bf16[768,768]{1,0:T(8,128)(2,1)} async-done(((bf16[768,768]{1,0:T(8,128)(2,1)}), bf16[768,768]{1,0:T(8,128)(2,1)}) %all-reduce.12.cloned.1.call-update) | async-done | bytes 1179664 | tf_op jit(solution)/shard_map/psum | solution.py:58
  225.2 40.8 %all-gather.10.cloned.1.call-done = bf16[768,1536]{1,0:T(8,128)(2,1)} async-done(((bf16[48,1536]{1,0:T(8,128)(2,1)}), bf16[768,1536]{1,0:T(8,128)(2,1)}) %all-gather.10.cloned.1.call-update) | async-done | bytes 2359312 | tf_op jit(solution)/shard_map/all_gather | solution.py:101
  266.1 16.3 %fusion.194 = (f32[768]{0:T(1024)S(1)}, f32[768]{0:T(1024)S(1)}, f32[768,1536]{1,0:T(8,128)}, f32[768,1536]{1,0:T(8,128)}, f32[768,1536]{1,0:T(8,128)}) fusion(bf16[768,1536]{1,0:T(8,128)(2,1)} %all-gather.10.cloned.1.call-done, f32[768,768]{1,0:T(8,128)} %subtract_multiply_fusion.1, f32[768]{0:T(1024)S(1)} %copy-done.56), kind=kOutput, calls=%fused_computation.284 | convolution fusion | flops 1892153856 | bytes 18883584 | tf_op jit(solution)/shard_map/dot_general | solution.py:202
  282.4 5.0 all-reduce.4
  287.4 22.1 %all-gather.12.cloned.1.call-done = bf16[1536,768]{0,1:T(8,128)(2,1)} async-done(((bf16[1536,48]{0,1:T(8,128)(2,1)}), bf16[1536,768]{0,1:T(8,128)(2,1)}) %all-gather.12.cloned.1.call-update) | async-done | bytes 2359312 | tf_op jit(solution)/shard_map/all_gather | solution.py:102
  309.5 8.4 multiply_reduce_fusion
  317.9 5.0 all-reduce.3
  322.9 9.5 %add_convert_fusion = (bf16[768,1536]{1,0:T(8,128)(2,1)S(1)}, bf16[768,1536]{1,0:T(8,128)(2,1)}) fusion(f32[768,1536]{1,0:T(8,128)} %get-tuple-element.92, f32[768,1536]{1,0:T(8,128)} %get-tuple-element.126, f32[768,1536]{1,0:T(8,128)} %get-tuple-element.127, f32[768,1536]{1,0:T(8,128)} %get-tuple-element.91, f32[768]{0:T(1024)S(1)} %broadcast_multiply_fusion, ...), kind=kLoop, calls=%fused_computation.12 | loop fusion | flops 27131904 | bytes 23611392 | tf_op jit(solution)/shard_map/convert_element_type | solution.py:222
  333.8 3.0 convolution_convert_fusion.1
  337.1 41.6 %all-reduce.14.cloned.1.call-done = bf16[768,768]{1,0:T(8,128)(2,1)} async-done(((bf16[768,768]{1,0:T(8,128)(2,1)}), bf16[768,768]{1,0:T(8,128)(2,1)}) %all-reduce.14.cloned.1.call-update) | async-done | bytes 1179664 | tf_op jit(solution)/shard_map/psum | solution.py:58
  378.8 3.5 fusion.16
  386.9 5.0 all-reduce.2
  395.1 8.6 gather_fusion.7
  407.0 3.7 gather_fusion.6
  412.6 3.7 gather_fusion.8
  416.6 26.3 %all_gather.31 = f32[256,6,6]{2,1,0:T(8,128)S(1)} all-gather(f32[16,6,6]{2,1,0:T(8,128)S(1)} %copy.113), channel_id=1, replica_groups=mesh['seq'=16,'head'=2] {'seq'}, dimensions={0}, use_global_device_ids=true | all-gather | bytes 39168 | tf_op jit(solution)/shard_map/all_gather | solution.py:300
  443.9 21.1 %all_gather.32 = f32[256,6,6]{2,1,0:T(8,128)S(1)} all-gather(f32[16,6,6]{2,1,0:T(8,128)S(1)} %copy.116), channel_id=1, replica_groups=mesh['seq'=16,'head'=2] {'seq'}, dimensions={0}, use_global_device_ids=true | all-gather | bytes 39168 | tf_op jit(solution)/shard_map/all_gather | solution.py:301
  466.0 3.9 fusion.113
  484.0 2.9 fusion.123
  493.9 3.3 reshape.746
  497.1 5.1 convolution_bitcast_fusion
  502.2 6.2 copy.121
  510.2 4.9 convolution_convert_fusion.2
  515.0 2.8 bitcast_convert_fusion
  519.5 3.4 fusion.133
  522.9 6.7 fusion.139
  529.7 6.2 fusion.200
  537.8 86.7 %all-reduce.16.cloned.1.call-done = f32[3,768,384]{2,0,1:T(4,128)} async-done(((f32[3,768,384]{2,0,1:T(4,128)}), f32[3,768,384]{2,0,1:T(4,128)}) %all-reduce.16.cloned.1.call-update) | async-done | bytes 3538960
  626.2 69.8 %all-reduce.18.cloned.1.call-done = (bf16[768,768]{1,0:T(8,128)(2,1)}, bf16[768,768]{1,0:T(8,128)(2,1)}) async-done(((bf16[768,768]{1,0:T(8,128)(2,1)}, bf16[768,768]{1,0:T(8,128)(2,1)}), (bf16[768,768]{1,0:T(8,128)(2,1)}, bf16[768,768]{1,0:T(8,128)(2,1)})) %all-reduce.18.cloned.1.call-update) | async-done | bytes 2359312 | tf_op jit(solution)/shard_map/psum | solution.py:58
  696.0 3.1 fusion.22
  699.1 61.3 %all-reduce.1 = (f32[768]{0:T(1024)}, f32[384]{0:T(512)}, f32[768]{0:T(1024)}, f32[1536]{0:T(1024)}) all-reduce(f32[768]{0:T(1024)} %get-tuple-element.61, f32[384]{0:T(512)} %get-tuple-element.59, f32[768]{0:T(1024)} %get-tuple-element.57, f32[1536]{0:T(1024)} %get-tuple-element.52), channel_id=1, replica_groups=mesh['seq'=16,'head'=2] {'seq'}, use_global_device_ids=true, to_apply=%region_39.42 | all-reduce | flops 3456 | bytes 27648 | tf_op jit(solution)/shard_map/psum | solution.py:372
  761.1 3.7 fusion.20
  764.8 73.3 %reduce-scatter.6.cloned.1.call-done = f32[48,1536]{1,0:T(8,128)} async-done(((f32[768,1536]{1,0:T(8,128)}), f32[48,1536]{1,0:T(8,128)}) %reduce-scatter.6.cloned.1.call-update) | async-done | bytes 294928 | tf_op jit(solution)/shard_map/reduce_scatter | solution.py:369
  838.1 78.9 %reduce-scatter.8.cloned.1.call-done = f32[1536,48]{0,1:T(8,128)} async-done(((f32[1536,768]{0,1:T(8,128)}), f32[1536,48]{0,1:T(8,128)}) %reduce-scatter.8.cloned.1.call-update) | async-done | bytes 294928 | tf_op jit(solution)/shard_map/reduce_scatter | solution.py:370
  (258 shorter events, 84.5 us)
Async XLA Ops:
  7.2 46.3 %all-gather.6.cloned.1.call-start = ((), (), s32[]{:S(2)}) async-start(), calls=%async_computation.3 | async-start | bytes 1880064 | tf_op jit(solution)/shard_map/all_gather | solution.py:99
  7.9 153.6 %all-gather.8.cloned.1.call-start = ((), (), s32[]{:S(2)}) async-start(), calls=%async_computation.4 | async-start | bytes 2506752 | tf_op jit(solution)/shard_map/all_gather | solution.py:152
  12.2 44.4 %copy-start.37 = (f32[768]{0:T(1024)}, f32[768]{0:T(1024)S(1)}, u32[]{:S(2)}) copy-start(f32[768]{0:T(1024)S(1)} %fusion.186) | copy-start | bytes 9220
  12.3 91.5 %copy-start.41 = (pred[6,6,16]{2,1,0:T(8,128)(4,1)}, pred[6,6,16]{2,1,0:T(8,128)(4,1)S(1)}, u32[]{:S(2)}) copy-start(pred[6,6,16]{2,1,0:T(8,128)(4,1)S(1)} %fusion.178) | copy-start | bytes 1732
  12.9 43.7 %copy-start.39 = (f32[768]{0:T(1024)}, f32[768]{0:T(1024)S(1)}, u32[]{:S(2)}) copy-start(f32[768]{0:T(1024)S(1)} %get-tuple-element.111) | copy-start | bytes 9220
  66.2 80.4 %copy-start.7 = (bf16[3,6,128,6,64]{2,4,3,1,0:T(8,128)(2,1)}, bf16[3,6,128,6,64]{2,4,3,1,0:T(8,128)(2,1)S(1)}, u32[]{:S(2)}) copy-start(bf16[3,6,128,6,64]{2,4,3,1,0:T(8,128)(2,1)S(1)} %copy.98) | copy-start | bytes 5308420
  91.8 14.6 %copy-start.64 = (s32[6]{0:T(128)S(1)}, s32[6]{0:T(128)}, u32[]{:S(2)}) copy-start(s32[6]{0:T(128)} %param.28) | copy-start | bytes 76
  91.8 15.7 %copy-start.49 = (bf16[384,48]{0,1:T(8,128)(2,1)S(1)}, bf16[384,48]{0,1:T(8,128)(2,1)}, u32[]{:S(2)}) copy-start(bf16[384,48]{0,1:T(8,128)(2,1)} %param.19) | copy-start | bytes 110596
  106.4 115.0 %all-reduce.12.cloned.1.call-start = ((), (), s32[]{:S(2)}) async-start(), calls=%async_computation.5 | async-start | bytes 2359296 | tf_op jit(solution)/shard_map/psum | solution.py:58
  106.6 34.1 %copy-start.60 = (s32[256]{0:T(256)}, s32[256]{0:T(256)S(1)}, u32[]{:S(2)}) copy-start(s32[256]{0:T(256)S(1)} %and_select_fusion.1) | copy-start | bytes 3076
  106.7 59.7 %copy-start.45 = (pred[6,16]{1,0:T(8,128)(4,1)}, pred[6,16]{1,0:T(8,128)(4,1)S(1)}, u32[]{:S(2)}) copy-start(pred[6,16]{1,0:T(8,128)(4,1)S(1)} %iota_compare_fusion.4) | copy-start | bytes 292
  106.8 59.6 %copy-start.27 = (s32[6,6,16]{2,1,0:T(8,128)}, s32[6,6,16]{2,1,0:T(8,128)S(1)}, u32[]{:S(2)}) copy-start(s32[6,6,16]{2,1,0:T(8,128)S(1)} %add_minimum_fusion) | copy-start | bytes 6916
  107.0 33.7 %copy-start.54 = (pred[6,256]{1,0:T(8,128)(4,1)}, pred[6,256]{1,0:T(8,128)(4,1)S(1)}, u32[]{:S(2)}) copy-start(pred[6,256]{1,0:T(8,128)(4,1)S(1)} %broadcast_compare_fusion.1) | copy-start | bytes 4612
  107.3 57.7 %copy-start.32 = (pred[6,16,256]{2,1,0:T(8,128)(4,1)}, pred[6,16,256]{2,1,0:T(8,128)(4,1)S(1)}, u32[]{:S(2)}) copy-start(pred[6,16,256]{2,1,0:T(8,128)(4,1)S(1)} %and_and_fusion.1) | copy-start | bytes 73732
  134.9 39.6 %copy-start.14 = (bf16[384,768]{0,1:T(8,128)(2,1)}, bf16[384,768]{0,1:T(8,128)(2,1)S(1)}, u32[]{:S(2)}) copy-start(bf16[384,768]{0,1:T(8,128)(2,1)S(1)} %all_gather.27) | copy-start | bytes 1769476
  168.7 5.7 copy-start.50
  169.4 222.5 %copy-start.5 = (f32[6,128,6,64]{1,0,3,2:T(8,128)}, f32[6,128,6,64]{1,0,3,2:T(8,128)S(1)}, u32[]{:S(2)}) copy-start(f32[6,128,6,64]{1,0,3,2:T(8,128)S(1)} %copy.106) | copy-start | bytes 3538948
  169.4 8.8 copy-start.63
  176.5 45.0 %copy-start = (bf16[6,128,768]{2,1,0:T(8,128)(2,1)S(1)}, bf16[6,128,768]{2,1,0:T(8,128)(2,1)}, u32[]{:S(2)}) copy-start(bf16[6,128,768]{2,1,0:T(8,128)(2,1)} %param.17) | copy-start | bytes 3538948
  176.5 89.6 %all-gather.10.cloned.1.call-start = ((), (), s32[]{:S(2)}) async-start(), calls=%async_computation.6 | async-start | bytes 2506752 | tf_op jit(solution)/shard_map/all_gather | solution.py:101
  177.1 132.4 %all-gather.12.cloned.1.call-start = ((), (), s32[]{:S(2)}) async-start(), calls=%async_computation.7 | async-start | bytes 2506752 | tf_op jit(solution)/shard_map/all_gather | solution.py:102
  177.7 201.1 %all-reduce.14.cloned.1.call-start = ((), (), s32[]{:S(2)}) async-start(), calls=%async_computation.8 | async-start | bytes 2359296 | tf_op jit(solution)/shard_map/psum | solution.py:58
  223.4 42.7 %copy-start.56 = (f32[768]{0:T(1024)S(1)}, f32[768]{0:T(1024)}, u32[]{:S(2)}) copy-start(f32[768]{0:T(1024)} %param.24) | copy-start | bytes 9220
  225.2 84.3 %copy-start.62 = (f32[1536]{0:T(1024)S(1)}, f32[1536]{0:T(1024)}, u32[]{:S(2)}) copy-start(f32[1536]{0:T(1024)} %param.25) | copy-start | bytes 18436
  322.9 10.9 %copy-start.65 = (bf16[768,1536]{1,0:T(8,128)(2,1)S(1)}, bf16[768,1536]{1,0:T(8,128)(2,1)}, u32[]{:S(2)}) copy-start(bf16[768,1536]{1,0:T(8,128)(2,1)} %all-gather.10.cloned.1.call-done) | copy-start | bytes 7077892
  336.9 142.2 %all-gather.14.cloned.1.call-start = ((), (), s32[]{:S(2)}) async-start(), calls=%async_computation.9 | async-start | bytes 2506752 | tf_op jit(solution)/shard_map/all_gather | solution.py:304
  393.5 10.2 %copy-start.42 = (pred[6,6,16]{2,1,0:T(8,128)(4,1)S(1)}, pred[6,6,16]{2,1,0:T(8,128)(4,1)}, u32[]{:S(2)}) copy-start(pred[6,6,16]{2,1,0:T(8,128)(4,1)} %copy-done.41) | copy-start | bytes 1732
  394.2 16.6 %copy-start.9 = (bf16[6,128,6,64]{1,0,3,2:T(8,128)(2,1)}, bf16[6,128,6,64]{1,0,3,2:T(8,128)(2,1)S(1)}, u32[]{:S(2)}) copy-start(bf16[6,128,6,64]{1,0,3,2:T(8,128)(2,1)S(1)} %reshape.745) | copy-start | bytes 1769476
  394.2 10.5 %copy-start.61 = (s32[256]{0:T(256)S(1)}, s32[256]{0:T(256)}, u32[]{:S(2)}) copy-start(s32[256]{0:T(256)} %copy-done.60) | copy-start | bytes 3076
  394.2 10.5 %copy-start.46 = (pred[6,16]{1,0:T(8,128)(4,1)S(1)}, pred[6,16]{1,0:T(8,128)(4,1)}, u32[]{:S(2)}) copy-start(pred[6,16]{1,0:T(8,128)(4,1)} %copy-done.45) | copy-start | bytes 292
  394.2 10.5 %copy-start.55 = (pred[6,256]{1,0:T(8,128)(4,1)S(1)}, pred[6,256]{1,0:T(8,128)(4,1)}, u32[]{:S(2)}) copy-start(pred[6,256]{1,0:T(8,128)(4,1)} %copy-done.54) | copy-start | bytes 4612
  394.2 11.2 %copy-start.35 = (f32[768]{0:T(1024)S(1)}, f32[768]{0:T(1024)}, u32[]{:S(2)}) copy-start(f32[768]{0:T(1024)} %param.22) | copy-start | bytes 9220
  394.3 11.2 %copy-start.58 = (f32[6,128]{1,0:T(8,128)S(1)}, f32[6,128]{1,0:T(8,128)}, u32[]{:S(2)}) copy-start(f32[6,128]{1,0:T(8,128)} %get-tuple-element.110) | copy-start | bytes 9220
  394.3 11.2 %copy-start.59 = (f32[6,128]{1,0:T(8,128)S(1)}, f32[6,128]{1,0:T(8,128)}, u32[]{:S(2)}) copy-start(f32[6,128]{1,0:T(8,128)} %get-tuple-element.112) | copy-start | bytes 9220
  404.7 219.9 %all-reduce.16.cloned.1.call-start = ((), (), s32[]{:S(2)}) async-start(), calls=%async_computation.13 | async-start | bytes 9437184
  416.4 49.6 %copy-start.31 = (bf16[6,6,16,64]{3,2,1,0:T(8,128)(2,1)S(1)}, bf16[6,6,16,64]{3,2,1,0:T(8,128)(2,1)}, u32[]{:S(2)}) copy-start(bf16[6,6,16,64]{3,2,1,0:T(8,128)(2,1)} %copy-done.30) | copy-start | bytes 221188
  416.4 49.6 %copy-start.33 = (pred[6,16,256]{2,1,0:T(8,128)(4,1)S(1)}, pred[6,16,256]{2,1,0:T(8,128)(4,1)}, u32[]{:S(2)}) copy-start(pred[6,16,256]{2,1,0:T(8,128)(4,1)} %copy-done.32) | copy-start | bytes 73732
  416.4 48.7 %copy-start.34 = (f32[6,6,16]{2,1,0:T(8,128)}, f32[6,6,16]{2,1,0:T(8,128)S(1)}, u32[]{:S(2)}) copy-start(f32[6,6,16]{2,1,0:T(8,128)S(1)} %get-tuple-element.106) | copy-start | bytes 6916
  466.0 5.2 copy-start.8
  486.9 5.2 copy-start.21
  508.5 187.5 %all-reduce.18.cloned.1.call-start = ((), (), s32[]{:S(2)}) async-start(), calls=%async_computation.14 | async-start | bytes 4718592 | tf_op jit(solution)/shard_map/psum | solution.py:58
  517.8 5.1 copy-start.57
  517.8 246.9 %reduce-scatter.4.cloned.1.call-start = ((), (), s32[]{:S(2)}) async-start(), calls=%async_computation.10 | async-start | bytes 1253376 | tf_op jit(solution)/shard_map/reduce_scatter | solution.py:368
  522.9 315.2 %reduce-scatter.6.cloned.1.call-start = ((), (), s32[]{:S(2)}) async-start(), calls=%async_computation.11 | async-start | bytes 5013504 | tf_op jit(solution)/shard_map/reduce_scatter | solution.py:369
  529.7 387.3 %reduce-scatter.8.cloned.1.call-start = ((), (), s32[]{:S(2)}) async-start(), calls=%async_computation.12 | async-start | bytes 5013504 | tf_op jit(solution)/shard_map/reduce_scatter | solution.py:370
  535.9 160.1 %copy-start.36 = (f32[768]{0:T(1024)S(1)}, f32[768]{0:T(1024)}, u32[]{:S(2)}) copy-start(f32[768]{0:T(1024)} %param.22) | copy-start | bytes 9220
  535.9 160.1 %copy-start.38 = (f32[768]{0:T(1024)S(1)}, f32[768]{0:T(1024)}, u32[]{:S(2)}) copy-start(f32[768]{0:T(1024)} %copy-done.37) | copy-start | bytes 9220
  535.9 160.1 %copy-start.40 = (f32[768]{0:T(1024)S(1)}, f32[768]{0:T(1024)}, u32[]{:S(2)}) copy-start(f32[768]{0:T(1024)} %copy-done.39) | copy-start | bytes 9220
  (32 other events, 86.1 us)
Sparse Core Ops, SparseCore 0:
  10.3 43.1 all-gather.5
  106.5 47.8 all-gather.7
  176.6 44.7 all-reduce.11
  223.8 42.2 all-gather.9
  268.5 40.9 all-gather.11
  337.0 41.6 all-reduce.13
  404.8 46.4 all-gather.13
  508.6 115.8 all-reduce.15
  627.5 68.4 all-reduce.17
  700.5 58.0 reduce-scatter.3
  763.5 74.5 reduce-scatter.5
  842.4 74.5 reduce-scatter.7
where the time goes:
time: 928 us; the launch traced here: 924 us
  waiting for transfers between devices  495 us (53%)
  blocking collectives  156 us (17%)
  local copies, waits for them, and re-layouts  107 us (12%)
  matrix products  100 us (11%)
  other arithmetic  48.7 us (5%)
  between operations  16.3 us (2%)
    psum x3, waiting for transfers between devices, head_total(): lax.psum(partial_sum.astype(jnp.bfloat16), 'head').astype(jnp.float32)  152 us
    unnamed x13, waiting for transfers between devices  88.6 us
    reduce_scatter x1, waiting for transfers between devices, per_device(): lax.psum_scatter(grad_reduce, 'seq', scatter_dimension=1, tiled=True)  78.9 us
    reduce_scatter x1, waiting for transfers between devices, per_device(): lax.psum_scatter(grad_expand, 'seq', scatter_dimension=0, tiled=True)  73.3 us
    gather x15, local copies, waits for them, and re-layouts, at_slots(): return jnp.take_along_axis(tensor, indices, axis=2)  63.4 us
    psum x1, blocking collectives, per_device(): lax.psum((grad_first, grad_heads, grad_second, grad_hidden), 'seq')  61.3 us
    all_gather x1, waiting for transfers between devices, per_device(): lax.all_gather(expand_weight, 'seq', axis=0, tiled=True)  40.8 us
    all_gather x1, waiting for transfers between devices, per_device(): lax.all_gather(attend_weight, 'seq', axis=1, tiled=True)  38.8 us
  transfers between devices with their start and end apart: 12, of which 9 were waited for; matrix products, arithmetic and copies ran while one was open for 13% of the time, Pallas kernels for 0%

commit v1 on v0

v1 whole, which is shorter than its diff:
```python
from functools import partial

import jax
import jax.numpy as jnp
from jax import lax
from jax.experimental import pallas as pl
from jax.experimental.pallas import tpu as pltpu
from jax.sharding import PartitionSpec as P

HD = 64
DILATION_SMALL = 8
NORM_EPSILON = 1e-05
MASKED_SCORE = -1e30
SCALE = HD ** (-0.5)
F32 = jnp.float32
BF16 = jnp.bfloat16
ANY = pl.BlockSpec(memory_space=pl.ANY)
SMEM = pl.BlockSpec(memory_space=pltpu.SMEM)
VMEM_LIMIT = 56 * 1024 * 1024


def nn(left, right):
    return lax.dot_general(left, right, (((1,), (0,)), ((), ())), preferred_element_type=F32)


def nt(left, right):
    return lax.dot_general(left, right, (((1,), (1,)), ((), ())), preferred_element_type=F32)


def tn(left, right):
    return lax.dot_general(left, right, (((0,), (0,)), ((), ())), preferred_element_type=F32)


def row_norm(values):
    center = jnp.mean(values, axis=-1, keepdims=True)
    spread = jnp.mean(values * values, axis=-1, keepdims=True) - center * center
    inverse = lax.rsqrt(spread + NORM_EPSILON)
    return (values - center) * inverse, inverse


def row_norm_back(incoming, normal, inverse, gain_row):
    scaled = incoming * gain_row
    first_mean = jnp.mean(scaled, axis=-1, keepdims=True)
    second_mean = jnp.mean(scaled * normal, axis=-1, keepdims=True)
    return inverse * (scaled - first_mean - normal * second_mean)


def three_parts(values):
    high = values.astype(BF16)
    rest = values - high.astype(F32)
    middle = rest.astype(BF16)
    low = (rest - middle.astype(F32)).astype(BF16)
    return high, middle, low


def gelu_parts(values):
    expo = jnp.exp(values * values * -0.5)
    term = 1.0 / (1.0 + (0.3275911 * 0.7071067811865476) * jnp.abs(values))
    poly = term * (
        0.254829592
        + term
        * (-0.284496736 + term * (1.421413741 + term * (-1.453152027 + term * 1.061405429)))
    )
    tail = 0.5 * poly * expo
    phi = jnp.where(values >= 0.0, 1.0 - tail, tail)
    return values * phi, phi + values * expo * 0.3989422804014327


def iota(shape, dim):
    return lax.broadcasted_iota(jnp.int32, shape, dim)


def exchange(value, seq_mask, head_mask):
    seq_size, head_size = lax.axis_size("seq"), lax.axis_size("head")
    pairs = [
        (s * head_size + h, (s ^ seq_mask) * head_size + (h ^ head_mask))
        for s in range(seq_size)
        for h in range(head_size)
    ]
    return lax.ppermute(value, ("seq", "head"), pairs)


def far_stages(seq_size):
    unit, left, stages = 4, seq_size // 4, []
    while left > 1:
        radix = 4 if left % 4 == 0 else 2
        stages.append((unit, radix))
        unit, left = unit * radix, left // radix
    return stages


def shard_masks(seq_size):
    return [
        4 * z + 2 * y + core for core in range(2) for y in range(2) for z in range(seq_size // 4)
    ]


def gather_chunk(shard):
    seq_size = lax.axis_size("seq")
    rows, width = shard.shape
    half = width // 2
    held = shard[None]
    for unit, radix in far_stages(seq_size):
        held = jnp.stack([held] + [exchange(held, unit * i, 0) for i in range(1, radix)])
        held = held.reshape(-1, rows, width)
    part_a, part_b = held[..., :half], held[..., half:]
    next_a, next_b = exchange(part_a, 0, 1), exchange(part_b, 2, 0)
    part_a, part_b = jnp.stack([part_a, next_a]), jnp.stack([part_b, next_b])
    next_a, next_b = exchange(part_a, 2, 0), exchange(part_b, 0, 1)
    part_a = jnp.stack([part_a, next_a], axis=1)
    part_b = jnp.stack([part_b, next_b], axis=0)
    own = jnp.stack([part_a, part_b])
    other = exchange(own, 1, 0)
    shape = (2, 2, seq_size // 2 * rows, half)
    return own.reshape(shape), other.reshape(shape)


def scatter_chunk(own, other):
    seq_size = lax.axis_size("seq")
    half_count, head_size, rows_all, half = own.shape
    rows = rows_all * 2 // seq_size
    shape = (half_count, head_size, 2, seq_size // 4, rows, half)
    got = exchange(other, 1, 0).reshape(shape)
    own = own.reshape(shape)
    total = own.astype(F32) + got.astype(F32)
    part_a, part_b = total[0], total[1]
    next_a = exchange(part_a[:, 1].astype(BF16), 2, 0)
    next_b = exchange(part_b[1].astype(BF16), 0, 1)
    part_a = part_a[:, 0] + next_a.astype(F32)
    part_b = part_b[0] + next_b.astype(F32)
    next_a = exchange(part_a[1].astype(BF16), 0, 1)
    next_b = exchange(part_b[1].astype(BF16), 2, 0)
    held = jnp.stack(
        [part_a[0] + next_a.astype(F32), part_b[0] + next_b.astype(F32)], axis=1
    )
    for unit, radix in reversed(far_stages(seq_size)):
        held = held.reshape(radix, -1, *held.shape[1:])
        low = held.astype(BF16)
        kept = held[0]
        for i in range(1, radix):
            kept = kept + exchange(low[i], unit * i, 0).astype(F32)
        held = kept
    return held[0]


def copies_of(pairs, sems):
    return [
        pltpu.make_async_copy(source, target, sems.at[i]) for i, (source, target) in enumerate(pairs)
    ]


def attend_copies(own, other, pair_w, value_w, sems):
    half_rows = own.shape[2]
    width = value_w.shape[2]
    pairs = []
    for hh in range(2):
        for c, source in enumerate((own, other)):
            rows = pl.ds(c * half_rows, half_rows)
            pairs.append((source.at[0, hh], pair_w.at[hh, rows]))
            pairs.append((source.at[1, hh, :, pl.ds(0, width)], value_w.at[hh, rows]))
    return copies_of(pairs, sems)


def head_columns(head, per_group, width):
    group, inside = divmod(head, per_group)
    start = group * 3 * width + inside * HD
    return [slice(start + e * width, start + e * width + HD) for e in range(3)]


def slot_select(offset, groups, positions):
    shape = (groups, positions)
    return (iota(shape, 1) == DILATION_SMALL * iota(shape, 0) + offset).astype(BF16)


def project_kernel(
    offs, x_ref, bias_ref, gain_ref, own, other, first_ref, qkv_ref, slot_ref, out_ref, lse_ref,
    pair_w, value_w, sems,
):
    positions, model = x_ref.shape[1:]
    width = value_w.shape[2]
    heads = model // HD
    per_group = heads // 2

    @pl.when(pl.program_id(0) == 0)
    def _():
        copies = attend_copies(own, other, pair_w, value_w, sems)
        for copy in copies:
            copy.start()
        for copy in copies:
            copy.wait()

    normal, _ = row_norm(x_ref[0].astype(F32))
    first = (normal * gain_ref[...]).astype(BF16)
    first_ref[0] = first
    for hh in range(2):
        start = hh * 3 * width
        qkv_ref[0, :, start : start + 2 * width] = nn(first, pair_w[hh]).astype(BF16)
        qkv_ref[0, :, start + 2 * width : start + 3 * width] = nn(first, value_w[hh]).astype(BF16)
    bias = bias_ref[0]
    lane = iota((positions, 2 * HD), 1)
    groups = positions // DILATION_SMALL
    for pair in range(heads // 2):
        outs, logs = [], []
        for head in (2 * pair, 2 * pair + 1):
            cq, ck, cv = head_columns(head, per_group, width)
            query, key, value = qkv_ref[0, :, cq], qkv_ref[0, :, ck], qkv_ref[0, :, cv]
            chosen = slot_select(offs[head], groups, positions)
            slot_ref[head] = nn(chosen, jnp.concatenate([query, key, value], axis=1)).astype(BF16)
            score = nt(query, key) * SCALE + bias
            peak = jnp.max(score, axis=-1, keepdims=True)
            expo = jnp.exp(score - peak)
            total = jnp.sum(expo, axis=-1, keepdims=True)
            outs.append(nn(expo.astype(BF16), value) / total)
            logs.append(peak + jnp.log(total))
        columns = slice(2 * pair * HD, 2 * (pair + 1) * HD)
        out_ref[0, :, columns] = jnp.concatenate(outs, axis=1)
        lse_ref[0, :, columns] = jnp.where(lane < HD, logs[0], logs[1])


def far_masks(parity, row_start, row_count, slots):
    row = row_start + iota((row_count, slots), 0)
    column = iota((row_count, slots), 1)
    live_row = (parity == 0) | ((row & 1) == parity - 1)
    live_column = (parity == 0) | ((column & 1) == parity - 1)
    return (column <= row) & live_column, live_row


def for_blocks(count, body):
    if count == 1:
        body(0)
    else:
        lax.fori_loop(0, count, lambda b, carry: (body(b), carry)[1], 0)


def far_kernel(parity_ref, qkv_ref, out_ref, kv_scr):
    devices, _, groups, _ = qkv_ref.shape
    slots = devices * groups
    block = min(slots, 256)
    per_block = block // groups
    parity = parity_ref[pl.program_id(0)]
    kv_scr[...] = qkv_ref[:, 0].reshape(slots, 3 * HD)[:, HD:]

    def body(index):
        piece = pl.ds(index * per_block, per_block)
        query = qkv_ref[piece, 0].reshape(block, 3 * HD)[:, :HD]
        key, value = kv_scr[:, :HD], kv_scr[:, HD:]
        allowed, live = far_masks(parity, index * block, block, slots)
        score = jnp.where(allowed, nt(query, key) * SCALE, MASKED_SCORE)
        peak = jnp.max(score, axis=-1, keepdims=True)
        expo = jnp.exp(score - peak)
        total = jnp.sum(expo, axis=-1, keepdims=True)
        out = nn(expo.astype(BF16), value) / total
        log = jnp.where(live[:, :1], peak + jnp.log(total), MASKED_SCORE)
        high, middle, low = three_parts(log)
        lane = iota((block, 2 * HD), 1)
        tile = jnp.concatenate([out, out], axis=1)
        tile = jnp.where(lane == HD, high.astype(F32), tile)
        tile = jnp.where(lane == HD + 1, middle.astype(F32), tile)
        tile = jnp.where(lane == HD + 2, low.astype(F32), tile)
        out_ref[piece, 0] = tile.astype(BF16).reshape(per_block, groups, 2 * HD)

    for_blocks(slots // block, body)


def middle_kernel(
    offs, x_ref, near_ref, log_ref, far_ref, seed_ref, gain_heads, gain_second, gain_hidden,
    place_ref, own_1, other_1, own_2, other_2, own_3, other_3,
    block_ref, heads_ref, second_ref, hidden_ref, pre_ref, resid_ref, low_ref, att_ref, lse_ref,
    dot_ref, slot_ref, grad_heads, grad_second, grad_hidden,
    merge_w, expand_w, reduce_w, act_scr, slope_scr, grad_scr, sems,
):
    positions, model = x_ref.shape[1:]
    half_rows, half = own_2.shape[2], own_2.shape[3]
    width = merge_w.shape[2]
    heads = model // HD
    groups = positions // DILATION_SMALL
    hidden_width = 4 * half
    step = pl.program_id(0)
    merge_pairs, expand_pairs, reduce_pairs = [], [], []
    for hh in range(2):
        for c, (one, two, three) in enumerate(((own_1, own_2, own_3), (other_1, other_2, other_3))):
            rows = pl.ds(c * half_rows, half_rows)
            merge_pairs.append((one.at[1, hh, :, pl.ds(half - width, width)], merge_w.at[hh, rows]))
            for part in range(2):
                expand_pairs.append((two.at[part, hh], expand_w.at[2 * hh + part, rows]))
                reduce_pairs.append((three.at[part, hh], reduce_w.at[2 * hh + part, rows]))
    copies = copies_of(merge_pairs + expand_pairs + reduce_pairs, sems)

    def await_copies(start, count):
        @pl.when(step == 0)
        def _():
            for copy in copies[start : start + count]:
                copy.wait()

    @pl.when(step == 0)
    def _():
        for copy in copies:
            copy.start()
        grad_heads[...] = jnp.zeros_like(grad_heads)
        grad_second[...] = jnp.zeros_like(grad_second)
        grad_hidden[...] = jnp.zeros_like(grad_hidden)

    lane = iota((positions, 2 * HD), 1)
    place = iota((positions, 2 * HD), 0)
    for pair in range(heads // 2):
        spread, logs = [], []
        for head in (2 * pair, 2 * pair + 1):
            chosen = slot_select(offs[head], groups, positions)
            tile = tn(chosen, far_ref[head])
            log = jnp.sum(
                jnp.where((lane >= HD) & (lane < HD + 3), tile, 0.0), axis=-1, keepdims=True
            )
            here = (place & (DILATION_SMALL - 1)) == offs[head]
            spread.append(tile[:, :HD])
            logs.append(jnp.where(here, log, MASKED_SCORE))
        columns = slice(2 * pair * HD, 2 * (pair + 1) * HD)
        log_near = log_ref[0, :, columns]
        log_far = jnp.where(lane < HD, logs[0], logs[1])
        peak = jnp.maximum(log_near, log_far)
        weight_near, weight_far = jnp.exp(log_near - peak), jnp.exp(log_far - peak)
        total = weight_near + weight_far
        lse_ref[0, :, columns] = peak + jnp.log(total)
        act_scr[:, columns] = (
            near_ref[0, :, columns] * weight_near + jnp.concatenate(spread, axis=1) * weight_far
        ) / total
    attended = act_scr[:, :model]
    normal_heads, inverse_heads = row_norm(attended)
    heads_in = (normal_heads * gain_heads[...]).astype(BF16)
    heads_ref[0] = heads_in
    await_copies(0, 4)
    merged = [nt(heads_in[:, hh * width : (hh + 1) * width], merge_w[hh]) for hh in range(2)]
    residual = x_ref[0].astype(F32) + (merged[0] + merged[1])
    normal_two, inverse_two = row_norm(residual)
    second_in = (normal_two * gain_second[...]).astype(BF16)
    second_ref[0] = second_in
    dot_ref[0] = attended
    await_copies(4, 8)
    total_one = jnp.zeros((positions, 1), F32)
    total_two = jnp.zeros((positions, 1), F32)
    for block in range(4):
        columns = slice(block * half, (block + 1) * half)
        act, slope = gelu_parts(nn(second_in, expand_w[block]))
        act_scr[:, columns] = act
        slope_scr[:, columns] = slope
        total_one += jnp.sum(act, axis=-1, keepdims=True)
        total_two += jnp.sum(act * act, axis=-1, keepdims=True)
    center = total_one / hidden_width
    inverse = lax.rsqrt(total_two / hidden_width - center * center + NORM_EPSILON)
    await_copies(12, 8)
    seed = seed_ref[0]
    total_one = jnp.zeros((positions, 1), F32)
    total_two = jnp.zeros((positions, 1), F32)
    block_out = jnp.zeros((positions, model), F32)
    for block in range(4):
        columns = slice(block * half, (block + 1) * half)
        normal = (act_scr[:, columns] - center) * inverse
        act_scr[:, columns] = normal
        gain = gain_hidden[:, columns]
        hidden_in = (normal * gain).astype(BF16)
        hidden_ref[0, :, columns] = hidden_in
        block_out += nt(hidden_in, reduce_w[block])
        grad = nn(seed, reduce_w[block])
        through = grad * normal
        grad_hidden[:, columns] += jnp.sum(through, axis=0, keepdims=True)
        total_one += jnp.sum(grad * gain, axis=-1, keepdims=True)
        total_two += jnp.sum(through * gain, axis=-1, keepdims=True)
        grad_scr[:, columns] = grad
    block_ref[0] = nt((residual + block_out).astype(BF16), place_ref[...]).astype(BF16)
    total_one = total_one / hidden_width
    total_two = total_two / hidden_width
    grad_second_in = jnp.zeros((positions, model), F32)
    for block in range(4):
        columns = slice(block * half, (block + 1) * half)
        grad = grad_scr[:, columns] * gain_hidden[:, columns]
        grad = inverse * (grad - total_one - act_scr[:, columns] * total_two)
        grad_pre = (grad * slope_scr[:, columns]).astype(BF16)
        pre_ref[0, :, columns] = grad_pre
        grad_second_in += nt(grad_pre, expand_w[block])
    grad_second[...] += jnp.sum(grad_second_in * normal_two, axis=0, keepdims=True)
    resid = seed.astype(F32) + row_norm_back(
        grad_second_in, normal_two, inverse_two, gain_second[...]
    )
    resid_ref[0] = resid
    resid_low = resid.astype(BF16)
    low_ref[0] = resid_low
    grad_heads_in = jnp.concatenate([nn(resid_low, merge_w[hh]) for hh in range(2)], axis=1)
    attended = dot_ref[0]
    normal_heads, inverse_heads = row_norm(attended)
    grad_heads[...] += jnp.sum(grad_heads_in * normal_heads, axis=0, keepdims=True)
    grad_att = row_norm_back(
        grad_heads_in, normal_heads, inverse_heads, gain_heads[...]
    ).astype(BF16)
    att_ref[0] = grad_att
    product = grad_att.astype(F32) * attended
    same = (iota((2 * HD, 2 * HD), 0) // HD == iota((2 * HD, 2 * HD), 1) // HD).astype(BF16)
    slot_lane = iota((groups, 2 * HD), 1)
    for pair in range(heads // 2):
        columns = slice(2 * pair * HD, 2 * (pair + 1) * HD)
        dots = sum(nn(part, same) for part in three_parts(product[:, columns]))
        dot_ref[0, :, columns] = dots
        lse = lse_ref[0, :, columns]
        for inside, head in enumerate((2 * pair, 2 * pair + 1)):
            chosen = slot_select(offs[head], groups, positions)
            part = slice(inside * HD, (inside + 1) * HD)
            grad_slot = nn(chosen, att_ref[0, :, head * HD : (head + 1) * HD])
            tile = jnp.concatenate([grad_slot, grad_slot], axis=1)
            for index, piece in enumerate(
                three_parts(lse[:, part]) + three_parts(dots[:, part])
            ):
                value = nn(chosen, piece)
                tile = jnp.where(
                    slot_lane == HD + index, jnp.concatenate([value, value], axis=1), tile
                )
            slot_ref[head] = tile.astype(BF16)


def far_back_kernel(parity_ref, qkv_ref, grad_ref, out_ref, kv_scr, total_scr):
    devices, _, groups, _ = qkv_ref.shape
    slots = devices * groups
    block = min(slots, 256)
    per_block = block // groups
    parity = parity_ref[pl.program_id(0)]
    kv_scr[...] = qkv_ref[:, 0].reshape(slots, 3 * HD)[:, HD:]
    total_scr[...] = jnp.zeros_like(total_scr)

    def body(index):
        piece = pl.ds(index * per_block, per_block)
        query = qkv_ref[piece, 0].reshape(block, 3 * HD)[:, :HD]
        tile = grad_ref[piece, 0].reshape(block, 2 * HD)
        key, value = kv_scr[:, :HD], kv_scr[:, HD:]
        grad = tile[:, :HD]
        stats = tile[:, HD:].astype(F32)
        log = stats[:, 0:1] + stats[:, 1:2] + stats[:, 2:3]
        dots = stats[:, 3:4] + stats[:, 4:5] + stats[:, 5:6]
        allowed, live = far_masks(parity, index * block, block, slots)
        score = jnp.where(allowed & live, nt(query, key) * SCALE - log, MASKED_SCORE)
        weight = jnp.exp(score)
        grad_score = (weight * (nt(grad, value) - dots)).astype(BF16)
        grad_query = nn(grad_score, key) * SCALE
        total_scr[:, :HD] += tn(grad_score, query) * SCALE
        total_scr[:, HD:] += tn(weight.astype(BF16), grad)
        out_ref[piece, 0, :, :HD] = grad_query.astype(BF16).reshape(per_block, groups, HD)

    for_blocks(slots // block, body)
    out_ref[:, 0, :, HD:] = total_scr[...].astype(BF16).reshape(devices, groups, 2 * HD)


def near_back_kernel(offs, bias_ref, qkv_ref, att_ref, lse_ref, dot_ref, far_ref, out_ref):
    positions, model = att_ref.shape[1:]
    heads = model // HD
    per_group = heads // 2
    width = per_group * HD
    groups = positions // DILATION_SMALL
    bias = bias_ref[0]
    for head in range(heads):
        cq, ck, cv = head_columns(head, per_group, width)
        query, key, value = qkv_ref[0, :, cq], qkv_ref[0, :, ck], qkv_ref[0, :, cv]
        own = slice(head * HD, (head + 1) * HD)
        grad = att_ref[0, :, own]
        log = lse_ref[0, :, head * HD : head * HD + 1]
        dots = dot_ref[0, :, head * HD : head * HD + 1]
        weight = jnp.exp(nt(query, key) * SCALE + bias - log)
        grad_score = (weight * (nt(grad, value) - dots)).astype(BF16)
        chosen = slot_select(offs[head], groups, positions)
        far = tn(chosen, far_ref[head])
        out_ref[0, :, cq] = (nn(grad_score, key) * SCALE + far[:, :HD]).astype(BF16)
        out_ref[0, :, ck] = (tn(grad_score, query) * SCALE + far[:, HD : 2 * HD]).astype(BF16)
        out_ref[0, :, cv] = (tn(weight.astype(BF16), grad) + far[:, 2 * HD :]).astype(BF16)


def product_kernel(left_ref, right_ref, out_ref):
    out_ref[0, 0, 0] = tn(left_ref[...], right_ref[...]).astype(BF16)


def attend_grad_kernel(first_ref, low_ref, qkv_ref, heads_ref, out_ref):
    width = heads_ref.shape[1]
    first = first_ref[...]
    out_ref[0, 0, 0] = tn(first, qkv_ref[:, : 2 * width]).astype(BF16)
    out_ref[0, 1, 0, :, :width] = tn(first, qkv_ref[:, 2 * width :]).astype(BF16)
    out_ref[0, 1, 0, :, width:] = tn(low_ref[...], heads_ref[...]).astype(BF16)


def input_grad_kernel(
    x_ref, qkv_ref, resid_ref, gain_ref, place_ref, own, other, grad_ref, gain_grad,
    pair_w, value_w, sems,
):
    width = value_w.shape[2]

    @pl.when(pl.program_id(0) == 0)
    def _():
        copies = attend_copies(own, other, pair_w, value_w, sems)
        for copy in copies:
            copy.start()
        for copy in copies:
            copy.wait()
        gain_grad[...] = jnp.zeros_like(gain_grad)

    normal, inverse = row_norm(x_ref[0].astype(F32))
    grad_first = jnp.zeros(normal.shape, F32)
    for hh in range(2):
        start = hh * 3 * width
        grad_first += nt(qkv_ref[0, :, start : start + 2 * width], pair_w[hh])
        grad_first += nt(qkv_ref[0, :, start + 2 * width : start + 3 * width], value_w[hh])
    gain_grad[...] += jnp.sum(grad_first * normal, axis=0, keepdims=True)
    grad = resid_ref[0] + row_norm_back(grad_first, normal, inverse, gain_ref[...])
    grad_ref[0] = nt(grad.astype(BF16), place_ref[...]).astype(BF16)


def by_row(*tail):
    return pl.BlockSpec((1, *tail), lambda r: (r, *(0 for _ in tail)))


def whole(*shape):
    return pl.BlockSpec(shape, lambda *_: tuple(0 for _ in shape))


def sds(shape, dtype):
    return jax.ShapeDtypeStruct(shape, dtype)


def call(kernel, grid, in_specs, out_specs, out_shape, scratch=(), flops=0, moved=0):
    return pl.pallas_call(
        kernel,
        grid=grid,
        in_specs=in_specs,
        out_specs=out_specs,
        out_shape=out_shape,
        scratch_shapes=list(scratch),
        compiler_params=pltpu.CompilerParams(
            dimension_semantics=("arbitrary",) * len(grid), vmem_limit_bytes=VMEM_LIMIT
        ),
        cost_estimate=pl.CostEstimate(flops=flops, bytes_accessed=moved, transcendentals=0),
    )


def per_device(
    inputs,
    attend_weight,
    merge_weight,
    expand_weight,
    reduce_weight,
    gain_first,
    gain_heads,
    gain_second,
    gain_hidden,
    cotangent,
    lengths,
    local_span,
    dilation,
):
    seq_size, head_size = lax.axis_size("seq"), lax.axis_size("head")
    row_count, positions, model = inputs.shape
    rows = row_count // head_size
    tokens = rows * positions
    shard_rows, width = attend_weight.shape[1:]
    heads = width * head_size // HD
    group_heads = heads // head_size
    hidden_here = expand_weight.shape[1]
    hidden_width = hidden_here * head_size
    half = hidden_here // 2
    half_rows = model // 2
    groups = positions // DILATION_SMALL
    pairs = rows * heads
    owned = -(-pairs // seq_size)
    padded = owned * seq_size
    seq_index, head_index = lax.axis_index("seq"), lax.axis_index("head")

    chunk_1 = jnp.concatenate(
        [attend_weight[0], attend_weight[1], attend_weight[2], merge_weight.T], axis=1
    )
    own_1, other_1 = gather_chunk(chunk_1)
    own_2, other_2 = gather_chunk(expand_weight)
    own_3, other_3 = gather_chunk(reduce_weight.T)
    both_gains = jnp.concatenate([gain_heads, gain_hidden])
    partner_gains = exchange(both_gains.reshape(-1, 128), 0, 1).reshape(-1)
    gain_heads_all = jnp.concatenate([gain_heads, partner_gains[:width]])[None]
    gain_hidden_all = jnp.concatenate([gain_hidden, partner_gains[width:]])[None]

    masks = jnp.array(shard_masks(seq_size), jnp.int32)
    block_of = seq_index ^ masks
    feature_of = (block_of[:, None] * shard_rows + jnp.arange(shard_rows)).reshape(-1)
    place = (jnp.arange(model)[:, None] == feature_of[None, :]).astype(BF16)

    def to_own_order(gain):
        return jnp.take(gain.reshape(seq_size, shard_rows), block_of, axis=0).reshape(1, model)

    gain_one, gain_two = to_own_order(gain_first), to_own_order(gain_second)
    row_start = head_index * rows

    def own_rows(tensor):
        return lax.dynamic_slice_in_dim(tensor, row_start, rows, axis=0)

    in_own_order = partial(jnp.einsum, "rtd,de->rte", preferred_element_type=F32)
    x_own = in_own_order(own_rows(inputs), place).astype(BF16)
    places = jnp.arange(positions)
    in_length = (seq_index * positions + places)[None, :] < own_rows(lengths)[:, None]
    seed = jnp.where(in_length[..., None], own_rows(cotangent), jnp.zeros((), BF16))
    seed = in_own_order(seed, place).astype(BF16)
    span_block = places[None, :] // own_rows(local_span)[:, None]
    within = (span_block[:, :, None] == span_block[:, None, :]) & (
        places[None, :] <= places[:, None]
    )
    bias = jnp.where(within, 0.0, MASKED_SCORE).astype(F32)

    local_head = jnp.arange(heads)
    head_ids = (head_index ^ (local_head // group_heads)) * group_heads + local_head % group_heads
    offsets = (head_ids % DILATION_SMALL).astype(jnp.int32)
    pair_ids = jnp.minimum(seq_index * owned + jnp.arange(owned), pairs - 1)
    pair_rate = own_rows(dilation)[pair_ids // heads]
    pair_head = head_ids[pair_ids % heads]
    parity = jnp.where(
        pair_rate == DILATION_SMALL, 0, 1 + (pair_head % pair_rate) // DILATION_SMALL
    ).astype(jnp.int32)

    attend_scratch = [
        pltpu.VMEM((2, model, 2 * width), BF16),
        pltpu.VMEM((2, model, width), BF16),
        pltpu.SemaphoreType.DMA((8,)),
    ]
    first_in, qkv, slots, near, log_near = call(
        project_kernel,
        (rows,),
        [SMEM, by_row(positions, model), by_row(positions, positions), whole(1, model), ANY, ANY],
        [
            by_row(positions, model),
            by_row(positions, 3 * model),
            pl.BlockSpec((heads, groups, 3 * HD), lambda r: (r, 0, 0)),
            by_row(positions, model),
            by_row(positions, model),
        ],
        [
            sds((rows, positions, model), BF16),
            sds((rows, positions, 3 * model), BF16),
            sds((padded, groups, 3 * HD), BF16),
            sds((rows, positions, model), F32),
            sds((rows, positions, model), F32),
        ],
        attend_scratch,
        flops=2 * tokens * model * 3 * model,
        moved=16 * tokens * model,
    )(offsets, x_own, bias, gain_one, own_1, other_1)

    def to_owners(value):
        value = value.reshape(seq_size, owned, groups, value.shape[-1])
        return lax.all_to_all(value, "seq", 0, 0, tiled=True)

    def from_owners(value):
        value = lax.all_to_all(value, "seq", 0, 0, tiled=True)
        return value.reshape(padded, groups, value.shape[-1])

    def by_pair(size):
        return pl.BlockSpec((seq_size, 1, groups, size), lambda i: (0, i, 0, 0))

    def owned_shape(size):
        return sds((seq_size, owned, groups, size), BF16)

    slot_count = seq_size * groups
    kv_scratch = pltpu.VMEM((slot_count, 2 * HD), BF16)
    far_qkv = to_owners(slots)
    far_out = call(
        far_kernel,
        (owned,),
        [SMEM, by_pair(3 * HD)],
        by_pair(2 * HD),
        owned_shape(2 * HD),
        [kv_scratch],
        flops=4 * owned * slot_count**2 * HD,
        moved=owned * slot_count * HD * 10,
    )(parity, far_qkv)
    far_here = from_owners(far_out)

    def of_row(size):
        return pl.BlockSpec((heads, groups, size), lambda r: (r, 0, 0))

    model_row, hidden_row = by_row(positions, model), by_row(positions, hidden_width)
    model_shape = (rows, positions, model)
    hidden_shape = (rows, positions, hidden_width)
    (
        block_mine, heads_in, second_in, hidden_in, grad_pre, grad_resid, resid_low, grad_att,
        log_all, row_dot, grad_slots, grad_heads, grad_second, grad_hidden,
    ) = call(
        middle_kernel,
        (rows,),
        [
            SMEM, model_row, model_row, model_row, of_row(2 * HD), model_row, whole(1, model),
            whole(1, model), whole(1, hidden_width), whole(model, model),
            ANY, ANY, ANY, ANY, ANY, ANY,
        ],
        [
            model_row, model_row, model_row, hidden_row, hidden_row, model_row, model_row,
            model_row, model_row, model_row, of_row(2 * HD), whole(1, model), whole(1, model),
            whole(1, hidden_width),
        ],
        [
            sds(model_shape, BF16), sds(model_shape, BF16), sds(model_shape, BF16),
            sds(hidden_shape, BF16), sds(hidden_shape, BF16), sds(model_shape, F32),
            sds(model_shape, BF16), sds(model_shape, BF16), sds(model_shape, F32),
            sds(model_shape, F32), sds((padded, groups, 2 * HD), BF16), sds((1, model), F32),
            sds((1, model), F32), sds((1, hidden_width), F32),
        ],
        [
            pltpu.VMEM((2, model, width), BF16),
            pltpu.VMEM((4, model, half), BF16),
            pltpu.VMEM((4, model, half), BF16),
            pltpu.VMEM((positions, hidden_width), F32),
            pltpu.VMEM((positions, hidden_width), F32),
            pltpu.VMEM((positions, hidden_width), F32),
            pltpu.SemaphoreType.DMA((20,)),
        ],
        flops=8 * tokens * model * hidden_width,
        moved=4 * model * hidden_width,
    )(
        offsets, x_own, near, log_near, far_here, seed, gain_heads_all, gain_two,
        gain_hidden_all, place, own_1, other_1, own_2, other_2, own_3, other_3,
    )

    def flat(tensor):
        return tensor.reshape(tokens, tensor.shape[-1])

    def weight_grad(left, right):
        return call(
            product_kernel,
            (2, 2, 2),
            [
                pl.BlockSpec((tokens, half_rows), lambda c, x, p: (0, c)),
                pl.BlockSpec((tokens, half), lambda c, x, p: (0, 2 * x + p)),
            ],
            pl.BlockSpec((1, 1, 1, half_rows, half), lambda c, x, p: (c, p, x, 0, 0)),
            sds((2, 2, 2, half_rows, half), BF16),
            flops=2 * tokens * model * hidden_width,
            moved=2 * model * hidden_width,
        )(flat(left), flat(right))

    reduce_parts = weight_grad(seed, hidden_in)
    grad_reduce = scatter_chunk(reduce_parts[0], reduce_parts[1])
    expand_parts = weight_grad(second_in, grad_pre)
    grad_expand = scatter_chunk(expand_parts[0], expand_parts[1])

    def both_rows(mine):
        other = exchange(mine, 0, 1)
        first = jnp.where(head_index == 0, mine, other)
        second = jnp.where(head_index == 0, other, mine)
        return jnp.concatenate([first, second])

    block_out = both_rows(block_mine)

    far_grads = to_owners(grad_slots)
    far_back = call(
        far_back_kernel,
        (owned,),
        [SMEM, by_pair(3 * HD), by_pair(2 * HD)],
        by_pair(3 * HD),
        owned_shape(3 * HD),
        [kv_scratch, pltpu.VMEM((slot_count, 2 * HD), F32)],
        flops=10 * owned * slot_count**2 * HD,
        moved=owned * slot_count * HD * 16,
    )(parity, far_qkv, far_grads)
    back_here = from_owners(far_back)
    grad_qkv = call(
        near_back_kernel,
        (rows,),
        [
            SMEM, by_row(positions, positions), by_row(positions, 3 * model), model_row,
            model_row, model_row, of_row(3 * HD),
        ],
        by_row(positions, 3 * model),
        sds((rows, positions, 3 * model), BF16),
        flops=10 * tokens * positions * model,
        moved=20 * tokens * model,
    )(offsets, bias, qkv, grad_att, log_all, row_dot, back_here)

    def left_spec(size):
        return pl.BlockSpec((tokens, size), lambda c, x: (0, c))

    def right_spec(size):
        return pl.BlockSpec((tokens, size), lambda c, x: (0, x))

    attend_parts = call(
        attend_grad_kernel,
        (2, 2),
        [left_spec(half_rows), left_spec(half_rows), right_spec(3 * width), right_spec(width)],
        pl.BlockSpec((1, 2, 1, half_rows, 2 * width), lambda c, x: (c, 0, x, 0, 0)),
        sds((2, 2, 2, half_rows, 2 * width), BF16),
        flops=2 * tokens * model * 4 * model,
        moved=8 * model * model,
    )(flat(first_in), flat(resid_low), flat(grad_qkv), flat(heads_in))
    grad_attend = scatter_chunk(attend_parts[0], attend_parts[1])

    grad_mine, grad_first = call(
        input_grad_kernel,
        (rows,),
        [
            model_row, by_row(positions, 3 * model), model_row, whole(1, model),
            whole(model, model), ANY, ANY,
        ],
        [model_row, whole(1, model)],
        [sds(model_shape, BF16), sds((1, model), F32)],
        attend_scratch,
        flops=2 * tokens * model * 3 * model,
        moved=8 * model * model,
    )(x_own, grad_qkv, grad_resid, gain_one, place, own_1, other_1)
    grad_inputs = both_rows(grad_mine)

    inverse_masks = [0] * seq_size
    for index, mask in enumerate(shard_masks(seq_size)):
        inverse_masks[mask] = index
    found = jnp.array(inverse_masks, jnp.int32)[seq_index ^ jnp.arange(seq_size)]

    def to_common_order(grad):
        return jnp.take(grad.reshape(seq_size, shard_rows), found, axis=0).reshape(-1)

    shared = [to_common_order(grad_first), to_common_order(grad_second)]
    kept = jnp.concatenate(shared + [grad_heads[0, :width], grad_hidden[0, :hidden_here]])
    sent = jnp.concatenate(shared + [grad_heads[0, width:], grad_hidden[0, hidden_here:]])
    total = kept.reshape(-1, 128) + exchange(sent.reshape(-1, 128), 0, 1)
    mask = 1
    while mask < seq_size:
        total = total + exchange(total, mask, 0)
        mask *= 2
    total = total.reshape(-1)

    return (
        block_out,
        grad_inputs,
        jnp.stack(
            [grad_attend[0, :, :width], grad_attend[0, :, width:], grad_attend[1, :, :width]]
        ),
        grad_attend[1, :, width:].T,
        jnp.concatenate([grad_expand[0], grad_expand[1]], axis=1),
        jnp.concatenate([grad_reduce[0], grad_reduce[1]], axis=1).T,
        total[:model],
        total[2 * model : 2 * model + width],
        total[model : 2 * model],
        total[2 * model + width :],
    )


def solution(mesh):
    placed = (
        P(None, "seq", None),
        P(None, "seq", "head"),
        P("head", "seq"),
        P("seq", "head"),
        P("head", "seq"),
        P(),
        P("head"),
        P(),
        P("head"),
        P(None, "seq", None),
        P(),
        P(),
        P(),
    )
    return jax.shard_map(
        per_device,
        mesh=mesh,
        in_specs=placed,
        out_specs=(
            P(None, "seq", None),
            P(None, "seq", None),
            P(None, "seq", "head"),
            P("head", "seq"),
            P("seq", "head"),
            P("head", "seq"),
            P(),
            P("head"),
            P(),
            P("head"),
        ),
        check_vma=False,
    )
```

time: 928 us -> 396 us (0.43)
  waiting for transfers between devices: 495 us -> 108 us
  blocking collectives: 156 us -> 0 us
  Pallas kernels: 0 us -> 103 us
  matrix products: 100 us -> 3.08 us
  starting transfers between devices: 1.12 us -> 94.9 us
  local copies, waits for them, and re-layouts: 107 us -> 36.1 us
  between operations: 16.3 us -> 1.57 us
    reduce_scatter x3 -> x0, waiting for transfers between devices: 152 us -> none  [the longest x1 78.9 us: per_device(): lax.psum_scatter(grad_reduce, 'seq', scatter_dimension=1, tiled=True)]
    psum x3 -> x0, waiting for transfers between devices: 152 us -> none  [head_total(): lax.psum(partial_sum.astype(jnp.bfloat16), 'head').astype(jnp.float32)]
    pallas_call x0 -> x9, Pallas kernels: none -> 103 us  [the longest x1 36.5 us: per_device(): call(middle_kernel, (rows,), [SMEM, model_row, model_row, model_row, of_r...]
    all_gather x5 -> x0, waiting for transfers between devices: 102 us -> none  [the longest x1 40.8 us: per_device(): lax.all_gather(expand_weight, 'seq', axis=0, tiled=True)]
    dot_general x29 -> x2, matrix products: 100 us -> 3.08 us  [the longest x1 1.56 us: per_device(): seed = in_own_order(seed, place).astype(BF16)]
    ppermute x0 -> x56, waiting for transfers between devices: none -> 93.8 us  [exchange(): return lax.ppermute(value, ('seq', 'head'), pairs)]
    unnamed x13 -> x0, waiting for transfers between devices: 88.6 us -> none
    psum x5 -> x0, blocking collectives: 81.2 us -> none  [the longest x1 61.3 us: per_device(): lax.psum((grad_first, grad_heads, grad_second, grad_hidden), 'seq')]
  transfers between devices with their start and end apart: 12 -> 60, of which waited for: 9 -> 22; matrix products, arithmetic and copies ran while one was open for 13% -> 20% of each run, Pallas kernels for 0% -> 16%
where the time goes in v1:
time: 396 us; the launch traced here: 395 us
  waiting for transfers between devices  108 us (27%)
  Pallas kernels  103 us (26%)
  starting transfers between devices  94.9 us (24%)
  other arithmetic  47.8 us (12%)
  local copies, waits for them, and re-layouts  36.1 us (9%)
    ppermute x56, waiting for transfers between devices, exchange(): return lax.ppermute(value, ('seq', 'head'), pairs)  93.8 us
    ppermute x56, starting transfers between devices, exchange(): return lax.ppermute(value, ('seq', 'head'), pairs)  75 us
    pallas_call x1, Pallas kernels, per_device(): call(middle_kernel, (rows,), [SMEM, model_row, model_row, model_row, of_r...  36.5 us
    another operation x12, other arithmetic, gather_chunk(): own = jnp.stack([part_a, part_b])  18.6 us
    pallas_call x2, Pallas kernels, weight_grad(): call(product_kernel, (2, 2, 2), [pl.BlockSpec((tokens, half_rows), lambda...  17.3 us
    pallas_call x1, Pallas kernels, per_device(): call(near_back_kernel, (rows,), [SMEM, by_row(positions, positions), by_r...  12.3 us
    pallas_call x1, Pallas kernels, per_device(): call(input_grad_kernel, (rows,), [model_row, by_row(positions, 3 * model)...  11.4 us
    pallas_call x1, Pallas kernels, per_device(): call(project_kernel, (rows,), [SMEM, by_row(positions, model), by_row(pos...  10.9 us
  transfers between devices with their start and end apart: 60, of which 22 were waited for; matrix products, arithmetic and copies ran while one was open for 20% of the time, Pallas kernels for 16%

profile of v1, /device:TPU:0, one launch (start us, length us, event | category | flops | bytes accessed | tf_op | source)
XLA Modules:
  0.0 394.7 jit_solution(2087243156604509513)
XLA Ops:
  2.4 3.1 collective-permute-start
  5.5 2.6 collective-permute-start.1
  9.0 3.5 collective-permute-start.10
  25.9 3.8 collective-permute-start.18
  32.1 2.0 collective-permute-done.11
  37.3 7.5 %collective-permute-done.18 = bf16[1,48,1536]{2,1,0:T(8,128)(2,1)S(1)} collective-permute-done((bf16[1,48,1536]{2,1,0:T(8,128)(2,1)S(1)}, bf16[1,48,1536]{2,1,0:T(8,128)(2,1)S(1)}, u32[]{:S(2)}, u32[]{:S(2)}) %collective-permute-start.18) | collective-permute-done | bytes 147488 | tf_op jit(solution)/shard_map/ppermute | solution.py:80
  52.9 1.8 collective-permute-done.14
  60.0 7.3 %collective-permute-done.4 = bf16[2,4,48,768]{3,2,1,0:T(8,128)(2,1)S(1)} collective-permute-done((bf16[2,4,48,768]{3,2,1,0:T(8,128)(2,1)S(1)}, bf16[2,4,48,768]{3,2,1,0:T(8,128)(2,1)S(1)}, u32[]{:S(2)}, u32[]{:S(2)}) %collective-permute-start.4) | collective-permute-done | bytes 589856 | tf_op jit(solution)/shard_map/ppermute | solution.py:80
  80.0 6.3 %collective-permute-done.13 = bf16[2,4,48,768]{3,2,1,0:T(8,128)(2,1)} collective-permute-done((bf16[2,4,48,768]{3,2,1,0:T(8,128)(2,1)}, bf16[2,4,48,768]{3,2,1,0:T(8,128)(2,1)}, u32[]{:S(2)}, u32[]{:S(2)}) %collective-permute-start.13) | collective-permute-done | bytes 589856 | tf_op jit(solution)/shard_map/ppermute | solution.py:80
  87.9 2.4 fusion.99
  93.3 2.5 collective-permute-done.21
  95.7 2.3 fusion.98
  108.9 10.9 %shard_map.222 = (bf16[3,128,768]{2,1,0:T(8,128)(2,1)}, bf16[3,128,2304]{2,1,0:T(8,128)(2,1)}, bf16[48,16,192]{2,1,0:T(8,128)(2,1)}, f32[3,128,768]{2,1,0:T(8,128)}, f32[3,128,768]{2,1,0:T(8,128)}) custom-call(s32[12]{0:T(128)} %and_select_fusion.5.offs, bf16[3,128,768]{2,1,0:T(8,128)(2,1)} %fusion.6.x_ref, f32[3,128,128]{2,1,0:T(8,128)} %and_select_fusion.bias_ref, ...), custom_call_target="tpu_custom_call" | custom-call | flops 1358954496 | bytes 4718592 | tf_op jit(solution)/shard_map/pallas_call | solution.py:620
  119.8 7.0 %all-to-all-start = ((bf16[16,3,16,192]{3,2,1,0:T(8,128)(2,1)}), bf16[16,3,16,192]{3,2,1,0:T(8,128)(2,1)S(1)}, u32[]{:S(2)}, u32[]{:S(2)}) async-start(bf16[16,3,16,192]{3,2,1,0:T(8,128)(2,1)} %bitcast.388), calls=%async_computation | async-start | bytes 786432 | tf_op jit(solution)/shard_map/all_to_all | solution.py:645
  128.8 10.2 %all-to-all-done.qkv_ref = bf16[16,3,16,192]{3,2,1,0:T(8,128)(2,1)S(1)} async-done(((bf16[16,3,16,192]{3,2,1,0:T(8,128)(2,1)}), bf16[16,3,16,192]{3,2,1,0:T(8,128)(2,1)S(1)}, u32[]{:S(2)}, u32[]{:S(2)}) %all-to-all-start) | async-done | bytes 294944 | tf_op jit(solution)/shard_map/all_to_all | solution.py:645
  139.8 3.7 shard_map.223
  143.5 3.7 all-to-all-start.1
  147.8 3.0 maximum_maximum_fusion.1.own_2
  152.5 3.5 all-to-all-done.1
  156.7 36.5 %shard_map.224 = (bf16[3,128,768]{2,1,0:T(8,128)(2,1)}, bf16[3,128,768]{2,1,0:T(8,128)(2,1)}, bf16[3,128,768]{2,1,0:T(8,128)(2,1)}, bf16[3,128,3072]{2,1,0:T(8,1...) custom-call(s32[12]{0:T(128)} %and_select_fusion.5.offs, ...), custom_call_target="tpu_custom_call" | custom-call | flops 7247757312 | bytes 9437184 | tf_op jit(solution)/shard_map/pallas_call | solution.py:681
  193.2 3.5 all-to-all-start.2
  196.8 8.6 %shard_map.230 = bf16[2,2,2,384,768]{4,3,2,1,0:T(8,128)(2,1)} custom-call(bf16[384,768]{1,0:T(8,128)(2,1)} %bitcast.386, bf16[384,3072]{1,0:T(8,128)(2,1)} %bitcast.380), custom_call_target="tpu_custom_call" | custom-call | flops 1811939328 | bytes 4718592 | tf_op jit(solution)/shard_map/pallas_call | solution.py:721
  206.4 4.2 %shard_map.225 = bf16[16,3,16,192]{3,2,1,0:T(8,128)(2,1)} custom-call(s32[3]{0:T(128)} %compare_select_fusion.8.parity_ref, bf16[16,3,16,192]{3,2,1,0:T(8,128)(2,1)} %copy-done.6, bf16[16,3,16,128]{3,2,1,0:T(8,128)(2,1)} %copy-done.18), custom_call_target="tpu_custom_call" | custom-call | flops 125829120 | bytes 786432 | tf_op jit(solution)/shard_map/pallas_call | solution.py:748
  210.6 5.7 %all-to-all-start.3 = ((bf16[16,3,16,192]{3,2,1,0:T(8,128)(2,1)}), bf16[16,3,16,192]{3,2,1,0:T(8,128)(2,1)S(1)}, u32[]{:S(2)}, u32[]{:S(2)}) async-start(bf16[16,3,16,192]{3,2,1,0:T(8,128)(2,1)} %shard_map.225), calls=%async_computation.3 | async-start | bytes 786432 | tf_op jit(solution)/shard_map/all_to_all | solution.py:648
  216.3 4.3 %fusion.102 = (bf16[1,2,2,384,768]{4,3,2,1,0:T(8,128)(2,1)S(1)}, bf16[2,2,384,768]{3,2,1,0:T(8,128)(2,1)}) fusion(bf16[2,2,2,384,768]{4,3,2,1,0:T(8,128)(2,1)} %shard_map.230), kind=kLoop, calls=%fused_computation.252 | loop fusion | bytes 9437184 | tf_op jit(solution)/shard_map/slice | solution.py:735
  223.2 8.6 %shard_map.229 = bf16[2,2,2,384,768]{4,3,2,1,0:T(8,128)(2,1)} custom-call(bf16[384,768]{1,0:T(8,128)(2,1)} %bitcast.387, bf16[384,3072]{1,0:T(8,128)(2,1)} %bitcast.379), custom_call_target="tpu_custom_call" | custom-call | flops 1811939328 | bytes 4718592 | tf_op jit(solution)/shard_map/pallas_call | solution.py:721
  232.6 12.3 %shard_map.226.qkv_ref = bf16[3,128,2304]{2,1,0:T(8,128)(2,1)} custom-call(s32[12]{0:T(128)} %and_select_fusion.5.offs, f32[3,128,128]{2,1,0:T(8,128)} %and_select_fusion.bias_ref, bf16[3,128,2304]{2,1,0:T(8,128)(2,1)} %get-tuple-element.36.qkv_ref, bf16[3,128,768]{2,1,0:T(8,128)(2,1)} %get-tuple-element.37.att_ref, ...), custom_call_target="tpu_custom_call" | custom-call | flops 377487360 | bytes 5898240 | tf_op jit(solution)/shard_map/pallas_call | solution.py:759
  244.9 11.4 %shard_map.227 = (bf16[3,128,768]{2,1,0:T(8,128)(2,1)}, f32[1,768]{1,0:T(1,128)}) custom-call(bf16[3,128,768]{2,1,0:T(8,128)(2,1)} %fusion.6.x_ref, bf16[3,128,2304]{2,1,0:T(8,128)(2,1)} %shard_map.226.qkv_ref, f32[3,128,768]{2,1,0:T(8,128)} %get-tuple-element.41.resid_ref, f32[1,768]{1,0:T(1,128)} %reshape.580.gain_ref, bf16[768,768]{1,0:T(8,128)(2,1)} %fusion.place_ref, ...), custom_call_target="tpu_custom_call" | custom-call | flops 1358954496 | bytes 4718592 | tf_op jit(solution)/shard_map/pallas_call | solution.py:789
  258.5 4.2 %fusion.103 = (bf16[1,2,2,384,768]{4,3,2,1,0:T(8,128)(2,1)S(1)}, bf16[2,2,384,768]{3,2,1,0:T(8,128)(2,1)}) fusion(bf16[2,2,2,384,768]{4,3,2,1,0:T(8,128)(2,1)} %shard_map.229), kind=kLoop, calls=%fused_computation.253 | loop fusion | bytes 9437184 | tf_op jit(solution)/shard_map/slice | solution.py:737
  264.4 2.4 collective-permute-done.52
  266.9 1.8 collective-permute-start.53
  272.4 7.1 %shard_map.228 = bf16[2,2,2,384,768]{4,3,2,1,0:T(8,128)(2,1)} custom-call(bf16[384,768]{1,0:T(8,128)(2,1)} %bitcast.382, bf16[384,768]{1,0:T(8,128)(2,1)} %bitcast.384, bf16[384,2304]{1,0:T(8,128)(2,1)} %bitcast.362, bf16[384,768]{1,0:T(8,128)(2,1)} %bitcast.383), custom_call_target="tpu_custom_call" | custom-call | flops 1811939328 | bytes 4718592 | tf_op jit(solution)/shard_map/pallas_call | solution.py:778
  279.5 2.4 collective-permute-start.55
  281.9 2.7 fusion.104
  288.0 12.4 %collective-permute-done.26 = bf16[3,128,768]{2,1,0:T(8,128)(2,1)S(1)} collective-permute-done((bf16[3,128,768]{2,1,0:T(8,128)(2,1)S(1)}, bf16[3,128,768]{2,1,0:T(8,128)(2,1)S(1)}, u32[]{:S(2)}, u32[]{:S(2)}) %collective-permute-start.26) | collective-permute-done | bytes 589856 | tf_op jit(solution)/shard_map/ppermute | solution.py:80
  301.6 2.4 convert_add_fusion
  307.4 2.4 convert_add_fusion.1
  311.3 9.3 %collective-permute-done.44 = bf16[2,4,48,768]{3,2,1,0:T(8,128)(2,1)S(1)} collective-permute-done((bf16[2,4,48,768]{3,2,1,0:T(8,128)(2,1)S(1)}, bf16[2,4,48,768]{3,2,1,0:T(8,128)(2,1)S(1)}, u32[]{:S(2)}, u32[]{:S(2)}) %collective-permute-start.44) | collective-permute-done | bytes 589856 | tf_op jit(solution)/shard_map/ppermute | solution.py:80
  324.0 9.2 %collective-permute-done.36 = bf16[2,4,48,768]{3,2,1,0:T(8,128)(2,1)S(1)} collective-permute-done((bf16[2,4,48,768]{3,2,1,0:T(8,128)(2,1)S(1)}, bf16[2,4,48,768]{3,2,1,0:T(8,128)(2,1)S(1)}, u32[]{:S(2)}, u32[]{:S(2)}) %collective-permute-start.36) | collective-permute-done | bytes 589856 | tf_op jit(solution)/shard_map/ppermute | solution.py:80
  336.6 4.5 %collective-permute-done.45 = bf16[4,48,768]{2,1,0:T(8,128)(2,1)S(1)} collective-permute-done((bf16[4,48,768]{2,1,0:T(8,128)(2,1)S(1)}, bf16[4,48,768]{2,1,0:T(8,128)(2,1)S(1)}, u32[]{:S(2)}, u32[]{:S(2)}) %collective-permute-start.45) | collective-permute-done | bytes 294944 | tf_op jit(solution)/shard_map/ppermute | solution.py:80
  342.5 3.3 collective-permute-done.37
  347.2 3.3 collective-permute-start.41
  352.2 2.8 collective-permute-done.49
  357.1 9.5 %collective-permute-done.41 = bf16[1,2,48,768]{3,2,1,0:T(8,128)(2,1)S(1)} collective-permute-done((bf16[1,2,48,768]{3,2,1,0:T(8,128)(2,1)S(1)}, bf16[1,2,48,768]{3,2,1,0:T(8,128)(2,1)S(1)}, u32[]{:S(2)}, u32[]{:S(2)}) %collective-permute-start.41) | collective-permute-done | bytes 147488 | tf_op jit(solution)/shard_map/ppermute | solution.py:80
  370.0 3.7 collective-permute-done.29
  375.6 8.5 %collective-permute-start.32 = (bf16[1,2,48,768]{3,2,1,0:T(8,128)(2,1)S(1)}, bf16[1,2,48,768]{3,2,1,0:T(8,128)(2,1)S(1)}, u32[]{:S(2)}, u32[]{:S(2)}) collective-permute-start(bf16[1,2,48,768]{3,2,1,0:T(8,128)(2,1)S(1)} %get-tuple-element.95), channel_id=1, source_target_pairs={{0,8},{1,9},{2,10},{3,11},{4,12},{5,13},{6,14},{7,15},{8,0},{9,1},... | collective-permute-start | bytes 442376 | tf_op jit(solution)/shard_map/ppermute | solution.py:80
  384.2 2.4 collective-permute-start.34
  387.3 6.0 %collective-permute-done.33 = bf16[1,2,48,768]{3,2,1,0:T(8,128)(2,1)S(1)} collective-permute-done((bf16[1,2,48,768]{3,2,1,0:T(8,128)(2,1)S(1)}, bf16[1,2,48,768]{3,2,1,0:T(8,128)(2,1)S(1)}, u32[]{:S(2)}, u32[]{:S(2)}) %collective-permute-start.33) | collective-permute-done | bytes 147488 | tf_op jit(solution)/shard_map/ppermute | solution.py:80
  (301 shorter events, 110.8 us)
Async XLA Ops:
  2.4 22.9 %collective-permute-start = (bf16[1,48,1536]{2,1,0:T(8,128)(2,1)S(1)}, bf16[1,48,1536]{2,1,0:T(8,128)(2,1)S(1)}, u32[]{:S(2)}, u32[]{:S(2)}) collective-permute-start(bf16[1,48,1536]{2,1,0:T(8,128)(2,1)S(1)} %get-tuple-element.131), channel_id=1, source_target_pairs={{0,8},{1,9},{2,10},{3,11},{4,12},{5,13},{6,14},{7,15},{8,0},{9,1},... | collective-permute-start | bytes 442376 | tf_op jit(solution)/shard_map/ppermute | solution.py:80
  5.5 19.8 %collective-permute-start.1 = (bf16[1,48,1536]{2,1,0:T(8,128)(2,1)S(1)}, bf16[1,48,1536]{2,1,0:T(8,128)(2,1)S(1)}, u32[]{:S(2)}, u32[]{:S(2)}) collective-permute-start(bf16[1,48,1536]{2,1,0:T(8,128)(2,1)S(1)} %get-tuple-element.131), channel_id=1, source_target_pairs={{0,16},{1,17},{2,18},{3,19},{4,20},{5,21},{6,22},{7,23},{8,24},{9,... | collective-permute-start | bytes 442376 | tf_op jit(solution)/shard_map/ppermute | solution.py:80
  8.1 17.8 %collective-permute-start.2 = (bf16[1,48,1536]{2,1,0:T(8,128)(2,1)S(1)}, bf16[1,48,1536]{2,1,0:T(8,128)(2,1)S(1)}, u32[]{:S(2)}, u32[]{:S(2)}) collective-permute-start(bf16[1,48,1536]{2,1,0:T(8,128)(2,1)S(1)} %get-tuple-element.131), channel_id=1, source_target_pairs={{0,24},{1,25},{2,26},{3,27},{4,28},{5,29},{6,30},{7,31},{8,16},{9,... | collective-permute-start | bytes 442376 | tf_op jit(solution)/shard_map/ppermute | solution.py:80
  8.1 21.8 %collective-permute-start.9 = (bf16[1,48,1536]{2,1,0:T(8,128)(2,1)}, bf16[1,48,1536]{2,1,0:T(8,128)(2,1)S(1)}, u32[]{:S(2)}, u32[]{:S(2)}) collective-permute-start(bf16[1,48,1536]{2,1,0:T(8,128)(2,1)} %bitcast.396), channel_id=1, source_target_pairs={{0,8},{1,9},{2,10},{3,11},{4,12},{5,13},{6,14},{7,15},{8,0},{9,1},... | collective-permute-start | bytes 442376 | tf_op jit(solution)/shard_map/ppermute | solution.py:80
  9.0 21.6 %collective-permute-start.10 = (bf16[1,48,1536]{2,1,0:T(8,128)(2,1)}, bf16[1,48,1536]{2,1,0:T(8,128)(2,1)S(1)}, u32[]{:S(2)}, u32[]{:S(2)}) collective-permute-start(bf16[1,48,1536]{2,1,0:T(8,128)(2,1)} %bitcast.397), channel_id=1, source_target_pairs={{0,16},{1,17},{2,18},{3,19},{4,20},{5,21},{6,22},{7,23},{8,24},{9,... | collective-permute-start | bytes 442376 | tf_op jit(solution)/shard_map/ppermute | solution.py:80
  25.4 10.3 %collective-permute-start.17 = (bf16[1,48,1536]{2,1,0:T(8,128)(2,1)S(1)}, bf16[1,48,1536]{2,1,0:T(8,128)(2,1)S(1)}, u32[]{:S(2)}, u32[]{:S(2)}) collective-permute-start(bf16[1,48,1536]{2,1,0:T(8,128)(2,1)S(1)} %bitcast.400), channel_id=1, source_target_pairs={{0,8},{1,9},{2,10},{3,11},{4,12},{5,13},{6,14},{7,15},{8,0},{9,1},... | collective-permute-start | bytes 442376 | tf_op jit(solution)/shard_map/ppermute | solution.py:80
  25.9 18.9 %collective-permute-start.18 = (bf16[1,48,1536]{2,1,0:T(8,128)(2,1)S(1)}, bf16[1,48,1536]{2,1,0:T(8,128)(2,1)S(1)}, u32[]{:S(2)}, u32[]{:S(2)}) collective-permute-start(bf16[1,48,1536]{2,1,0:T(8,128)(2,1)S(1)} %bitcast.401), channel_id=1, source_target_pairs={{0,16},{1,17},{2,18},{3,19},{4,20},{5,21},{6,22},{7,23},{8,24},{9,... | collective-permute-start | bytes 442376 | tf_op jit(solution)/shard_map/ppermute | solution.py:80
  29.9 16.4 %collective-permute-start.19 = (bf16[1,48,1536]{2,1,0:T(8,128)(2,1)S(1)}, bf16[1,48,1536]{2,1,0:T(8,128)(2,1)S(1)}, u32[]{:S(2)}, u32[]{:S(2)}) collective-permute-start(bf16[1,48,1536]{2,1,0:T(8,128)(2,1)S(1)} %bitcast.402), channel_id=1, source_target_pairs={{0,24},{1,25},{2,26},{3,27},{4,28},{5,29},{6,30},{7,31},{8,16},{9,... | collective-permute-start | bytes 442376 | tf_op jit(solution)/shard_map/ppermute | solution.py:80
  30.6 18.2 %collective-permute-start.3 = (bf16[4,48,768]{2,1,0:T(8,128)(2,1)S(1)}, bf16[4,48,768]{2,1,0:T(8,128)(2,1)S(1)}, u32[]{:S(2)}, u32[]{:S(2)}) collective-permute-start(bf16[4,48,768]{2,1,0:T(8,128)(2,1)S(1)} %get-tuple-element.121), channel_id=1, source_target_pairs={{0,1},{1,0},{2,3},{3,2},{4,5},{5,4},{6,7},{7,6},{8,9},{9,8},{10,11... | collective-permute-start | bytes 884744 | tf_op jit(solution)/shard_map/ppermute | solution.py:80
  34.0 15.4 %collective-permute-start.5 = (bf16[4,48,768]{2,1,0:T(8,128)(2,1)S(1)}, bf16[4,48,768]{2,1,0:T(8,128)(2,1)S(1)}, u32[]{:S(2)}, u32[]{:S(2)}) collective-permute-start(bf16[4,48,768]{2,1,0:T(8,128)(2,1)S(1)} %get-tuple-element.120), channel_id=1, source_target_pairs={{0,4},{1,5},{2,6},{3,7},{4,0},{5,1},{6,2},{7,3},{8,12},{9,13},{10,... | collective-permute-start | bytes 884744 | tf_op jit(solution)/shard_map/ppermute | solution.py:80
  35.7 14.4 %collective-permute-start.12 = (bf16[4,48,768]{2,1,0:T(8,128)(2,1)S(1)}, bf16[4,48,768]{2,1,0:T(8,128)(2,1)S(1)}, u32[]{:S(2)}, u32[]{:S(2)}) collective-permute-start(bf16[4,48,768]{2,1,0:T(8,128)(2,1)S(1)} %get-tuple-element.113), channel_id=1, source_target_pairs={{0,1},{1,0},{2,3},{3,2},{4,5},{5,4},{6,7},{7,6},{8,9},{9,8},{10,11... | collective-permute-start | bytes 884744 | tf_op jit(solution)/shard_map/ppermute | solution.py:80
  47.3 10.2 %collective-permute-start.20 = (bf16[4,48,768]{2,1,0:T(8,128)(2,1)S(1)}, bf16[4,48,768]{2,1,0:T(8,128)(2,1)S(1)}, u32[]{:S(2)}, u32[]{:S(2)}) collective-permute-start(bf16[4,48,768]{2,1,0:T(8,128)(2,1)S(1)} %get-tuple-element.105), channel_id=1, source_target_pairs={{0,1},{1,0},{2,3},{3,2},{4,5},{5,4},{6,7},{7,6},{8,9},{9,8},{10,11... | collective-permute-start | bytes 884744 | tf_op jit(solution)/shard_map/ppermute | solution.py:80
  48.9 18.4 %collective-permute-start.4 = (bf16[2,4,48,768]{3,2,1,0:T(8,128)(2,1)S(1)}, bf16[2,4,48,768]{3,2,1,0:T(8,128)(2,1)S(1)}, u32[]{:S(2)}, u32[]{:S(2)}) collective-permute-start(bf16[2,4,48,768]{3,2,1,0:T(8,128)(2,1)S(1)} %get-tuple-element.117), channel_id=1, source_target_pairs={{0,4},{1,5},{2,6},{3,7},{4,0},{5,1},{6,2},{7,3},{8,12},{9,13},{10,... | collective-permute-start | bytes 1769480 | tf_op jit(solution)/shard_map/ppermute | solution.py:80
  49.5 20.5 %collective-permute-start.6 = (bf16[2,4,48,768]{3,2,1,0:T(8,128)(2,1)S(1)}, bf16[2,4,48,768]{3,2,1,0:T(8,128)(2,1)S(1)}, u32[]{:S(2)}, u32[]{:S(2)}) collective-permute-start(bf16[2,4,48,768]{3,2,1,0:T(8,128)(2,1)S(1)} %get-tuple-element.115), channel_id=1, source_target_pairs={{0,1},{1,0},{2,3},{3,2},{4,5},{5,4},{6,7},{7,6},{8,9},{9,8},{10,11... | collective-permute-start | bytes 1769480 | tf_op jit(solution)/shard_map/ppermute | solution.py:80
  50.2 27.2 %collective-permute-start.22 = (bf16[4,48,768]{2,1,0:T(8,128)(2,1)}, bf16[4,48,768]{2,1,0:T(8,128)(2,1)}, u32[]{:S(2)}, u32[]{:S(2)}) collective-permute-start(bf16[4,48,768]{2,1,0:T(8,128)(2,1)} %get-tuple-element.104), channel_id=1, source_target_pairs={{0,4},{1,5},{2,6},{3,7},{4,0},{5,1},{6,2},{7,3},{8,12},{9,13},{10,... | collective-permute-start | bytes 884744 | tf_op jit(solution)/shard_map/ppermute | solution.py:80
  54.7 31.7 %collective-permute-start.13 = (bf16[2,4,48,768]{3,2,1,0:T(8,128)(2,1)}, bf16[2,4,48,768]{3,2,1,0:T(8,128)(2,1)}, u32[]{:S(2)}, u32[]{:S(2)}) collective-permute-start(bf16[2,4,48,768]{3,2,1,0:T(8,128)(2,1)} %get-tuple-element.109), channel_id=1, source_target_pairs={{0,4},{1,5},{2,6},{3,7},{4,0},{5,1},{6,2},{7,3},{8,12},{9,13},{10,... | collective-permute-start | bytes 1769480 | tf_op jit(solution)/shard_map/ppermute | solution.py:80
  57.5 32.9 %collective-permute-start.15 = (bf16[2,4,48,768]{3,2,1,0:T(8,128)(2,1)}, bf16[2,4,48,768]{3,2,1,0:T(8,128)(2,1)}, u32[]{:S(2)}, u32[]{:S(2)}) collective-permute-start(bf16[2,4,48,768]{3,2,1,0:T(8,128)(2,1)} %get-tuple-element.107), channel_id=1, source_target_pairs={{0,1},{1,0},{2,3},{3,2},{4,5},{5,4},{6,7},{7,6},{8,9},{9,8},{10,11... | collective-permute-start | bytes 1769480 | tf_op jit(solution)/shard_map/ppermute | solution.py:80
  67.3 28.4 %collective-permute-start.21 = (bf16[2,4,48,768]{3,2,1,0:T(8,128)(2,1)}, bf16[2,4,48,768]{3,2,1,0:T(8,128)(2,1)}, u32[]{:S(2)}, u32[]{:S(2)}) collective-permute-start(bf16[2,4,48,768]{3,2,1,0:T(8,128)(2,1)} %get-tuple-element.101), channel_id=1, source_target_pairs={{0,4},{1,5},{2,6},{3,7},{4,0},{5,1},{6,2},{7,3},{8,12},{9,13},{10,... | collective-permute-start | bytes 1769480 | tf_op jit(solution)/shard_map/ppermute | solution.py:80
  72.7 34.8 %collective-permute-start.7 = (bf16[2,2,2,4,48,768]{5,4,3,2,1,0:T(8,128)(2,1)}, bf16[2,2,2,4,48,768]{5,4,3,2,1,0:T(8,128)(2,1)S(1)}, u32[]{:S(2)}, u32[]{:S(2)}) collective-permute-start(bf16[2,2,2,4,48,768]{5,4,3,2,1,0:T(8,128)(2,1)} %pad_maximum_fusion), channel_id=1, source_target_pairs={{0,2},{1,3},{2,0},{3,1},{4,6},{5,7},{6,4},{7,5},{8,10},{9,11},{10,... | collective-permute-start | bytes 7077896 | tf_op jit(solution)/shard_map/ppermute | solution.py:80
  77.3 49.5 %collective-permute-start.8 = (f32[15,128]{1,0:T(8,128)}, f32[15,128]{1,0:T(8,128)}, u32[]{:S(2)}, u32[]{:S(2)}) collective-permute-start(f32[15,128]{1,0:T(8,128)} %maximum_bitcast_fusion.14), channel_id=1, source_target_pairs={{0,1},{1,0},{2,3},{3,2},{4,5},{5,4},{6,7},{7,6},{8,9},{9,8},{10,11... | collective-permute-start | bytes 23048 | tf_op jit(solution)/shard_map/ppermute | solution.py:80
  86.4 11.6 %collective-permute-start.23 = (bf16[2,4,48,768]{3,2,1,0:T(8,128)(2,1)S(1)}, bf16[2,4,48,768]{3,2,1,0:T(8,128)(2,1)S(1)}, u32[]{:S(2)}, u32[]{:S(2)}) collective-permute-start(bf16[2,4,48,768]{3,2,1,0:T(8,128)(2,1)S(1)} %get-tuple-element.99), channel_id=1, source_target_pairs={{0,1},{1,0},{2,3},{3,2},{4,5},{5,4},{6,7},{7,6},{8,9},{9,8},{10,11... | collective-permute-start | bytes 1769480 | tf_op jit(solution)/shard_map/ppermute | solution.py:80
  93.3 59.2 %collective-permute-start.16 = (bf16[2,2,2,4,48,768]{5,4,3,2,1,0:T(8,128)(2,1)}, bf16[2,2,2,4,48,768]{5,4,3,2,1,0:T(8,128)(2,1)}, u32[]{:S(2)}, u32[]{:S(2)}) collective-permute-start(bf16[2,2,2,4,48,768]{5,4,3,2,1,0:T(8,128)(2,1)} %pad_maximum_fusion.1), channel_id=1, source_target_pairs={{0,2},{1,3},{2,0},{3,1},{4,6},{5,7},{6,4},{7,5},{8,10},{9,11},{10,... | collective-permute-start | bytes 7077896 | tf_op jit(solution)/shard_map/ppermute | solution.py:80
  99.8 52.7 %collective-permute-start.24 = (bf16[2,2,2,4,48,768]{5,4,3,2,1,0:T(8,128)(2,1)}, bf16[2,2,2,4,48,768]{5,4,3,2,1,0:T(8,128)(2,1)}, u32[]{:S(2)}, u32[]{:S(2)}) collective-permute-start(bf16[2,2,2,4,48,768]{5,4,3,2,1,0:T(8,128)(2,1)} %pad_maximum_fusion.2), channel_id=1, source_target_pairs={{0,2},{1,3},{2,0},{3,1},{4,6},{5,7},{6,4},{7,5},{8,10},{9,11},{10,... | collective-permute-start | bytes 7077896 | tf_op jit(solution)/shard_map/ppermute | solution.py:80
  119.8 19.2 %all-to-all-start = ((bf16[16,3,16,192]{3,2,1,0:T(8,128)(2,1)}), bf16[16,3,16,192]{3,2,1,0:T(8,128)(2,1)S(1)}, u32[]{:S(2)}, u32[]{:S(2)}) async-start(bf16[16,3,16,192]{3,2,1,0:T(8,128)(2,1)} %bitcast.388), calls=%async_computation | async-start | bytes 786432 | tf_op jit(solution)/shard_map/all_to_all | solution.py:645
  143.5 12.5 %all-to-all-start.1 = ((bf16[16,3,16,128]{3,2,1,0:T(8,128)(2,1)}), bf16[16,3,16,128]{3,2,1,0:T(8,128)(2,1)S(1)}, u32[]{:S(2)}, u32[]{:S(2)}) async-start(bf16[16,3,16,128]{3,2,1,0:T(8,128)(2,1)} %shard_map.223), calls=%async_computation.1 | async-start | bytes 393216 | tf_op jit(solution)/shard_map/all_to_all | solution.py:648
  193.2 12.5 %all-to-all-start.2 = ((bf16[16,3,16,128]{3,2,1,0:T(8,128)(2,1)}), bf16[16,3,16,128]{3,2,1,0:T(8,128)(2,1)S(1)}, u32[]{:S(2)}, u32[]{:S(2)}) async-start(bf16[16,3,16,128]{3,2,1,0:T(8,128)(2,1)} %bitcast.395), calls=%async_computation.2 | async-start | bytes 393216 | tf_op jit(solution)/shard_map/all_to_all | solution.py:645
  210.6 21.3 %all-to-all-start.3 = ((bf16[16,3,16,192]{3,2,1,0:T(8,128)(2,1)}), bf16[16,3,16,192]{3,2,1,0:T(8,128)(2,1)S(1)}, u32[]{:S(2)}, u32[]{:S(2)}) async-start(bf16[16,3,16,192]{3,2,1,0:T(8,128)(2,1)} %shard_map.225), calls=%async_computation.3 | async-start | bytes 786432 | tf_op jit(solution)/shard_map/all_to_all | solution.py:648
  220.7 80.9 %collective-permute-start.43 = (bf16[2,2,384,768]{3,2,1,0:T(8,128)(2,1)}, bf16[2,2,384,768]{3,2,1,0:T(8,128)(2,1)}, u32[]{:S(2)}, u32[]{:S(2)}) collective-permute-start(bf16[2,2,384,768]{3,2,1,0:T(8,128)(2,1)} %get-tuple-element.62), channel_id=1, source_target_pairs={{0,2},{1,3},{2,0},{3,1},{4,6},{5,7},{6,4},{7,5},{8,10},{9,11},{10,... | collective-permute-start | bytes 7077896 | tf_op jit(solution)/shard_map/ppermute | solution.py:80
  221.1 42.2 %collective-permute-start.25 = (bf16[3,128,768]{2,1,0:T(8,128)(2,1)S(1)}, bf16[3,128,768]{2,1,0:T(8,128)(2,1)}, u32[]{:S(2)}, u32[]{:S(2)}) collective-permute-start(bf16[3,128,768]{2,1,0:T(8,128)(2,1)S(1)} %copy-done.19), channel_id=1, source_target_pairs={{0,1},{1,0},{2,3},{3,2},{4,5},{5,4},{6,7},{7,6},{8,9},{9,8},{10,11... | collective-permute-start | bytes 1769480 | tf_op jit(solution)/shard_map/ppermute | solution.py:80
  262.7 44.7 %collective-permute-start.35 = (bf16[2,2,384,768]{3,2,1,0:T(8,128)(2,1)}, bf16[2,2,384,768]{3,2,1,0:T(8,128)(2,1)}, u32[]{:S(2)}, u32[]{:S(2)}) collective-permute-start(bf16[2,2,384,768]{3,2,1,0:T(8,128)(2,1)} %get-tuple-element.64), channel_id=1, source_target_pairs={{0,2},{1,3},{2,0},{3,1},{4,6},{5,7},{6,4},{7,5},{8,10},{9,11},{10,... | collective-permute-start | bytes 7077896 | tf_op jit(solution)/shard_map/ppermute | solution.py:80
  284.6 62.6 %collective-permute-start.27 = (bf16[2,2,384,768]{3,2,1,0:T(8,128)(2,1)S(1)}, bf16[2,2,384,768]{3,2,1,0:T(8,128)(2,1)S(1)}, u32[]{:S(2)}, u32[]{:S(2)}) collective-permute-start(bf16[2,2,384,768]{3,2,1,0:T(8,128)(2,1)S(1)} %get-tuple-element.66), channel_id=1, source_target_pairs={{0,2},{1,3},{2,0},{3,1},{4,6},{5,7},{6,4},{7,5},{8,10},{9,11},{10,... | collective-permute-start | bytes 7077896 | tf_op jit(solution)/shard_map/ppermute | solution.py:80
  284.7 15.7 %collective-permute-start.26 = (bf16[3,128,768]{2,1,0:T(8,128)(2,1)S(1)}, bf16[3,128,768]{2,1,0:T(8,128)(2,1)S(1)}, u32[]{:S(2)}, u32[]{:S(2)}) collective-permute-start(bf16[3,128,768]{2,1,0:T(8,128)(2,1)S(1)} %copy-done.21), channel_id=1, source_target_pairs={{0,1},{1,0},{2,3},{3,2},{4,5},{5,4},{6,7},{7,6},{8,9},{9,8},{10,11... | collective-permute-start | bytes 1769480 | tf_op jit(solution)/shard_map/ppermute | solution.py:80
  304.3 16.3 %collective-permute-start.44 = (bf16[2,4,48,768]{3,2,1,0:T(8,128)(2,1)S(1)}, bf16[2,4,48,768]{3,2,1,0:T(8,128)(2,1)S(1)}, u32[]{:S(2)}, u32[]{:S(2)}) collective-permute-start(bf16[2,4,48,768]{3,2,1,0:T(8,128)(2,1)S(1)} %fusion.24), channel_id=1, source_target_pairs={{0,4},{1,5},{2,6},{3,7},{4,0},{5,1},{6,2},{7,3},{8,12},{9,13},{10,... | collective-permute-start | bytes 1769480 | tf_op jit(solution)/shard_map/ppermute | solution.py:80
  305.9 16.4 %collective-permute-start.46 = (bf16[2,4,48,768]{3,2,1,0:T(8,128)(2,1)S(1)}, bf16[2,4,48,768]{3,2,1,0:T(8,128)(2,1)S(1)}, u32[]{:S(2)}, u32[]{:S(2)}) collective-permute-start(bf16[2,4,48,768]{3,2,1,0:T(8,128)(2,1)S(1)} %fusion.25), channel_id=1, source_target_pairs={{0,1},{1,0},{2,3},{3,2},{4,5},{5,4},{6,7},{7,6},{8,9},{9,8},{10,11... | collective-permute-start | bytes 1769480 | tf_op jit(solution)/shard_map/ppermute | solution.py:80
  310.1 23.1 %collective-permute-start.36 = (bf16[2,4,48,768]{3,2,1,0:T(8,128)(2,1)S(1)}, bf16[2,4,48,768]{3,2,1,0:T(8,128)(2,1)S(1)}, u32[]{:S(2)}, u32[]{:S(2)}) collective-permute-start(bf16[2,4,48,768]{3,2,1,0:T(8,128)(2,1)S(1)} %fusion.22), channel_id=1, source_target_pairs={{0,4},{1,5},{2,6},{3,7},{4,0},{5,1},{6,2},{7,3},{8,12},{9,13},{10,... | collective-permute-start | bytes 1769480 | tf_op jit(solution)/shard_map/ppermute | solution.py:80
  310.7 24.2 %collective-permute-start.38 = (bf16[2,4,48,768]{3,2,1,0:T(8,128)(2,1)S(1)}, bf16[2,4,48,768]{3,2,1,0:T(8,128)(2,1)S(1)}, u32[]{:S(2)}, u32[]{:S(2)}) collective-permute-start(bf16[2,4,48,768]{3,2,1,0:T(8,128)(2,1)S(1)} %fusion.23), channel_id=1, source_target_pairs={{0,1},{1,0},{2,3},{3,2},{4,5},{5,4},{6,7},{7,6},{8,9},{9,8},{10,11... | collective-permute-start | bytes 1769480 | tf_op jit(solution)/shard_map/ppermute | solution.py:80
  320.8 20.4 %collective-permute-start.45 = (bf16[4,48,768]{2,1,0:T(8,128)(2,1)S(1)}, bf16[4,48,768]{2,1,0:T(8,128)(2,1)S(1)}, u32[]{:S(2)}, u32[]{:S(2)}) collective-permute-start(bf16[4,48,768]{2,1,0:T(8,128)(2,1)S(1)} %fusion.58), channel_id=1, source_target_pairs={{0,1},{1,0},{2,3},{3,2},{4,5},{5,4},{6,7},{7,6},{8,9},{9,8},{10,11... | collective-permute-start | bytes 884744 | tf_op jit(solution)/shard_map/ppermute | solution.py:80
  322.5 18.8 %collective-permute-start.47 = (bf16[4,48,768]{2,1,0:T(8,128)(2,1)S(1)}, bf16[4,48,768]{2,1,0:T(8,128)(2,1)S(1)}, u32[]{:S(2)}, u32[]{:S(2)}) collective-permute-start(bf16[4,48,768]{2,1,0:T(8,128)(2,1)S(1)} %fusion.59), channel_id=1, source_target_pairs={{0,4},{1,5},{2,6},{3,7},{4,0},{5,1},{6,2},{7,3},{8,12},{9,13},{10,... | collective-permute-start | bytes 884744 | tf_op jit(solution)/shard_map/ppermute | solution.py:80
  333.4 12.4 %collective-permute-start.37 = (bf16[4,48,768]{2,1,0:T(8,128)(2,1)S(1)}, bf16[4,48,768]{2,1,0:T(8,128)(2,1)S(1)}, u32[]{:S(2)}, u32[]{:S(2)}) collective-permute-start(bf16[4,48,768]{2,1,0:T(8,128)(2,1)S(1)} %fusion.56), channel_id=1, source_target_pairs={{0,1},{1,0},{2,3},{3,2},{4,5},{5,4},{6,7},{7,6},{8,9},{9,8},{10,11... | collective-permute-start | bytes 884744 | tf_op jit(solution)/shard_map/ppermute | solution.py:80
  335.1 11.3 %collective-permute-start.39 = (bf16[4,48,768]{2,1,0:T(8,128)(2,1)S(1)}, bf16[4,48,768]{2,1,0:T(8,128)(2,1)S(1)}, u32[]{:S(2)}, u32[]{:S(2)}) collective-permute-start(bf16[4,48,768]{2,1,0:T(8,128)(2,1)S(1)} %fusion.57), channel_id=1, source_target_pairs={{0,4},{1,5},{2,6},{3,7},{4,0},{5,1},{6,2},{7,3},{8,12},{9,13},{10,... | collective-permute-start | bytes 884744 | tf_op jit(solution)/shard_map/ppermute | solution.py:80
  341.3 10.2 %collective-permute-start.48 = (bf16[1,2,48,768]{3,2,1,0:T(8,128)(2,1)S(1)}, bf16[1,2,48,768]{3,2,1,0:T(8,128)(2,1)S(1)}, u32[]{:S(2)}, u32[]{:S(2)}) collective-permute-start(bf16[1,2,48,768]{3,2,1,0:T(8,128)(2,1)S(1)} %get-tuple-element.89), channel_id=1, source_target_pairs={{0,8},{1,9},{2,10},{3,11},{4,12},{5,13},{6,14},{7,15},{8,0},{9,1},... | collective-permute-start | bytes 442376 | tf_op jit(solution)/shard_map/ppermute | solution.py:80
  342.0 13.0 %collective-permute-start.49 = (bf16[1,2,48,768]{3,2,1,0:T(8,128)(2,1)S(1)}, bf16[1,2,48,768]{3,2,1,0:T(8,128)(2,1)S(1)}, u32[]{:S(2)}, u32[]{:S(2)}) collective-permute-start(bf16[1,2,48,768]{3,2,1,0:T(8,128)(2,1)S(1)} %get-tuple-element.90), channel_id=1, source_target_pairs={{0,16},{1,17},{2,18},{3,19},{4,20},{5,21},{6,22},{7,23},{8,24},{9,... | collective-permute-start | bytes 442376 | tf_op jit(solution)/shard_map/ppermute | solution.py:80
  346.6 10.6 %collective-permute-start.40 = (bf16[1,2,48,768]{3,2,1,0:T(8,128)(2,1)S(1)}, bf16[1,2,48,768]{3,2,1,0:T(8,128)(2,1)S(1)}, u32[]{:S(2)}, u32[]{:S(2)}) collective-permute-start(bf16[1,2,48,768]{3,2,1,0:T(8,128)(2,1)S(1)} %get-tuple-element.92), channel_id=1, source_target_pairs={{0,8},{1,9},{2,10},{3,11},{4,12},{5,13},{6,14},{7,15},{8,0},{9,1},... | collective-permute-start | bytes 442376 | tf_op jit(solution)/shard_map/ppermute | solution.py:80
  347.2 19.5 %collective-permute-start.41 = (bf16[1,2,48,768]{3,2,1,0:T(8,128)(2,1)S(1)}, bf16[1,2,48,768]{3,2,1,0:T(8,128)(2,1)S(1)}, u32[]{:S(2)}, u32[]{:S(2)}) collective-permute-start(bf16[1,2,48,768]{3,2,1,0:T(8,128)(2,1)S(1)} %get-tuple-element.93), channel_id=1, source_target_pairs={{0,16},{1,17},{2,18},{3,19},{4,20},{5,21},{6,22},{7,23},{8,24},{9,... | collective-permute-start | bytes 442376 | tf_op jit(solution)/shard_map/ppermute | solution.py:80
  351.5 15.1 %collective-permute-start.42 = (bf16[1,2,48,768]{3,2,1,0:T(8,128)(2,1)S(1)}, bf16[1,2,48,768]{3,2,1,0:T(8,128)(2,1)S(1)}, u32[]{:S(2)}, u32[]{:S(2)}) collective-permute-start(bf16[1,2,48,768]{3,2,1,0:T(8,128)(2,1)S(1)} %get-tuple-element.94), channel_id=1, source_target_pairs={{0,24},{1,25},{2,26},{3,27},{4,28},{5,29},{6,30},{7,31},{8,16},{9,... | collective-permute-start | bytes 442376 | tf_op jit(solution)/shard_map/ppermute | solution.py:80
  355.0 11.8 %collective-permute-start.28 = (bf16[2,4,48,768]{3,2,1,0:T(8,128)(2,1)S(1)}, bf16[2,4,48,768]{3,2,1,0:T(8,128)(2,1)S(1)}, u32[]{:S(2)}, u32[]{:S(2)}) collective-permute-start(bf16[2,4,48,768]{3,2,1,0:T(8,128)(2,1)S(1)} %fusion.20), channel_id=1, source_target_pairs={{0,4},{1,5},{2,6},{3,7},{4,0},{5,1},{6,2},{7,3},{8,12},{9,13},{10,... | collective-permute-start | bytes 1769480 | tf_op jit(solution)/shard_map/ppermute | solution.py:80
  355.5 12.9 %collective-permute-start.30 = (bf16[2,4,48,768]{3,2,1,0:T(8,128)(2,1)S(1)}, bf16[2,4,48,768]{3,2,1,0:T(8,128)(2,1)S(1)}, u32[]{:S(2)}, u32[]{:S(2)}) collective-permute-start(bf16[2,4,48,768]{3,2,1,0:T(8,128)(2,1)S(1)} %fusion.21), channel_id=1, source_target_pairs={{0,1},{1,0},{2,3},{3,2},{4,5},{5,4},{6,7},{7,6},{8,9},{9,8},{10,11... | collective-permute-start | bytes 1769480 | tf_op jit(solution)/shard_map/ppermute | solution.py:80
  375.6 11.7 %collective-permute-start.32 = (bf16[1,2,48,768]{3,2,1,0:T(8,128)(2,1)S(1)}, bf16[1,2,48,768]{3,2,1,0:T(8,128)(2,1)S(1)}, u32[]{:S(2)}, u32[]{:S(2)}) collective-permute-start(bf16[1,2,48,768]{3,2,1,0:T(8,128)(2,1)S(1)} %get-tuple-element.95), channel_id=1, source_target_pairs={{0,8},{1,9},{2,10},{3,11},{4,12},{5,13},{6,14},{7,15},{8,0},{9,1},... | collective-permute-start | bytes 442376 | tf_op jit(solution)/shard_map/ppermute | solution.py:80
  (53 other events, 562.4 us)

commit v2 on v1

v2 whole, which is shorter than its diff:
```python
from functools import partial

import jax
import jax.numpy as jnp
from jax import lax
from jax.experimental import pallas as pl
from jax.experimental.pallas import tpu as pltpu
from jax.sharding import PartitionSpec as P

HD = 64
DILATION_SMALL = 8
NORM_EPSILON = 1e-05
MASKED_SCORE = -1e30
SCALE = HD ** (-0.5)
F32 = jnp.float32
BF16 = jnp.bfloat16
ANY = pl.BlockSpec(memory_space=pl.ANY)
SMEM = pl.BlockSpec(memory_space=pltpu.SMEM)
VMEM_LIMIT = 56 * 1024 * 1024


def nn(left, right):
    return lax.dot_general(left, right, (((1,), (0,)), ((), ())), preferred_element_type=F32)


def nt(left, right):
    return lax.dot_general(left, right, (((1,), (1,)), ((), ())), preferred_element_type=F32)


def tn(left, right):
    return lax.dot_general(left, right, (((0,), (0,)), ((), ())), preferred_element_type=F32)


def row_norm(values):
    center = jnp.mean(values, axis=-1, keepdims=True)
    spread = jnp.mean(values * values, axis=-1, keepdims=True) - center * center
    inverse = lax.rsqrt(spread + NORM_EPSILON)
    return (values - center) * inverse, inverse


def row_norm_back(incoming, normal, inverse, gain_row):
    scaled = incoming * gain_row
    first_mean = jnp.mean(scaled, axis=-1, keepdims=True)
    second_mean = jnp.mean(scaled * normal, axis=-1, keepdims=True)
    return inverse * (scaled - first_mean - normal * second_mean)


def three_parts(values):
    high = values.astype(BF16)
    rest = values - high.astype(F32)
    middle = rest.astype(BF16)
    low = (rest - middle.astype(F32)).astype(BF16)
    return high, middle, low


def gelu_parts(values):
    expo = jnp.exp(values * values * -0.5)
    term = 1.0 / (1.0 + (0.3275911 * 0.7071067811865476) * jnp.abs(values))
    poly = term * (
        0.254829592
        + term
        * (-0.284496736 + term * (1.421413741 + term * (-1.453152027 + term * 1.061405429)))
    )
    tail = 0.5 * poly * expo
    phi = jnp.where(values >= 0.0, 1.0 - tail, tail)
    return values * phi, phi + values * expo * 0.3989422804014327


def iota(shape, dim):
    return lax.broadcasted_iota(jnp.int32, shape, dim)


def permute(value, target):
    seq_size, head_size = lax.axis_size("seq"), lax.axis_size("head")
    pairs = []
    for s in range(seq_size):
        for h in range(head_size):
            to_seq, to_head = target(s, h)
            pairs.append((s * head_size + h, to_seq * head_size + to_head))
    return lax.ppermute(value, ("seq", "head"), pairs)


def exchange(value, seq_mask, head_mask):
    return permute(value, lambda s, h: (s ^ seq_mask, h ^ head_mask))


def exchange_near(value, turn):
    return permute(value, lambda s, h: (s, h ^ 1) if (s & 1) == turn else (s ^ 2, h))


def far_stages(seq_size):
    unit, left, stages = 4, seq_size // 4, []
    while left > 1:
        radix = 4 if left % 4 == 0 else 2
        stages.append((unit, radix))
        unit, left = unit * radix, left // radix
    return stages


def join(pieces, earlier=(), splits=None):
    rows, width = pieces[0].shape
    count = len(pieces)
    splits = splits or (width,)
    starts = [sum(splits[:i]) for i in range(len(splits))]
    if rows % 16:
        whole_array = jnp.concatenate(pieces)
        out = [whole_array[:, start : start + size] for start, size in zip(starts, splits)]
        return out if len(splits) > 1 else out[0]

    def kernel(*refs):
        refs = refs[len(earlier) :]
        sources, targets, sems = refs[:count], refs[count:-1], refs[-1]
        copies = [
            pltpu.make_async_copy(
                source.at[:, pl.ds(start, size)], target.at[pl.ds(i * rows, rows)], sems.at[i, j]
            )
            for i, source in enumerate(sources)
            for j, (target, start, size) in enumerate(zip(targets, starts, splits))
        ]
        start_all(copies)
        wait_all(copies)

    out = pl.pallas_call(
        kernel,
        in_specs=[ANY] * len(earlier) + [pl.BlockSpec(memory_space=pltpu.VMEM)] * count,
        out_specs=[ANY] * len(splits),
        out_shape=[jax.ShapeDtypeStruct((count * rows, size), pieces[0].dtype) for size in splits],
        scratch_shapes=[pltpu.SemaphoreType.DMA((count, len(splits)))],
        cost_estimate=pl.CostEstimate(flops=2_000_000_000, bytes_accessed=0, transcendentals=0),
    )(*earlier, *pieces)
    return out if len(splits) > 1 else out[0]


def gate(value, *earlier):
    def kernel(*refs):
        pass

    return pl.pallas_call(
        kernel,
        in_specs=[ANY] * (len(earlier) + 1),
        out_specs=ANY,
        out_shape=jax.ShapeDtypeStruct(value.shape, value.dtype),
        input_output_aliases={len(earlier): 0},
        cost_estimate=pl.CostEstimate(flops=0, bytes_accessed=0, transcendentals=0),
    )(*earlier, value)


def after(value, earlier):
    zero = earlier[(0,) * earlier.ndim].astype(F32) * 0.0
    return value + zero.astype(value.dtype)


def gather_core(shard):
    core = lax.axis_index("seq") & 1
    half = shard.shape[0] // 2
    kept = lax.dynamic_slice_in_dim(shard, core * half, half)
    sent = lax.dynamic_slice_in_dim(shard, (1 - core) * half, half)
    return jnp.concatenate([kept, exchange(sent, 1, 0)])


def gather_far(held, earlier=()):
    for unit, radix in far_stages(lax.axis_size("seq")):
        pieces = [held] + [exchange(held, unit * i, 0) for i in range(1, radix)]
        held = join(pieces, earlier) if earlier else jnp.concatenate(pieces)
    return held


def scatter_first(kept, sent):
    got = exchange_near(sent, 1)
    block = kept.shape[1]

    def total(index):
        return kept[index] + got[index * block : (index + 1) * block].astype(F32)

    return total(0), total(1).astype(BF16), got


def scatter_second(kept, sent):
    got = exchange_near(sent, 0)
    total = kept + got[: kept.shape[0]].astype(F32)
    unit, radix = far_stages(lax.axis_size("seq"))[-1]
    total = total.reshape(radix, -1, total.shape[-1])
    return total[0], [total[i].astype(BF16) for i in range(1, radix)], got


def scatter_far(kept, sent):
    stages = far_stages(lax.axis_size("seq"))
    for stage in reversed(range(len(stages))):
        unit, radix = stages[stage]
        for i, piece in enumerate(sent):
            kept = kept + exchange(piece, unit * (i + 1), 0).astype(F32)
        if stage:
            held = kept.reshape(stages[stage - 1][1], -1, kept.shape[-1])
            kept, sent = held[0], [piece.astype(BF16) for piece in held[1:]]
    return kept


def to_rows(sums):
    high = lax.reduce_precision(sums, 8, 7)
    low = sums - high
    spare = jnp.zeros((GAIN_ROWS - 2 * sums.shape[0], sums.shape[1]), F32)
    return jnp.concatenate([high, low, spare]).astype(BF16)


def from_rows(rows, count):
    return rows[:count].astype(F32) + rows[count : 2 * count].astype(F32)


GAIN_ROWS = 16


def scatter_core(held):
    core = lax.axis_index("seq") & 1
    half = held.shape[0] // 2
    kept, got = held[:half], exchange(held[half:], 1, 0)
    first = jnp.where(core == 0, kept, got)
    second = jnp.where(core == 0, got, kept)
    return jnp.concatenate([first, second])


def stream_copies(pieces, columns, target, sems, core):
    block = target.shape[1] // 4
    blocks = [
        piece.at[pl.ds(start, block), columns]
        for piece in pieces
        for start in range(0, piece.shape[0], block)
    ]
    copies = []
    for index, source in enumerate(blocks):
        part, second, first = index // 4, index // 2 % 2, index % 2
        straight = (core ^ part) == 0
        x = jnp.where(straight, first, second)
        y = jnp.where(straight, second, first)
        row = pl.multiple_of((2 * part + y) * block, block)
        copies.append(
            pltpu.make_async_copy(source, target.at[x, pl.ds(row, block)], sems.at[index])
        )
    return copies


def start_all(copies):
    for copy in copies:
        copy.start()


def wait_all(copies):
    for copy in copies:
        copy.wait()


def pair_columns(pair, per_group, width):
    group, inside = divmod(2 * pair, per_group)
    start = group * 3 * width + inside * HD
    return [slice(start + e * width, start + e * width + 2 * HD) for e in range(3)]


def slot_select(offset, groups, positions):
    shape = (groups, positions)
    return (iota(shape, 1) == DILATION_SMALL * iota(shape, 0) + offset).astype(BF16)


def slot_spread(offs, pair, groups, positions, times=1):
    shape = (positions, 2 * groups * times)
    slot = iota(shape, 1) & (2 * groups - 1)
    offset = jnp.where(slot < groups, offs[2 * pair], offs[2 * pair + 1])
    return (iota(shape, 0) == DILATION_SMALL * (slot & (groups - 1)) + offset).astype(BF16)


def side_masks():
    lane = iota((1, 2 * HD), 1)
    return (lane < HD).astype(BF16), (lane >= HD).astype(BF16)


def beside(even, odd):
    nothing = jnp.zeros_like(even)
    return jnp.concatenate(
        [jnp.concatenate([even, nothing], axis=1), jnp.concatenate([nothing, odd], axis=1)], axis=0
    )


def project_kernel(
    core_ref, offs, x_ref, bias_ref, gain_ref, w0, w1, w2, w3, w4, w5, w6, w7,
    first_ref, qkv_ref, slot_ref, out_ref, lse_ref, weights, score_scr, first_scr, qkv_scr,
    sems,
):
    _, positions = bias_ref.shape[:2]
    model = x_ref.shape[1]
    width = weights.shape[2] // 3
    heads = model // HD
    per_group = heads // 2
    groups = positions // DILATION_SMALL
    r = pl.program_id(0)

    @pl.when(r == 0)
    def _():
        pieces = (w0, w1, w2, w3, w4, w5, w6, w7)
        copies = stream_copies(pieces, slice(None), weights, sems, core_ref[0])
        start_all(copies)
        normal, _ = row_norm(x_ref[...].astype(F32))
        first_scr[...] = (normal * gain_ref[...]).astype(BF16)
        wait_all(copies)
        for hh in range(2):
            columns = slice(hh * 3 * width, (hh + 1) * 3 * width)
            qkv_scr[:, columns] = nn(first_scr[...], weights[hh]).astype(BF16)

    low, high = side_masks()
    side = iota((positions, 2 * HD), 1) < HD
    here = pl.ds(pl.multiple_of(r * positions, positions), positions)
    first_ref[...] = first_scr[here]
    qkv_ref[...] = qkv_scr[here]
    bias = bias_ref[0]
    bias = jnp.concatenate([bias, bias], axis=0)
    for pair in range(heads // 2):
        cq, ck, cv = pair_columns(pair, per_group, width)
        query, key = qkv_ref[:, cq], qkv_ref[:, ck]
        both = jnp.concatenate([query * low, query * high], axis=0)
        score_scr[pair] = nt(both, key) * SCALE + bias
        every = jnp.concatenate([query, key, qkv_ref[:, cv]], axis=1)
        for inside in range(2):
            chosen = slot_select(offs[2 * pair + inside], groups, positions)
            slots = nn(chosen, every).astype(BF16)
            starts = [2 * HD * e + HD * inside for e in range(3)]
            slot_ref[2 * pair + inside] = jnp.concatenate(
                [slots[:, start : start + HD] for start in starts], axis=1
            )
    for pair in range(heads // 2):
        value = qkv_ref[:, pair_columns(pair, per_group, width)[2]]
        score = score_scr[pair]
        peak = jnp.max(score, axis=-1, keepdims=True)
        expo = jnp.exp(score - peak)
        total = jnp.sum(expo, axis=-1, keepdims=True)
        expo = expo.astype(BF16)
        out = nn(
            jnp.concatenate([expo[:positions], expo[positions:]], axis=1),
            jnp.concatenate([value * low, value * high], axis=0),
        )
        columns = slice(2 * pair * HD, 2 * (pair + 1) * HD)
        log, scale = peak + jnp.log(total), 1.0 / total
        out_ref[:, columns] = out * jnp.where(side, scale[:positions], scale[positions:])
        lse_ref[:, columns] = jnp.where(side, log[:positions], log[positions:])


def far_masks(parity, row_start, row_count, slots):
    row = row_start + iota((row_count, slots), 0)
    column = iota((row_count, slots), 1)
    live_row = (parity == 0) | ((row & 1) == parity - 1)
    live_column = (parity == 0) | ((column & 1) == parity - 1)
    return (column <= row) & live_column, live_row


def for_blocks(count, body):
    if count == 1:
        body(0)
    else:
        lax.fori_loop(0, count, lambda b, carry: (body(b), carry)[1], 0)


def far_kernel(parity_ref, qkv_ref, out_ref, kv_scr):
    devices, _, groups, _ = qkv_ref.shape
    slots = devices * groups
    block = min(slots, 256)
    per_block = block // groups
    parity = parity_ref[pl.program_id(0)]
    kv_scr[...] = qkv_ref[:, 0].reshape(slots, 3 * HD)[:, HD:]

    def body(index):
        piece = pl.ds(index * per_block, per_block)
        query = qkv_ref[piece, 0].reshape(block, 3 * HD)[:, :HD]
        key, value = kv_scr[:, :HD], kv_scr[:, HD:]
        allowed, live = far_masks(parity, index * block, block, slots)
        score = jnp.where(allowed, nt(query, key) * SCALE, MASKED_SCORE)
        peak = jnp.max(score, axis=-1, keepdims=True)
        expo = jnp.exp(score - peak)
        total = jnp.sum(expo, axis=-1, keepdims=True)
        out = nn(expo.astype(BF16), value) / total
        log = jnp.where(live[:, :1], peak + jnp.log(total), MASKED_SCORE)
        high, middle, low = three_parts(log)
        lane = iota((block, 2 * HD), 1)
        tile = jnp.concatenate([out, out], axis=1)
        tile = jnp.where(lane == HD, high.astype(F32), tile)
        tile = jnp.where(lane == HD + 1, middle.astype(F32), tile)
        tile = jnp.where(lane == HD + 2, low.astype(F32), tile)
        out_ref[piece, 0] = tile.astype(BF16).reshape(per_block, groups, 2 * HD)

    for_blocks(slots // block, body)


def join_kernel(offs, near_ref, log_ref, far_ref, gain_ref, att_ref, heads_ref, lse_ref):
    positions, model = near_ref.shape
    heads = model // HD
    groups = far_ref.shape[1]
    side = iota((positions, 2 * HD), 1) < HD
    place = iota((positions, 2 * HD), 0) & (DILATION_SMALL - 1)

    for pair in range(heads // 2):
        even, odd = far_ref[2 * pair], far_ref[2 * pair + 1]
        far_out = nn(
            slot_spread(offs, pair, groups, positions), beside(even[:, :HD], odd[:, :HD])
        )
        even, odd = even.astype(F32), odd.astype(F32)
        shape = (groups, HD)
        logs = [
            beside(
                jnp.broadcast_to(even[:, HD + i : HD + i + 1], shape),
                jnp.broadcast_to(odd[:, HD + i : HD + i + 1], shape),
            )
            for i in range(3)
        ]
        spread = slot_spread(offs, pair, groups, positions)
        log_far = sum(nn(spread, log.astype(BF16)) for log in logs)
        slot = jnp.where(side, offs[2 * pair], offs[2 * pair + 1])
        log_far = jnp.where(place == slot, log_far, MASKED_SCORE)
        columns = slice(2 * pair * HD, 2 * (pair + 1) * HD)
        log_near = log_ref[:, columns]
        peak = jnp.maximum(log_near, log_far)
        weight_near, weight_far = jnp.exp(log_near - peak), jnp.exp(log_far - peak)
        total = weight_near + weight_far
        lse_ref[:, columns] = pltpu.roll(peak + jnp.log(total), HD, 1)
        att_ref[:, columns] = (
            near_ref[:, columns] * weight_near + far_out * weight_far
        ) / total
    normal, _ = row_norm(att_ref[...])
    heads_ref[...] = (normal * gain_ref[...]).astype(BF16)


def column_block(index, block):
    return pl.ds(pl.multiple_of(index * block, block), block)


def weight_block(weights, index, block):
    per_group = weights.shape[2] // block
    inside = lax.rem(index, per_group)
    return weights[lax.div(index, per_group), :, column_block(inside, block)]


def block_copy(source, target, index, block, sems):
    columns = column_block(index, block)
    return pltpu.make_async_copy(source.at[:, columns], target.at[:, columns], sems.at[index])


HIDDEN_BLOCKS = 6


def forward_kernel(
    core_ref, x_ref, heads_ref, seed_ref, gain_second, gain_hidden, e0, e1, e2, e3,
    hidden_ref, second_ref, resid_ref, inverse_ref, normal_ref, slope_ref,
    merge_w, expand_w, act_scr, normal_scr, slope_scr, sems, out_sems,
):
    tokens, model = x_ref.shape
    hidden_here, width = expand_w.shape[2], merge_w.shape[2]
    hidden_width = 2 * hidden_here
    block = hidden_width // HIDDEN_BLOCKS
    core = core_ref[0]
    expand = (e0, e1, e2, e3)
    merge_copies = stream_copies(expand, pl.ds(hidden_here, width), merge_w, sems.at[0], core)
    expand_copies = stream_copies(expand, pl.ds(0, hidden_here), expand_w, sems.at[1], core)
    start_all(merge_copies)
    start_all(expand_copies)
    wait_all(merge_copies)
    heads_in = heads_ref[...]
    merged = [nt(heads_in[:, hh * width : (hh + 1) * width], merge_w[hh]) for hh in range(2)]
    residual = x_ref[...].astype(F32) + (merged[0] + merged[1])
    resid_ref[...] = residual
    normal_two, _ = row_norm(residual)
    second_in = (normal_two * gain_second[...]).astype(BF16)
    second_ref[...] = second_in
    hidden_ref[:, hidden_width:] = seed_ref[:, model // 2 :]
    wait_all(expand_copies)

    def expand_step(index, totals):
        columns = column_block(index, block)
        act, slope = gelu_parts(nn(second_ref[...], weight_block(expand_w, index, block)))
        act_scr[:, columns] = act
        slope_scr[:, columns] = slope.astype(BF16)
        block_copy(slope_scr, slope_ref, index, block, out_sems.at[0]).start()
        return (
            totals[0] + jnp.sum(act, axis=-1, keepdims=True),
            totals[1] + jnp.sum(act * act, axis=-1, keepdims=True),
        )

    nothing = jnp.zeros((tokens, 1), F32)
    total_one, total_two = lax.fori_loop(0, HIDDEN_BLOCKS, expand_step, (nothing, nothing))
    center = total_one / hidden_width
    inverse = lax.rsqrt(total_two / hidden_width - center * center + NORM_EPSILON)
    inverse_ref[...] = jnp.broadcast_to(inverse, inverse_ref.shape)

    def normal_step(index, carry):
        columns = column_block(index, block)
        normal = (act_scr[:, columns] - center) * inverse
        normal_scr[:, columns] = normal.astype(BF16)
        block_copy(normal_scr, normal_ref, index, block, out_sems.at[1]).start()
        hidden_ref[:, columns] = (normal * gain_hidden[:, columns]).astype(BF16)
        return carry

    lax.fori_loop(0, HIDDEN_BLOCKS, normal_step, 0)
    for index in range(HIDDEN_BLOCKS):
        block_copy(slope_scr, slope_ref, index, block, out_sems.at[0]).wait()
        block_copy(normal_scr, normal_ref, index, block, out_sems.at[1]).wait()


def output_kernel(
    core_ref, hidden_ref, resid_ref, place_ref, r0, r1, r2, r3, block_ref, reduce_w, sems
):
    hidden_here = reduce_w.shape[2]
    copies = stream_copies((r0, r1, r2, r3), slice(None), reduce_w, sems, core_ref[0])
    start_all(copies)
    wait_all(copies)
    block_out = nt(hidden_ref[:, :hidden_here], reduce_w[0]) + nt(
        hidden_ref[:, hidden_here : 2 * hidden_here], reduce_w[1]
    )
    block_out = resid_ref[...] + block_out
    block_ref[...] = nt(block_out.astype(BF16), place_ref[...]).astype(BF16)


def backward_kernel(
    core_ref, offs, att_ref, heads_ref, lse_ref, seed_ref, second_ref, resid_ref, inverse_ref,
    gain_heads, gain_second, gain_hidden, normal_ref, slope_ref,
    e0, e1, e2, e3, r0, r1, r2, r3,
    pre_ref, left_ref, out_ref, grad_ref, stats_ref, slot_ref, grad_heads, grad_second, grad_hidden,
    merge_w, expand_w, reduce_w, normal_scr, slope_scr, grad_scr, sems, in_sems,
):
    tokens, model = att_ref.shape
    hidden_here = r0.shape[1]
    half_model = model // 2
    width = merge_w.shape[2]
    heads = model // HD
    groups = slot_ref.shape[1]
    positions = groups * DILATION_SMALL
    hidden_width = 2 * hidden_here
    block = hidden_width // HIDDEN_BLOCKS
    core = core_ref[0]
    expand = (e0, e1, e2, e3)
    merge_copies = stream_copies(expand, pl.ds(hidden_here, width), merge_w, sems.at[0], core)
    expand_copies = stream_copies(expand, pl.ds(0, hidden_here), expand_w, sems.at[1], core)
    reduce_copies = stream_copies((r0, r1, r2, r3), slice(None), reduce_w, sems.at[2], core)
    start_all(reduce_copies)
    for index in range(HIDDEN_BLOCKS):
        block_copy(normal_ref, normal_scr, index, block, in_sems.at[0]).start()
        block_copy(slope_ref, slope_scr, index, block, in_sems.at[1]).start()
    start_all(expand_copies)
    start_all(merge_copies)
    start = hidden_width + model
    pre_ref[:, hidden_width:start] = heads_ref[...]
    pre_ref[:, start : start + half_model] = second_ref[:, half_model:]
    left_ref[:, :half_model] = second_ref[:, :half_model]
    inverse = inverse_ref[:, :1]
    wait_all(reduce_copies)

    def reduce_step(index, totals):
        columns = column_block(index, block)
        grad = nn(seed_ref[...], weight_block(reduce_w, index, block))
        block_copy(normal_ref, normal_scr, index, block, in_sems.at[0]).wait()
        through = grad * normal_scr[:, columns].astype(F32)
        gain = gain_hidden[:, columns]
        grad_hidden[:, columns] = jnp.sum(through, axis=0, keepdims=True)
        grad_scr[:, columns] = grad * gain
        return (
            totals[0] + jnp.sum(grad * gain, axis=-1, keepdims=True),
            totals[1] + jnp.sum(through * gain, axis=-1, keepdims=True),
        )

    nothing = jnp.zeros((tokens, 1), F32)
    total_one, total_two = lax.fori_loop(0, HIDDEN_BLOCKS, reduce_step, (nothing, nothing))
    mean_one = total_one / hidden_width
    mean_two = total_two / hidden_width

    def pre_step(index, carry):
        columns = column_block(index, block)
        block_copy(slope_ref, slope_scr, index, block, in_sems.at[1]).wait()
        normal = normal_scr[:, columns].astype(F32)
        grad = inverse * (grad_scr[:, columns] - mean_one - normal * mean_two)
        pre_ref[:, columns] = (grad * slope_scr[:, columns].astype(F32)).astype(BF16)
        return carry

    lax.fori_loop(0, HIDDEN_BLOCKS, pre_step, 0)
    wait_all(expand_copies)
    grad_second_in = nt(pre_ref[:, :hidden_here], expand_w[0]) + nt(
        pre_ref[:, hidden_here:hidden_width], expand_w[1]
    )
    normal_two, inverse_two = row_norm(resid_ref[...])
    grad_second[...] = jnp.sum(grad_second_in * normal_two, axis=0, keepdims=True)
    resid = seed_ref[...].astype(F32) + row_norm_back(
        grad_second_in, normal_two, inverse_two, gain_second[...]
    )
    out_ref[...] = resid
    resid_low = resid.astype(BF16)
    left_ref[:, half_model:] = resid_low[:, :half_model]
    pre_ref[:, start + half_model :] = resid_low[:, half_model:]
    wait_all(merge_copies)
    grad_heads_in = jnp.concatenate([nn(resid_low, merge_w[hh]) for hh in range(2)], axis=1)
    normal_heads, inverse_heads = row_norm(att_ref[...])
    grad_heads[...] = jnp.sum(grad_heads_in * normal_heads, axis=0, keepdims=True)
    grad_att = row_norm_back(
        grad_heads_in, normal_heads, inverse_heads, gain_heads[...]
    ).astype(BF16)
    grad_ref[...] = grad_att
    grad_scr[:, :model] = grad_att.astype(F32) * att_ref[...]
    across = (iota((2 * HD, 2 * HD), 0) // HD != iota((2 * HD, 2 * HD), 1) // HD).astype(BF16)
    lane = iota((positions, 2 * HD), 1)
    side, inside_lane = lane < HD, lane & (HD - 1)

    def for_row(r, carry):
        here = pl.ds(pl.multiple_of(r * positions, positions), positions)
        for pair in range(heads // 2):
            columns = slice(2 * pair * HD, 2 * (pair + 1) * HD)
            top, middle, _ = three_parts(grad_scr[here, columns])
            dots = nn(top, across) + nn(middle, across)
            stats = jnp.zeros((positions, 2 * HD), F32)
            for index, part in enumerate(three_parts(lse_ref[here, columns]) + three_parts(dots)):
                stats = jnp.where(inside_lane == index, part.astype(F32), stats)
            stats_ref[here, columns] = stats.astype(BF16)
            grad = grad_ref[here, columns].astype(F32)
            tile = jnp.where(side, grad, stats).astype(BF16)
            chosen = slot_select(offs[2 * pair], groups, positions)
            slot_ref[r * heads + 2 * pair] = nn(chosen, tile).astype(BF16)
            tile = jnp.where(side, stats, grad).astype(BF16)
            chosen = slot_select(offs[2 * pair + 1], groups, positions)
            tile = nn(chosen, tile)
            slot_ref[r * heads + 2 * pair + 1] = jnp.concatenate(
                [tile[:, HD:], tile[:, :HD]], axis=1
            ).astype(BF16)
        return carry

    lax.fori_loop(0, tokens // positions, for_row, 0)


def far_back_kernel(parity_ref, qkv_ref, grad_ref, out_ref, kv_scr, total_scr):
    devices, _, groups, _ = qkv_ref.shape
    slots = devices * groups
    block = min(slots, 256)
    per_block = block // groups
    parity = parity_ref[pl.program_id(0)]
    kv_scr[...] = qkv_ref[:, 0].reshape(slots, 3 * HD)[:, HD:]
    total_scr[...] = jnp.zeros_like(total_scr)

    def body(index):
        piece = pl.ds(index * per_block, per_block)
        query = qkv_ref[piece, 0].reshape(block, 3 * HD)[:, :HD]
        tile = grad_ref[piece, 0].reshape(block, 2 * HD)
        key, value = kv_scr[:, :HD], kv_scr[:, HD:]
        grad = tile[:, :HD]
        stats = tile[:, HD:].astype(F32)
        log = stats[:, 0:1] + stats[:, 1:2] + stats[:, 2:3]
        dots = stats[:, 3:4] + stats[:, 4:5] + stats[:, 5:6]
        allowed, live = far_masks(parity, index * block, block, slots)
        score = jnp.where(allowed & live, nt(query, key) * SCALE - log, MASKED_SCORE)
        weight = jnp.exp(score)
        grad_score = (weight * (nt(grad, value) - dots)).astype(BF16)
        grad_query = nn(grad_score, key) * SCALE
        total_scr[:, :HD] += tn(grad_score, query) * SCALE
        total_scr[:, HD:] += tn(weight.astype(BF16), grad)
        out_ref[piece, 0, :, :HD] = grad_query.astype(BF16).reshape(per_block, groups, HD)

    for_blocks(slots // block, body)
    out_ref[:, 0, :, HD:] = total_scr[...].astype(BF16).reshape(devices, groups, 2 * HD)


def near_back_kernel(bias_ref, qkv_ref, grad_ref, stats_ref, out_ref, weight_scr, score_scr):
    positions, model = grad_ref.shape
    heads = model // HD
    per_group = heads // 2
    width = per_group * HD
    low, high = side_masks()
    inside = iota((1, 2 * HD), 1) & (HD - 1)
    less_log = jnp.where(inside < 3, -1.0 / SCALE, 0.0).astype(BF16)
    less_dots = jnp.where((inside >= 3) & (inside < 6), -1.0, 0.0).astype(BF16)

    bias = bias_ref[0]
    for pair in range(heads // 2):
        cq, ck, cv = pair_columns(pair, per_group, width)
        own = slice(2 * pair * HD, 2 * (pair + 1) * HD)
        query, key, value = qkv_ref[:, cq], qkv_ref[:, ck], qkv_ref[:, cv]
        grad, stats = grad_ref[:, own], stats_ref[:, own]
        for side, (mine, other) in enumerate(((low, high), (high, low))):
            more = stats * other
            score = nt(query * mine + more, key * mine + less_log * other)
            weight = jnp.exp(score * SCALE + bias)
            through = nt(grad * mine + more, value * mine + less_dots * other)
            weight_scr[2 * pair + side] = weight.astype(BF16)
            score_scr[2 * pair + side] = (weight * through).astype(BF16)
    for pair in range(heads // 2):
        cq, ck, cv = pair_columns(pair, per_group, width)
        own = slice(2 * pair * HD, 2 * (pair + 1) * HD)
        query, key, grad = qkv_ref[:, cq], qkv_ref[:, ck], grad_ref[:, own]
        even, odd = score_scr[2 * pair], score_scr[2 * pair + 1]
        out_ref[:, cq] = (SCALE * nn(
            jnp.concatenate([even, odd], axis=1),
            jnp.concatenate([key * low, key * high], axis=0),
        )).astype(BF16)
        out_ref[:, ck] = (SCALE * tn(
            jnp.concatenate([even, odd], axis=0),
            jnp.concatenate([query * low, query * high], axis=0),
        )).astype(BF16)
        out_ref[:, cv] = (tn(
            jnp.concatenate([weight_scr[2 * pair], weight_scr[2 * pair + 1]], axis=0),
            jnp.concatenate([grad * low, grad * high], axis=0),
        )).astype(BF16)


def join_back_kernel(offs, near_ref, far_ref, first_ref, out_ref):
    positions, model = first_ref.shape
    heads = model // HD
    per_group = heads // 2
    width = per_group * HD
    groups = far_ref.shape[1]
    out_ref[:, 3 * model :] = first_ref[:, model // 2 :]

    for pair in range(heads // 2):
        even, odd = far_ref[2 * pair], far_ref[2 * pair + 1]
        spread = slot_spread(offs, pair, groups, positions)
        for e, columns in enumerate(pair_columns(pair, per_group, width)):
            part = slice(e * HD, (e + 1) * HD)
            far = nn(spread, beside(even[:, part], odd[:, part]))
            out_ref[:, columns] = (near_ref[:, columns].astype(F32) + far).astype(BF16)


def weight_grad_kernel(
    change, core_ref, left, right_0, right_1, left_got, right_0_got, right_1_got,
    *refs,
):
    kept_ref, sent_ref, left_scr = refs[-3:]
    block = kept_ref.shape[1]
    if len(refs) > 3:
        sent_ref[2 * block :] = refs[0][...]
    step = pl.program_id(0)

    @pl.when((step == 0) | (step == change))
    def _():
        left_scr[0] = left[...].T
        left_scr[1] = left_got[...].T

    product = [
        nn(left_scr[0], right[...]) + nn(left_scr[1], got[...])
        for right, got in ((right_0, right_0_got), (right_1, right_1_got))
    ]
    kept_ref[0] = product[0][:block]
    sent_ref[block : 2 * block] = product[1][block:].astype(BF16)
    low, high = product[0][block:], product[1][:block]

    @pl.when(core_ref[0] == 0)
    def _():
        kept_ref[1] = high
        sent_ref[:block] = low.astype(BF16)

    @pl.when(core_ref[0] != 0)
    def _():
        kept_ref[1] = low
        sent_ref[:block] = high.astype(BF16)


def input_grad_kernel(
    core_ref, x_ref, pack_ref, resid_ref, gain_ref, second_ref, place_ref, w0, w1, w2, w3, w4, w5, w6, w7,
    grad_ref, gain_grad, weights, sems,
):
    span = weights.shape[2]
    copies = stream_copies((w0, w1, w2, w3, w4, w5, w6, w7), slice(None), weights, sems, core_ref[0])
    start_all(copies)
    normal, inverse = row_norm(x_ref[...].astype(F32))
    wait_all(copies)
    grad_first = nt(pack_ref[:, :span], weights[0]) + nt(pack_ref[:, span : 2 * span], weights[1])
    first = jnp.sum(grad_first * normal, axis=0, keepdims=True)
    parts = three_parts(jnp.concatenate([first, second_ref[...]] + [jnp.zeros_like(first)] * 6))
    gain_grad[...] = sum(nt(part, place_ref[...]) for part in parts)
    grad = resid_ref[...] + row_norm_back(grad_first, normal, inverse, gain_ref[...])
    grad_ref[...] = nt(grad.astype(BF16), place_ref[...]).astype(BF16)


def whole(*shape):
    return pl.BlockSpec(shape, lambda *_: tuple(0 for _ in shape))


def sds(shape, dtype):
    return jax.ShapeDtypeStruct(shape, dtype)


def call(
    kernel, grid, in_specs, out_specs, out_shape, scratch=(), earlier=(), cost=5
):
    def body(*refs):
        kernel(*refs[len(earlier) :])

    return partial(
        pl.pallas_call(
            body,
            grid=grid,
            in_specs=[ANY] * len(earlier) + in_specs,
            out_specs=out_specs,
            out_shape=out_shape,
            scratch_shapes=list(scratch),
            compiler_params=pltpu.CompilerParams(
                dimension_semantics=("arbitrary",) * len(grid), vmem_limit_bytes=VMEM_LIMIT
            ),
            cost_estimate=pl.CostEstimate(
                flops=cost * 1_150_000_000, bytes_accessed=0, transcendentals=0
            ),
        ),
        *earlier,
    )


def per_device(
    inputs,
    attend_weight,
    merge_weight,
    expand_weight,
    reduce_weight,
    gain_first,
    gain_heads,
    gain_second,
    gain_hidden,
    cotangent,
    lengths,
    local_span,
    dilation,
):
    seq_size, head_size = lax.axis_size("seq"), lax.axis_size("head")
    row_count, positions, model = inputs.shape
    rows = row_count // head_size
    tokens = rows * positions
    shard_rows, width = attend_weight.shape[1:]
    heads = width * head_size // HD
    group_heads = heads // head_size
    hidden_here = expand_weight.shape[1]
    hidden_width = hidden_here * head_size
    quarter = model // 4
    groups = positions // DILATION_SMALL
    pairs = rows * heads
    owned = -(-pairs // seq_size)
    padded = owned * seq_size
    seq_index, head_index = lax.axis_index("seq"), lax.axis_index("head")
    core = seq_index & 1
    core_ref = core.reshape(1)

    attend_shard = gather_core(jnp.concatenate(list(attend_weight), axis=1))
    attend_far = gather_far(attend_shard)
    attend_got = exchange_near(attend_far, 0)
    attend_more = exchange_near(attend_far, 1)
    attend_last = exchange_near(attend_got, 1)
    attend_all = (attend_far, attend_got, attend_more, attend_last)
    attend_all = attend_all + tuple(exchange(piece, 1, 0) for piece in attend_all)
    other_shard = jnp.concatenate([expand_weight, merge_weight.T, reduce_weight.T], axis=1)
    other_shard = gate(gather_core(after(other_shard, attend_shard)), attend_far)
    both_gains = jnp.concatenate([gain_heads, gain_hidden])
    partner_gains = exchange(both_gains.reshape(-1, 128), 0, 1).reshape(-1)
    gain_heads_all = jnp.concatenate([gain_heads, partner_gains[:width]])[None]
    gain_hidden_all = jnp.concatenate([gain_hidden, partner_gains[width:]])[None]

    half_rows = shard_rows // 2
    part, near, far, beside, inside = jnp.meshgrid(
        *[jnp.arange(n) for n in (2, 2, seq_size // 4, 2, half_rows)], indexing="ij"
    )
    shard_of = seq_index ^ (4 * far + 2 * near + (beside ^ part))
    feature_of = (shard_of * shard_rows + (core ^ part) * half_rows + inside).reshape(-1)
    place = (jnp.arange(model)[:, None] == feature_of[None, :]).astype(BF16)

    def to_own_order(gain):
        return jnp.dot(
            gain[None], place.astype(F32), precision=lax.Precision.HIGHEST
        )

    gain_one, gain_two = to_own_order(gain_first), to_own_order(gain_second)
    row_start = head_index * rows

    def own_rows(tensor):
        return lax.dynamic_slice_in_dim(tensor, row_start, rows, axis=0)

    def in_own_order(tensor):
        return nn(tensor.reshape(tokens, model), place).astype(BF16)

    x_own = in_own_order(own_rows(inputs))
    places = jnp.arange(positions)
    in_length = (seq_index * positions + places)[None, :] < own_rows(lengths)[:, None]
    seed = in_own_order(
        jnp.where(in_length[..., None], own_rows(cotangent), jnp.zeros((), BF16))
    )
    span_block = places[None, :] // own_rows(local_span)[:, None]
    within = (span_block[:, :, None] == span_block[:, None, :]) & (
        places[None, :] <= places[:, None]
    )
    bias = jnp.where(within, 0.0, MASKED_SCORE).astype(F32)

    local_head = jnp.arange(heads)
    head_ids = (head_index ^ (local_head // group_heads)) * group_heads + local_head % group_heads
    offsets = (head_ids % DILATION_SMALL).astype(jnp.int32)
    pair_ids = jnp.minimum(seq_index * owned + jnp.arange(owned), pairs - 1)
    pair_rate = own_rows(dilation)[pair_ids // heads]
    pair_head = head_ids[pair_ids % heads]
    parity = jnp.where(
        pair_rate == DILATION_SMALL, 0, 1 + (pair_head % pair_rate) // DILATION_SMALL
    ).astype(jnp.int32)

    model_spec, model_shape = whole(tokens, model), (tokens, model)
    attend_scratch = pltpu.VMEM((2, model, 3 * width), BF16)

    def by_row(size):
        return pl.BlockSpec((positions, size), lambda r: (r, 0))

    def of_row(size):
        return pl.BlockSpec((heads, groups, size), lambda r: (r, 0, 0))

    model_row, qkv_row = by_row(model), by_row(3 * model)
    bias_row = pl.BlockSpec((1, positions, positions), lambda r: (r, 0, 0))
    first_in, qkv, slots, near_out, log_near = call(
        project_kernel,
        (rows,),
        [SMEM, SMEM, model_spec, bias_row, whole(1, model)] + [ANY] * 8,
        [model_row, qkv_row, of_row(3 * HD), model_row, model_row],
        [
            sds(model_shape, BF16),
            sds((tokens, 3 * model), BF16),
            sds((padded, groups, 3 * HD), BF16),
            sds(model_shape, F32),
            sds(model_shape, F32),
        ],
        [
            attend_scratch,
            pltpu.VMEM((heads // 2, 2 * positions, positions), F32),
            pltpu.VMEM((tokens, model), BF16),
            pltpu.VMEM((tokens, 3 * model), BF16),
            pltpu.SemaphoreType.DMA((8,)),
        ],
        cost=1,
    )(core_ref, offsets, x_own, bias, gain_one, *attend_all)
    other_far = gather_far(other_shard, (first_in,))
    other_got = exchange_near(other_far, 0)

    def to_owners(value):
        value = value.reshape(seq_size, owned, groups, value.shape[-1])
        return lax.all_to_all(value, "seq", 0, 0, tiled=True)

    def from_owners(value):
        value = lax.all_to_all(value, "seq", 0, 0, tiled=True)
        return value.reshape(padded, groups, value.shape[-1])

    def by_pair(size):
        return pl.BlockSpec((seq_size, 1, groups, size), lambda i: (0, i, 0, 0))

    def owned_shape(size):
        return sds((seq_size, owned, groups, size), BF16)

    slot_count = seq_size * groups
    kv_scratch = pltpu.VMEM((slot_count, 2 * HD), BF16)
    far_qkv = to_owners(slots)
    far_out = call(
        far_kernel,
        (owned,),
        [SMEM, by_pair(3 * HD)],
        by_pair(2 * HD),
        owned_shape(2 * HD),
        [kv_scratch],
        cost=4,
    )(parity, far_qkv)
    far_here = from_owners(far_out)
    expand_held, reduce_held = join(
        [other_far, other_got], (far_out,), (hidden_here + width, hidden_here)
    )
    expand_more = exchange_near(expand_held, 1)
    reduce_more = exchange_near(reduce_held, 1)

    attended, heads_in, log_all = call(
        join_kernel,
        (rows,),
        [SMEM, model_row, model_row, of_row(2 * HD), whole(1, model)],
        [model_row, model_row, model_row],
        [sds(model_shape, F32), sds(model_shape, BF16), sds(model_shape, F32)],
        cost=5,
    )(offsets, near_out, log_near, far_here, gain_heads_all)
    expand_more = gate(expand_more, heads_in)
    expand_all = (
        expand_held, expand_more, exchange(expand_held, 1, 0), exchange(expand_more, 1, 0)
    )
    hidden_scratch = pltpu.VMEM((tokens, hidden_width), F32)
    hidden_low = pltpu.VMEM((tokens, hidden_width), BF16)
    hidden_pack = (tokens, hidden_width + model // 2)
    pre_pack = (tokens, hidden_width + 2 * model)
    merge_scratch = pltpu.VMEM((2, model, width), BF16)
    weight_scratch = pltpu.VMEM((2, model, hidden_here), BF16)
    hidden_in, second_in, residual, inverse_hidden, normal_hidden, slope = call(
        forward_kernel,
        (),
        [SMEM] + [model_spec] * 3 + [whole(1, model), whole(1, hidden_width)] + [ANY] * 4,
        [whole(*hidden_pack), model_spec, model_spec, whole(tokens, 128), ANY, ANY],
        [
            sds(hidden_pack, BF16), sds(model_shape, BF16), sds(model_shape, F32),
            sds((tokens, 128), F32), sds((tokens, hidden_width), BF16),
            sds((tokens, hidden_width), BF16),
        ],
        [
            merge_scratch, weight_scratch, hidden_scratch, hidden_low, hidden_low,
            pltpu.SemaphoreType.DMA((2, 8)), pltpu.SemaphoreType.DMA((2, HIDDEN_BLOCKS)),
        ],
        cost=16,
    )(core_ref, x_own, heads_in, seed, gain_two, gain_hidden_all, *expand_all)
    reduce_more = gate(reduce_more, hidden_in)
    reduce_all = (
        reduce_held, reduce_more, exchange(reduce_held, 1, 0), exchange(reduce_more, 1, 0)
    )
    block_mine = call(
        output_kernel,
        (),
        [SMEM, whole(*hidden_pack), model_spec, whole(model, model)] + [ANY] * 4,
        model_spec,
        sds(model_shape, BF16),
        [weight_scratch, pltpu.SemaphoreType.DMA((8,))],
        cost=40,
    )(core_ref, hidden_in, residual, place, *reduce_all)

    def weight_grad(
        size, left, left_at, right, right_at, left_got_at, earlier=(), change=0, extra=None
    ):
        got = exchange(right, 1, 0)

        def spec(at):
            return pl.BlockSpec((tokens, width), lambda j: (0, at(j)))

        def rights():
            return [spec(lambda j, x=x: right_at(x, j)) for x in range(2)]

        sent_rows = 2 * quarter
        extras = []
        if extra is not None:
            sent_rows += GAIN_ROWS
            extras = [extra]
        return call(
            partial(weight_grad_kernel, change),
            (size // width,),
            [SMEM, spec(left_at)] + rights() + [spec(left_got_at)] + rights()
            + [pl.BlockSpec((GAIN_ROWS, width), lambda j: (0, j))] * len(extras),
            [
                pl.BlockSpec((2, quarter, width), lambda j: (0, 0, j)),
                pl.BlockSpec((sent_rows, width), lambda j: (0, j)),
            ],
            [sds((2, quarter, size), F32), sds((sent_rows, size), BF16)],
            [pltpu.VMEM((2, model // 2, tokens), BF16)],
            earlier=earlier,
            cost=7,
        )(core_ref, left, right, right, got, got, got, *extras)

    per_half = hidden_here // width
    hidden_blocks = hidden_width // width

    def both_rows(mine, earlier=None):
        mine = mine.reshape(rows, positions, model)
        other = exchange(mine, 0, 1)
        if earlier is not None:
            other = after(other, earlier)
        first = jnp.where(head_index == 0, mine, other)
        second = jnp.where(head_index == 0, other, mine)
        return jnp.concatenate([first, second])

    reduce_kept, reduce_sent = weight_grad(
        hidden_here, seed, lambda j: 0, hidden_in, lambda x, j: x * per_half + j,
        lambda j: hidden_blocks, earlier=(block_mine,),
    )
    (
        grad_pre, lefts, grad_resid, grad_att, stats, grad_slots, grad_heads, grad_second,
        grad_hidden,
    ) = call(
        backward_kernel,
        (),
        [SMEM, SMEM] + [model_spec] * 6
        + [whole(tokens, 128), whole(1, model), whole(1, model), whole(1, hidden_width)]
        + [ANY] * 10,
        [
            whole(*pre_pack), model_spec, model_spec, model_spec, model_spec,
            whole(padded, groups, 2 * HD), whole(1, model), whole(1, model),
            whole(1, hidden_width),
        ],
        [
            sds(pre_pack, BF16), sds(model_shape, BF16), sds(model_shape, F32),
            sds(model_shape, BF16), sds(model_shape, BF16),
            sds((padded, groups, 2 * HD), BF16), sds((1, model), F32), sds((1, model), F32),
            sds((1, hidden_width), F32),
        ],
        [
            merge_scratch, weight_scratch, weight_scratch, hidden_low, hidden_low, hidden_scratch,
            pltpu.SemaphoreType.DMA((3, 8)), pltpu.SemaphoreType.DMA((2, HIDDEN_BLOCKS)),
        ],
        earlier=(reduce_sent,),
        cost=22,
    )(
        core_ref, offsets, attended, heads_in, log_all, seed, second_in, residual,
        inverse_hidden, gain_heads_all, gain_two, gain_hidden_all, normal_hidden, slope,
        *expand_all, *reduce_all,
    )
    far_grads = to_owners(grad_slots)
    reduce_kept, reduce_sent, _ = scatter_first(reduce_kept, reduce_sent)
    near_grad = call(
        near_back_kernel,
        (rows,),
        [bias_row, qkv_row, model_row, model_row],
        qkv_row,
        sds((tokens, 3 * model), BF16),
        [pltpu.VMEM((heads, positions, positions), BF16)] * 2,
        earlier=(reduce_sent,),
        cost=60,
    )(bias, qkv, grad_att, stats)
    block_out = both_rows(block_mine, near_grad)
    expand_kept, expand_sent = weight_grad(
        hidden_here + width, lefts, lambda j: jnp.where(j < per_half, 0, 1), grad_pre,
        lambda x, j: jnp.where(j < per_half, x * per_half + j, hidden_blocks + x),
        lambda j: hidden_blocks + 2 + jnp.where(j < per_half, 0, 1),
        earlier=(near_grad,), change=per_half,
    )
    far_back = call(
        far_back_kernel,
        (owned,),
        [SMEM, by_pair(3 * HD), by_pair(2 * HD)],
        by_pair(3 * HD),
        owned_shape(3 * HD),
        [kv_scratch, pltpu.VMEM((slot_count, 2 * HD), F32)],
        earlier=(expand_sent,),
        cost=1,
    )(parity, far_qkv, far_grads)
    back_here = from_owners(far_back)
    expand_kept, expand_sent, _ = scatter_first(expand_kept, expand_sent)
    reduce_kept, reduce_sent, _ = scatter_second(reduce_kept, reduce_sent)
    grad_pack_shape = (tokens, 3 * model + model // 2)
    grad_pack = call(
        join_back_kernel,
        (rows,),
        [SMEM, qkv_row, of_row(3 * HD), model_row],
        by_row(grad_pack_shape[1]),
        sds(grad_pack_shape, BF16),
        earlier=(*reduce_sent, block_out, expand_sent),
        cost=1,
    )(offsets, near_grad, back_here, first_in)
    grad_mine, grad_shared = call(
        input_grad_kernel,
        (),
        [
            SMEM, model_spec, whole(*grad_pack_shape), model_spec, whole(1, model),
            whole(1, model), whole(model, model),
        ]
        + [ANY] * 8,
        [model_spec, whole(8, model)],
        [sds(model_shape, BF16), sds((8, model), F32)],
        [attend_scratch, pltpu.SemaphoreType.DMA((8,))],
        cost=40,
    )(core_ref, x_own, grad_pack, grad_resid, gain_one, grad_second, place, *attend_all)

    def by_head(grad):
        size = grad.shape[1] // 2
        return jnp.where(head_index == 0, grad[0], jnp.roll(grad[0], size))

    gains = jnp.concatenate(
        [
            grad_shared[0], grad_shared[1], by_head(grad_heads), by_head(grad_hidden),
        ]
    )
    gain_rows = -(-gains.shape[0] // (3 * width))
    gains = jnp.pad(gains, (0, gain_rows * 3 * width - gains.shape[0])).reshape(gain_rows, -1)
    gain_sent = to_rows(gains)
    attend_kept, attend_sent = weight_grad(
        3 * width, first_in, lambda j: 0, grad_pack, lambda x, j: 3 * x + j, lambda j: 6,
        earlier=(grad_mine,), extra=gain_sent,
    )
    attend_kept, attend_sent, attend_near = scatter_first(attend_kept, attend_sent)
    gains = from_rows(gain_sent, gain_rows) + from_rows(attend_near[2 * quarter :], gain_rows)
    gain_sent = to_rows(gains)
    expand_kept, expand_sent, _ = scatter_second(expand_kept, expand_sent)
    attend_kept, attend_sent, attend_got = scatter_second(
        attend_kept, jnp.concatenate([attend_sent, gain_sent])
    )
    gains = from_rows(gain_sent, gain_rows) + from_rows(attend_got[quarter:], gain_rows)
    stages = far_stages(seq_size)
    for stage in reversed(range(len(stages))):
        unit, radix = stages[stage]
        gain_sent = to_rows(gains)
        everyone = [from_rows(gain_sent, gain_rows)]
        rows_sent = attend_sent[0].shape[0]
        for i, piece in enumerate(attend_sent):
            got = exchange(jnp.concatenate([piece, gain_sent]), unit * (i + 1), 0)
            attend_kept = attend_kept + got[:rows_sent].astype(F32)
            everyone.append(from_rows(got[rows_sent:], gain_rows))
        while len(everyone) > 1:
            everyone = [one + two for one, two in zip(everyone[::2], everyone[1::2])]
        gains = everyone[0]
        if stage:
            held = attend_kept.reshape(stages[stage - 1][1], -1, 3 * width)
            attend_kept, attend_sent = held[0], [piece.astype(BF16) for piece in held[1:]]
    attend_last = jnp.concatenate([attend_kept[half_rows:], gains])
    attend_last = exchange(attend_last, 1, 0)
    gains = (gains + attend_last[half_rows:]).reshape(-1)
    attend_last = attend_last[:half_rows]
    attend_kept = attend_kept[:half_rows]
    grad_attend = jnp.concatenate(
        [
            jnp.where(core == 0, attend_kept, attend_last),
            jnp.where(core == 0, attend_last, attend_kept),
        ]
    )
    grad_reduce = scatter_core(scatter_far(after(reduce_kept, attend_near), reduce_sent))
    grad_expand = scatter_core(scatter_far(after(expand_kept, attend_near), expand_sent))
    grad_inputs = both_rows(grad_mine, attend_near)

    def own_half(start, size):
        return lax.dynamic_slice_in_dim(gains, start + head_index * size, size)

    return (
        block_out,
        grad_inputs,
        jnp.stack([grad_attend[:, e * width : (e + 1) * width] for e in range(3)]),
        grad_expand[:, hidden_here:].T,
        grad_expand[:, :hidden_here],
        grad_reduce.T,
        gains[:model],
        own_half(2 * model, width),
        gains[model : 2 * model],
        own_half(3 * model, hidden_here),
    )


def solution(mesh):
    placed = (
        P(None, "seq", None),
        P(None, "seq", "head"),
        P("head", "seq"),
        P("seq", "head"),
        P("head", "seq"),
        P(),
        P("head"),
        P(),
        P("head"),
        P(None, "seq", None),
        P(),
        P(),
        P(),
    )
    return jax.shard_map(
        per_device,
        mesh=mesh,
        in_specs=placed,
        out_specs=(
            P(None, "seq", None),
            P(None, "seq", None),
            P(None, "seq", "head"),
            P("head", "seq"),
            P("seq", "head"),
            P("head", "seq"),
            P(),
            P("head"),
            P(),
            P("head"),
        ),
        check_vma=False,
    )
```

time: 396 us -> 345 us (0.87)
  other arithmetic: 47.8 us -> 28.6 us
  waiting for transfers between devices: 108 us -> 90.5 us
  starting transfers between devices: 94.9 us -> 79 us
  local copies, waits for them, and re-layouts: 36.1 us -> 21.5 us
  Pallas kernels: 103 us -> 115 us
    ppermute x56 -> x46, waiting for transfers between devices: 93.8 us -> 67.8 us  [permute(): return lax.ppermute(value, ('seq', 'head'), pairs)]
    ppermute x56 -> x46, starting transfers between devices: 75 us -> 49.7 us  [permute(): return lax.ppermute(value, ('seq', 'head'), pairs)]
    another operation x26 -> x5, other arithmetic: 25.2 us -> 4.36 us  [the longest x12 18.6 us: gather_chunk(): own = jnp.stack([part_a, part_b])]
    pallas_call x7 -> x16, Pallas kernels: 95.5 us -> 107 us  [the longest x3 22.4 us: weight_grad(): call(partial(weight_grad_kernel, change), (size // width,), [SMEM, spec(l...]
    all_to_all x2, waiting for transfers between devices: 3.52 us -> 12.5 us  [from_owners(): value = lax.all_to_all(value, 'seq', 0, 0, tiled=True)]
    all_to_all x2, starting transfers between devices: 10.5 us -> 17.5 us  [to_owners(): return lax.all_to_all(value, 'seq', 0, 0, tiled=True)]
    slice x8 -> x12, local copies, waits for them, and re-layouts: 12.9 us -> 6.14 us  [the longest x2 1.64 us: after(): zero = earlier[(0,) * earlier.ndim].astype(F32) * 0.0]
    unnamed x82 -> x90, local copies, waits for them, and re-layouts: 5.26 us -> 10.3 us
  transfers between devices with their start and end apart: 60 -> 50, of which waited for: 22 -> 16; matrix products, arithmetic and copies ran while one was open for 20% -> 12% of each run, Pallas kernels for 16% -> 32%
where the time goes in v2:
time: 345 us; the launch traced here: 343 us
  Pallas kernels  115 us (33%)
  waiting for transfers between devices  90.5 us (26%)
  starting transfers between devices  79 us (23%)
  other arithmetic  28.6 us (8%)
  local copies, waits for them, and re-layouts  21.5 us (6%)
  matrix products  5.77 us (2%)
    ppermute x46, waiting for transfers between devices, permute(): return lax.ppermute(value, ('seq', 'head'), pairs)  67.8 us
    ppermute x46, starting transfers between devices, permute(): return lax.ppermute(value, ('seq', 'head'), pairs)  49.7 us
    pallas_call x3, Pallas kernels, weight_grad(): call(partial(weight_grad_kernel, change), (size // width,), [SMEM, spec(l...  22.4 us
    pallas_call x1, Pallas kernels, per_device(): call(backward_kernel, (), [SMEM, SMEM] + [model_spec] * 6 + [whole(tokens...  21.5 us
    all_to_all x2, starting transfers between devices, to_owners(): return lax.all_to_all(value, 'seq', 0, 0, tiled=True)  17.5 us
    pallas_call x1, Pallas kernels, per_device(): call(forward_kernel, (), [SMEM] + [model_spec] * 3 + [whole(1, model), wh...  15.8 us
    all_to_all x2, waiting for transfers between devices, from_owners(): value = lax.all_to_all(value, 'seq', 0, 0, tiled=True)  12.5 us
    all_to_all x2, starting transfers between devices, from_owners(): value = lax.all_to_all(value, 'seq', 0, 0, tiled=True)  11.8 us
  transfers between devices with their start and end apart: 50, of which 16 were waited for; matrix products, arithmetic and copies ran while one was open for 12% of the time, Pallas kernels for 32%

profile of v2, /device:TPU:0, one launch (start us, length us, event | category | flops | bytes accessed | tf_op | source)
XLA Modules:
  0.0 342.9 jit_solution(9286627329602369929)
XLA Ops:
  2.7 1.7 maximum_add_fusion
  6.9 3.1 collective-permute-start.1
  10.0 2.6 collective-permute-start.2
  13.2 8.3 %collective-permute-done.2 = bf16[48,1152]{1,0:T(8,128)(2,1)S(1)} collective-permute-done((bf16[48,1152]{1,0:T(8,128)(2,1)S(1)}, bf16[48,1152]{1,0:T(8,128)(2,1)S(1)}, u32[]{:S(2)}, u32[]{:S(2)}) %collective-permute-start.2) | collective-permute-done | bytes 110624 | tf_op jit(solution)/shard_map/ppermute | solution.py:80
  26.4 8.2 %collective-permute-done.4.refs_6_.refs_8_ = bf16[192,1152]{1,0:T(8,128)(2,1)S(1)} collective-permute-done((bf16[192,1152]{1,0:T(8,128)(2,1)S(1)}, bf16[192,1152]{1,0:T(8,128)(2,1)S(1)}, u32[]{:S(2)}, u32[]{:S(2)}) %collective-permute-start.4) | collective-permute-done | bytes 442400 | tf_op jit(solution)/shard_map/ppermute | solution.py:80
  38.2 4.8 %collective-permute-done.6.refs_8_.refs_10_ = bf16[192,1152]{1,0:T(8,128)(2,1)S(1)} collective-permute-done((bf16[192,1152]{1,0:T(8,128)(2,1)S(1)}, bf16[192,1152]{1,0:T(8,128)(2,1)S(1)}, u32[]{:S(2)}, u32[]{:S(2)}) %collective-permute-start.6) | collective-permute-done | bytes 442400 | tf_op jit(solution)/shard_map/ppermute | solution.py:80
  43.0 1.8 pad_maximum_fusion.3.refs_1_
  46.1 1.8 collective-permute-start.14
  50.6 8.7 %shard_map.204 = (bf16[384,768]{1,0:T(8,128)(2,1)}, bf16[384,2304]{1,0:T(8,128)(2,1)}, bf16[48,16,192]{2,1,0:T(8,128)(2,1)}, f32[384,768]{1,0:T(8,128)}, f32[384,768]{1,0:T(8,128)}) custom-call(s32[1]{0:T(128)} %bitcast.refs_0_.refs_1_, s32[12]{0:T(128)} %and_select_fusion.5.refs_1_.refs_0_.refs_2_.refs_5_, bf16[384,768]{1,0:T(8,128)(2,1)} %fusion.7.refs_2_.refs_1_, ...), custom_call_target="tpu_custom_call" | custom-call | flops 1150000000 | tf_op jit(solution)/shard_map/pallas_call | solution.py:903
  59.3 2.4 collective-permute-done.13.refs_2_
  61.7 10.4 %collective-permute-done.14.refs_3_ = bf16[48,3456]{1,0:T(8,128)(2,1)S(1)} collective-permute-done((bf16[48,3456]{1,0:T(8,128)(2,1)}, bf16[48,3456]{1,0:T(8,128)(2,1)S(1)}, u32[]{:S(2)}, u32[]{:S(2)}) %collective-permute-start.14) | collective-permute-done | bytes 331808 | tf_op jit(solution)/shard_map/ppermute | solution.py:80
  72.9 2.4 shard_map.208.refs_1_
  76.9 10.0 %all-to-all-start = ((bf16[16,3,16,192]{3,2,1,0:T(8,128)(2,1)}), bf16[16,3,16,192]{3,2,1,0:T(8,128)(2,1)S(1)}, u32[]{:S(2)}, u32[]{:S(2)}) async-start(bf16[16,3,16,192]{3,2,1,0:T(8,128)(2,1)} %bitcast.7), calls=%async_computation | async-start | bytes 786432 | tf_op jit(solution)/shard_map/all_to_all | solution.py:929
  88.9 10.2 %all-to-all-done.refs_1_.refs_2_ = bf16[16,3,16,192]{3,2,1,0:T(8,128)(2,1)S(1)} async-done(((bf16[16,3,16,192]{3,2,1,0:T(8,128)(2,1)}), bf16[16,3,16,192]{3,2,1,0:T(8,128)(2,1)S(1)}, u32[]{:S(2)}, u32[]{:S(2)}) %all-to-all-start) | async-done | bytes 294944 | tf_op jit(solution)/shard_map/all_to_all | solution.py:929
  99.9 3.7 %shard_map.205.refs_0_ = bf16[16,3,16,128]{3,2,1,0:T(8,128)(2,1)} custom-call(s32[3]{0:T(128)} %compare_select_fusion.5.refs_0_.refs_1_, bf16[16,3,16,192]{3,2,1,0:T(8,128)(2,1)} %copy-done.23), custom_call_target="tpu_custom_call" | custom-call | flops 4600000000 | tf_op jit(solution)/shard_map/pallas_call | solution.py:944
  103.6 3.4 shard_map.209
  107.2 7.1 %all-to-all-start.1 = ((bf16[16,3,16,128]{3,2,1,0:T(8,128)(2,1)}), bf16[16,3,16,128]{3,2,1,0:T(8,128)(2,1)S(1)}, u32[]{:S(2)}, u32[]{:S(2)}) async-start(bf16[16,3,16,128]{3,2,1,0:T(8,128)(2,1)} %shard_map.205.refs_0_), calls=%async_computation.1 | async-start | bytes 393216 | tf_op jit(solution)/shard_map/all_to_all | solution.py:932
  115.6 2.7 collective-permute-done.11
  118.9 9.7 %all-to-all-done.1 = bf16[16,3,16,128]{3,2,1,0:T(8,128)(2,1)S(1)} async-done(((bf16[16,3,16,128]{3,2,1,0:T(8,128)(2,1)}), bf16[16,3,16,128]{3,2,1,0:T(8,128)(2,1)S(1)}, u32[]{:S(2)}, u32[]{:S(2)}) %all-to-all-start.1) | async-done | bytes 196640 | tf_op jit(solution)/shard_map/all_to_all | solution.py:932
  129.3 4.9 %shard_map.206 = (f32[384,768]{1,0:T(8,128)}, bf16[384,768]{1,0:T(8,128)(2,1)}, f32[384,768]{1,0:T(8,128)}) custom-call(s32[12]{0:T(128)} %and_select_fusion.5.refs_1_.refs_0_.refs_2_.refs_5_, f32[384,768]{1,0:T(8,128)} %get-tuple-element.43.refs_1_, f32[384,768]{1,0:T(8,128)} %get-tuple-element.44.refs_2_, bf16[48,16,128]{2,1,0:T(8,128)(2,1)} %bitcast.81, ...), custom_call_target="tpu_custom_call" | custom-call | flops 5750000128 | tf_op jit(solution)/shard_map/pallas_call | solution.py:960
  141.5 15.8 %shard_map.211 = (bf16[384,3456]{1,0:T(8,128)(2,1)}, bf16[384,768]{1,0:T(8,128)(2,1)}, f32[384,768]{1,0:T(8,128)}, f32[384,128]{1,0:T(8,128)}, bf16[384,3072]{1,0:T(8,128)(2,1)}, /*index=5*/bf16[384,3072]{1,0:T(8,128)(2,1)}) custom-call(s32[1]{0:T(128)} %bitcast.refs_0_.refs_1_, bf16[384,768]{1,0:T(8,128)(2,1)} %fusion.7.refs_2_.refs_1_, ...), custom_call_target="tpu_custom_call" | custom-call | flops 18400000000 | tf_op jit(solution)/shard_map/pallas_call | solution.py:978
  161.4 8.8 %shard_map.213.refs_0_ = bf16[384,768]{1,0:T(8,128)(2,1)} custom-call(s32[1]{0:T(128)} %bitcast.refs_0_.refs_1_, bf16[384,3456]{1,0:T(8,128)(2,1)} %get-tuple-element.49.refs_0_.refs_1_.refs_3_.refs_4_, f32[384,768]{1,0:T(8,128)} %get-tuple-element.50.refs_2_.refs_8_, bf16[768,768]{1,0:T(8,128)(2,1)} %fusion.refs_3_.refs_6_, ...), custom_call_target="tpu_custom_call" | custom-call | flops 46000001024 | tf_op jit(solution)/shard_map/pallas_call | solution.py:998
  173.4 7.2 %shard_map.214 = (f32[2,192,1536]{2,1,0:T(8,128)}, bf16[384,1536]{1,0:T(8,128)(2,1)}) custom-call(bf16[384,768]{1,0:T(8,128)(2,1)} %shard_map.213.refs_0_, s32[1]{0:T(128)} %bitcast.refs_0_.refs_1_, bf16[384,768]{1,0:T(8,128)(2,1)} %fusion.8.refs_3_.refs_2_.refs_6_, bf16[384,3456]{1,0:T(8,128)(2,1)} %get-tuple-element.49.refs_0_.refs_1_.refs_3_.refs_4_, ...), custom_call_target="tpu_custom_call" | custom-call | flops 8049999872 | tf_op jit(solution)/shard_map/pallas_call | solution.py:1024
  181.1 21.5 %shard_map.215 = (bf16[384,4608]{1,0:T(8,128)(2,1)}, bf16[384,768]{1,0:T(8,128)(2,1)}, f32[384,768]{1,0:T(8,128)}, bf16[384,768]{1,0:T(8,128)(2,1)}, bf16[384,76...) custom-call(bf16[384,1536]{1,0:T(8,128)(2,1)} %get-tuple-element.53., ...), custom_call_target="tpu_custom_call" | custom-call | flops 25300000768 | tf_op jit(solution)/shard_map/pallas_call | solution.py:1058
  202.7 7.5 %all-to-all-start.2 = ((bf16[16,3,16,128]{3,2,1,0:T(8,128)(2,1)}), bf16[16,3,16,128]{3,2,1,0:T(8,128)(2,1)}, u32[]{:S(2)}, u32[]{:S(2)}) async-start(bf16[16,3,16,128]{3,2,1,0:T(8,128)(2,1)} %bitcast.80), calls=%async_computation.2 | async-start | bytes 393216 | tf_op jit(solution)/shard_map/all_to_all | solution.py:929
  214.2 5.6 %shard_map.216.refs_0_.refs_6_ = bf16[384,2304]{1,0:T(8,128)(2,1)} custom-call(bf16[192,1536]{1,0:T(8,128)(2,1)} %copy-done.18, f32[3,128,128]{2,1,0:T(8,128)} %and_select_fusion.refs_3_.refs_1_, bf16[384,2304]{1,0:T(8,128)(2,1)} %get-tuple-element.54.refs_2_, bf16[384,768]{1,0:T(8,128)(2,1)} %get-tuple-element.61.refs_3_, ...), custom_call_target="tpu_custom_call" | custom-call | flops 69000003584 | tf_op jit(solution)/shard_map/pallas_call | solution.py:1088
  221.5 9.0 %shard_map.217 = (f32[2,192,1920]{2,1,0:T(8,128)}, bf16[384,1920]{1,0:T(8,128)(2,1)}) custom-call(bf16[384,2304]{1,0:T(8,128)(2,1)} %shard_map.216.refs_0_.refs_6_, s32[1]{0:T(128)} %bitcast.refs_0_.refs_1_, bf16[384,768]{1,0:T(8,128)(2,1)} %get-tuple-element.63.refs_2_, bf16[384,4608]{1,0:T(8,128)(2,1)} %get-tuple-element.64.refs_3_.refs_4_, ...), custom_call_target="tpu_custom_call" | custom-call | flops 8049999872 | tf_op jit(solution)/shard_map/pallas_call | solution.py:1024
  230.6 1.9 collective-permute-start.28
  236.4 4.2 %shard_map.218 = bf16[16,3,16,192]{3,2,1,0:T(8,128)(2,1)} custom-call(bf16[384,1920]{1,0:T(8,128)(2,1)} %get-tuple-element.66.refs_0_, s32[3]{0:T(128)} %compare_select_fusion.5.refs_0_.refs_1_, bf16[16,3,16,192]{3,2,1,0:T(8,128)(2,1)} %copy-done.23, bf16[16,3,16,128]{3,2,1,0:T(8,128)(2,1)} %all-to-all-done.2.refs_3_), custom_call_target="tpu_custom_call" | custom-call | flops 1150000000 | tf_op jit(solution)/shard_map/pallas_call | solution.py:1105
  240.6 4.7 %all-to-all-start.3 = ((bf16[16,3,16,192]{3,2,1,0:T(8,128)(2,1)}), bf16[16,3,16,192]{3,2,1,0:T(8,128)(2,1)S(1)}, u32[]{:S(2)}, u32[]{:S(2)}) async-start(bf16[16,3,16,192]{3,2,1,0:T(8,128)(2,1)} %shard_map.218), calls=%async_computation.3 | async-start | bytes 786432 | tf_op jit(solution)/shard_map/all_to_all | solution.py:932
  246.1 1.9 collective-permute-start.42
  248.0 2.4 collective-permute-start.43
  250.4 1.8 collective-permute-done.28
  252.2 1.7 fusion.6.refs_4_
  255.2 2.8 all-to-all-done.3
  258.7 4.4 %shard_map.219.refs_2_.refs_3_.refs_4_ = bf16[384,2688]{1,0:T(8,128)(2,1)} custom-call(bf16[48,1536]{1,0:T(8,128)(2,1)} %get-tuple-element.103.refs_0_, bf16[48,1536]{1,0:T(8,128)(2,1)} %get-tuple-element.102.refs_1_, bf16[48,1536]{1,0:T(8,128)(2,1)} %copy-done.15, bf16[6,128,768]{2,1,0:T(8,128)(2,1)} %pad_maximum_fusion.refs_3_, ...), custom_call_target="tpu_custom_call" | custom-call | flops 1150000000 | tf_op jit(solution)/shard_map/pallas_call | solution.py:1119
  263.1 9.0 %shard_map.220 = (bf16[384,768]{1,0:T(8,128)(2,1)}, f32[8,768]{1,0:T(8,128)}) custom-call(s32[1]{0:T(128)} %bitcast.refs_0_.refs_1_, bf16[384,768]{1,0:T(8,128)(2,1)} %fusion.7.refs_2_.refs_1_, bf16[384,2688]{1,0:T(8,128)(2,1)} %shard_map.219.refs_2_.refs_3_.refs_4_, f32[384,768]{1,0:T(8,128)} %get-tuple-element.68.refs_3_, f32[1,768]{1,0:T(1,128)} %fusion.3.refs_4_, ...), custom_call_target="tpu_custom_call" | custom-call | flops 46000001024 | tf_op jit(solution)/shard_map/pallas_call | solution.py:1128
  274.9 6.2 %shard_map.221 = (f32[2,192,1152]{2,1,0:T(8,128)}, bf16[400,1152]{1,0:T(8,128)(2,1)}) custom-call(bf16[384,768]{1,0:T(8,128)(2,1)} %get-tuple-element.70.refs_0_, s32[1]{0:T(128)} %bitcast.refs_0_.refs_1_, bf16[384,768]{1,0:T(8,128)(2,1)} %get-tuple-element.47.refs_0_.refs_8_.refs_2_, bf16[384,2688]{1,0:T(8,128)(2,1)} %shard_map.219.refs_2_.refs_3_.refs_4_, ...), custom_call_target="tpu_custom_call" | custom-call | flops 8049999872 | tf_op jit(solution)/shard_map/pallas_call | solution.py:1024
  283.9 10.9 %collective-permute-done.31 = bf16[400,1152]{1,0:T(8,128)(2,1)S(1)} collective-permute-done((bf16[400,1152]{1,0:T(8,128)(2,1)}, bf16[400,1152]{1,0:T(8,128)(2,1)S(1)}, u32[]{:S(2)}, u32[]{:S(2)}) %collective-permute-start.31) | collective-permute-done | bytes 921632 | tf_op jit(solution)/shard_map/ppermute | solution.py:80
  299.3 1.6 collective-permute-start.39
  300.9 1.8 collective-permute-start.40
  304.9 4.2 %collective-permute-start.45 = (f32[24,1536]{1,0:T(8,128)S(1)}, f32[24,1536]{1,0:T(8,128)S(1)}, u32[]{:S(2)}, u32[]{:S(2)}) collective-permute-start(f32[24,1536]{1,0:T(8,128)S(1)} %slice.396), channel_id=1, source_target_pairs={{0,2},{1,3},{2,0},{3,1},{4,6},{5,7},{6,4},{7,5},{8,10},{9,11},{10,... | collective-permute-start | bytes 442376 | tf_op jit(solution)/shard_map/ppermute | solution.py:80
  309.1 5.0 %collective-permute-done.39 = bf16[48,1920]{1,0:T(8,128)(2,1)S(1)} collective-permute-done((bf16[48,1920]{1,0:T(8,128)(2,1)S(1)}, bf16[48,1920]{1,0:T(8,128)(2,1)S(1)}, u32[]{:S(2)}, u32[]{:S(2)}) %collective-permute-start.39) | collective-permute-done | bytes 184352 | tf_op jit(solution)/shard_map/ppermute | solution.py:80
  314.2 3.1 collective-permute-start.41
  321.7 3.0 collective-permute-start.33
  325.2 1.8 collective-permute-start.35
  327.1 3.6 %collective-permute-done.33 = bf16[64,1152]{1,0:T(8,128)(2,1)S(1)} collective-permute-done((bf16[64,1152]{1,0:T(8,128)(2,1)S(1)}, bf16[64,1152]{1,0:T(8,128)(2,1)S(1)}, u32[]{:S(2)}, u32[]{:S(2)}) %collective-permute-start.33) | collective-permute-done | bytes 147488 | tf_op jit(solution)/shard_map/ppermute | solution.py:80
  330.7 7.9 %collective-permute-done.34 = bf16[64,1152]{1,0:T(8,128)(2,1)S(1)} collective-permute-done((bf16[64,1152]{1,0:T(8,128)(2,1)S(1)}, bf16[64,1152]{1,0:T(8,128)(2,1)S(1)}, u32[]{:S(2)}, u32[]{:S(2)}) %collective-permute-start.34) | collective-permute-done | bytes 147488 | tf_op jit(solution)/shard_map/ppermute | solution.py:80
  (252 shorter events, 72.8 us)
Async XLA Ops:
  1.7 5.2 %collective-permute-start = (bf16[24,1152]{1,0:T(8,128)(2,1)S(1)}, bf16[24,1152]{1,0:T(8,128)(2,1)S(1)}, u32[]{:S(2)}, u32[]{:S(2)}) collective-permute-start(bf16[24,1152]{1,0:T(8,128)(2,1)S(1)} %get-tuple-element.120), channel_id=1, source_target_pairs={{0,2},{1,3},{2,0},{3,1},{4,6},{5,7},{6,4},{7,5},{8,10},{9,11},{10,... | collective-permute-start | bytes 165896 | tf_op jit(solution)/shard_map/ppermute | solution.py:80
  5.1 37.9 %collective-permute-start.12 = (bf16[24,3456]{1,0:T(8,128)(2,1)}, bf16[24,3456]{1,0:T(8,128)(2,1)}, u32[]{:S(2)}, u32[]{:S(2)}) collective-permute-start(bf16[24,3456]{1,0:T(8,128)(2,1)} %get-tuple-element.116), channel_id=1, source_target_pairs={{0,2},{1,3},{2,0},{3,1},{4,6},{5,7},{6,4},{7,5},{8,10},{9,11},{10,... | collective-permute-start | bytes 497672 | tf_op jit(solution)/shard_map/ppermute | solution.py:80
  6.9 6.3 %collective-permute-start.1 = (bf16[48,1152]{1,0:T(8,128)(2,1)S(1)}, bf16[48,1152]{1,0:T(8,128)(2,1)S(1)}, u32[]{:S(2)}, u32[]{:S(2)}) collective-permute-start(bf16[48,1152]{1,0:T(8,128)(2,1)S(1)} %pad_maximum_fusion.17), channel_id=1, source_target_pairs={{0,8},{1,9},{2,10},{3,11},{4,12},{5,13},{6,14},{7,15},{8,0},{9,1},... | collective-permute-start | bytes 331784 | tf_op jit(solution)/shard_map/ppermute | solution.py:80
  10.0 11.5 %collective-permute-start.2 = (bf16[48,1152]{1,0:T(8,128)(2,1)S(1)}, bf16[48,1152]{1,0:T(8,128)(2,1)S(1)}, u32[]{:S(2)}, u32[]{:S(2)}) collective-permute-start(bf16[48,1152]{1,0:T(8,128)(2,1)S(1)} %pad_maximum_fusion.17), channel_id=1, source_target_pairs={{0,16},{1,17},{2,18},{3,19},{4,20},{5,21},{6,22},{7,23},{8,24},{9,... | collective-permute-start | bytes 331784 | tf_op jit(solution)/shard_map/ppermute | solution.py:80
  12.6 9.0 %collective-permute-start.3 = (bf16[48,1152]{1,0:T(8,128)(2,1)S(1)}, bf16[48,1152]{1,0:T(8,128)(2,1)S(1)}, u32[]{:S(2)}, u32[]{:S(2)}) collective-permute-start(bf16[48,1152]{1,0:T(8,128)(2,1)S(1)} %pad_maximum_fusion.17), channel_id=1, source_target_pairs={{0,24},{1,25},{2,26},{3,27},{4,28},{5,29},{6,30},{7,31},{8,16},{9,... | collective-permute-start | bytes 331784 | tf_op jit(solution)/shard_map/ppermute | solution.py:80
  21.6 13.1 %collective-permute-start.4 = (bf16[192,1152]{1,0:T(8,128)(2,1)S(1)}, bf16[192,1152]{1,0:T(8,128)(2,1)S(1)}, u32[]{:S(2)}, u32[]{:S(2)}) collective-permute-start(bf16[192,1152]{1,0:T(8,128)(2,1)S(1)} %constant_dynamic-update-slice_fusion.refs_5_.refs_0_.refs_7_), channel_id=1, source_target_pairs={{0,1},{1,0},{2,6},{3,7},{4,5},{5,4},{6,2},{7,3},{8,9},{9,8},{10,14... | collective-permute-start | bytes 1327112 | tf_op jit(solution)/shard_map/ppermute | solution.py:80
  24.9 13.2 %collective-permute-start.5 = (bf16[192,1152]{1,0:T(8,128)(2,1)S(1)}, bf16[192,1152]{1,0:T(8,128)(2,1)S(1)}, u32[]{:S(2)}, u32[]{:S(2)}) collective-permute-start(bf16[192,1152]{1,0:T(8,128)(2,1)S(1)} %constant_dynamic-update-slice_fusion.refs_5_.refs_0_.refs_7_), channel_id=1, source_target_pairs={{0,4},{1,5},{2,3},{3,2},{4,0},{5,1},{6,7},{7,6},{8,12},{9,13},{10,... | collective-permute-start | bytes 1327112 | tf_op jit(solution)/shard_map/ppermute | solution.py:80
  34.7 8.3 %collective-permute-start.6 = (bf16[192,1152]{1,0:T(8,128)(2,1)S(1)}, bf16[192,1152]{1,0:T(8,128)(2,1)S(1)}, u32[]{:S(2)}, u32[]{:S(2)}) collective-permute-start(bf16[192,1152]{1,0:T(8,128)(2,1)S(1)} %collective-permute-done.4.refs_6_.refs_8_), channel_id=1, source_target_pairs={{0,4},{1,5},{2,3},{3,2},{4,0},{5,1},{6,7},{7,6},{8,12},{9,13},{10,... | collective-permute-start | bytes 1327112 | tf_op jit(solution)/shard_map/ppermute | solution.py:80
  37.6 8.5 %collective-permute-start.7 = (bf16[192,1152]{1,0:T(8,128)(2,1)S(1)}, bf16[192,1152]{1,0:T(8,128)(2,1)S(1)}, u32[]{:S(2)}, u32[]{:S(2)}) collective-permute-start(bf16[192,1152]{1,0:T(8,128)(2,1)S(1)} %constant_dynamic-update-slice_fusion.refs_5_.refs_0_.refs_7_), channel_id=1, source_target_pairs={{0,2},{1,3},{2,0},{3,1},{4,6},{5,7},{6,4},{7,5},{8,10},{9,11},{10,... | collective-permute-start | bytes 1327112 | tf_op jit(solution)/shard_map/ppermute | solution.py:80
  37.6 10.3 %collective-permute-start.8 = (bf16[192,1152]{1,0:T(8,128)(2,1)S(1)}, bf16[192,1152]{1,0:T(8,128)(2,1)}, u32[]{:S(2)}, u32[]{:S(2)}) collective-permute-start(bf16[192,1152]{1,0:T(8,128)(2,1)S(1)} %collective-permute-done.4.refs_6_.refs_8_), channel_id=1, source_target_pairs={{0,2},{1,3},{2,0},{3,1},{4,6},{5,7},{6,4},{7,5},{8,10},{9,11},{10,... | collective-permute-start | bytes 1327112 | tf_op jit(solution)/shard_map/ppermute | solution.py:80
  38.1 12.4 %collective-permute-start.9 = (bf16[192,1152]{1,0:T(8,128)(2,1)S(1)}, bf16[192,1152]{1,0:T(8,128)(2,1)}, u32[]{:S(2)}, u32[]{:S(2)}) collective-permute-start(bf16[192,1152]{1,0:T(8,128)(2,1)S(1)} %collective-permute-done.5.refs_7_.refs_9_), channel_id=1, source_target_pairs={{0,2},{1,3},{2,0},{3,1},{4,6},{5,7},{6,4},{7,5},{8,10},{9,11},{10,... | collective-permute-start | bytes 1327112 | tf_op jit(solution)/shard_map/ppermute | solution.py:80
  43.0 7.6 %collective-permute-start.10 = (bf16[192,1152]{1,0:T(8,128)(2,1)S(1)}, bf16[192,1152]{1,0:T(8,128)(2,1)}, u32[]{:S(2)}, u32[]{:S(2)}) collective-permute-start(bf16[192,1152]{1,0:T(8,128)(2,1)S(1)} %collective-permute-done.6.refs_8_.refs_10_), channel_id=1, source_target_pairs={{0,2},{1,3},{2,0},{3,1},{4,6},{5,7},{6,4},{7,5},{8,10},{9,11},{10,... | collective-permute-start | bytes 1327112 | tf_op jit(solution)/shard_map/ppermute | solution.py:80
  44.8 16.9 %collective-permute-start.13 = (bf16[48,3456]{1,0:T(8,128)(2,1)}, bf16[48,3456]{1,0:T(8,128)(2,1)S(1)}, u32[]{:S(2)}, u32[]{:S(2)}) collective-permute-start(bf16[48,3456]{1,0:T(8,128)(2,1)} %shard_map.207.refs_1_), channel_id=1, source_target_pairs={{0,8},{1,9},{2,10},{3,11},{4,12},{5,13},{6,14},{7,15},{8,0},{9,1},... | collective-permute-start | bytes 995336 | tf_op jit(solution)/shard_map/ppermute | solution.py:80
  46.1 26.0 %collective-permute-start.14 = (bf16[48,3456]{1,0:T(8,128)(2,1)}, bf16[48,3456]{1,0:T(8,128)(2,1)S(1)}, u32[]{:S(2)}, u32[]{:S(2)}) collective-permute-start(bf16[48,3456]{1,0:T(8,128)(2,1)} %shard_map.207.refs_1_), channel_id=1, source_target_pairs={{0,16},{1,17},{2,18},{3,19},{4,20},{5,21},{6,22},{7,23},{8,24},{9,... | collective-permute-start | bytes 995336 | tf_op jit(solution)/shard_map/ppermute | solution.py:80
  47.9 24.2 %collective-permute-start.15 = (bf16[48,3456]{1,0:T(8,128)(2,1)}, bf16[48,3456]{1,0:T(8,128)(2,1)}, u32[]{:S(2)}, u32[]{:S(2)}) collective-permute-start(bf16[48,3456]{1,0:T(8,128)(2,1)} %shard_map.207.refs_1_), channel_id=1, source_target_pairs={{0,24},{1,25},{2,26},{3,27},{4,28},{5,29},{6,30},{7,31},{8,16},{9,... | collective-permute-start | bytes 995336 | tf_op jit(solution)/shard_map/ppermute | solution.py:80
  75.2 28.3 %collective-permute-start.16 = (bf16[192,3456]{1,0:T(8,128)(2,1)}, bf16[192,3456]{1,0:T(8,128)(2,1)}, u32[]{:S(2)}, u32[]{:S(2)}) collective-permute-start(bf16[192,3456]{1,0:T(8,128)(2,1)} %shard_map.208.refs_1_), channel_id=1, source_target_pairs={{0,1},{1,0},{2,6},{3,7},{4,5},{5,4},{6,2},{7,3},{8,9},{9,8},{10,14... | collective-permute-start | bytes 3981320 | tf_op jit(solution)/shard_map/ppermute | solution.py:80
  76.9 22.2 %all-to-all-start = ((bf16[16,3,16,192]{3,2,1,0:T(8,128)(2,1)}), bf16[16,3,16,192]{3,2,1,0:T(8,128)(2,1)S(1)}, u32[]{:S(2)}, u32[]{:S(2)}) async-start(bf16[16,3,16,192]{3,2,1,0:T(8,128)(2,1)} %bitcast.7), calls=%async_computation | async-start | bytes 786432 | tf_op jit(solution)/shard_map/all_to_all | solution.py:929
  107.0 27.3 %collective-permute-start.17 = (bf16[384,1920]{1,0:T(8,128)(2,1)}, bf16[384,1920]{1,0:T(8,128)(2,1)S(1)}, u32[]{:S(2)}, u32[]{:S(2)}) collective-permute-start(bf16[384,1920]{1,0:T(8,128)(2,1)} %get-tuple-element.48.refs_6_.refs_15_), channel_id=1, source_target_pairs={{0,4},{1,5},{2,3},{3,2},{4,0},{5,1},{6,7},{7,6},{8,12},{9,13},{10,... | collective-permute-start | bytes 4423688 | tf_op jit(solution)/shard_map/ppermute | solution.py:80
  107.2 21.4 %all-to-all-start.1 = ((bf16[16,3,16,128]{3,2,1,0:T(8,128)(2,1)}), bf16[16,3,16,128]{3,2,1,0:T(8,128)(2,1)S(1)}, u32[]{:S(2)}, u32[]{:S(2)}) async-start(bf16[16,3,16,128]{3,2,1,0:T(8,128)(2,1)} %shard_map.205.refs_0_), calls=%async_computation.1 | async-start | bytes 393216 | tf_op jit(solution)/shard_map/all_to_all | solution.py:932
  114.4 3.9 %collective-permute-start.11 = (f32[15,128]{1,0:T(8,128)S(1)}, f32[15,128]{1,0:T(8,128)S(1)}, u32[]{:S(2)}, u32[]{:S(2)}) collective-permute-start(f32[15,128]{1,0:T(8,128)S(1)} %maximum_bitcast_fusion.2), channel_id=1, source_target_pairs={{0,1},{1,0},{2,3},{3,2},{4,5},{5,4},{6,7},{7,6},{8,9},{9,8},{10,11... | collective-permute-start | bytes 23048 | tf_op jit(solution)/shard_map/ppermute | solution.py:80
  134.2 6.1 %collective-permute-start.18 = (bf16[384,1920]{1,0:T(8,128)(2,1)}, bf16[384,1920]{1,0:T(8,128)(2,1)}, u32[]{:S(2)}, u32[]{:S(2)}) collective-permute-start(bf16[384,1920]{1,0:T(8,128)(2,1)} %get-tuple-element.48.refs_6_.refs_15_), channel_id=1, source_target_pairs={{0,2},{1,3},{2,0},{3,1},{4,6},{5,7},{6,4},{7,5},{8,10},{9,11},{10,... | collective-permute-start | bytes 4423688 | tf_op jit(solution)/shard_map/ppermute | solution.py:80
  135.5 4.8 %collective-permute-start.19 = (bf16[384,1920]{1,0:T(8,128)(2,1)}, bf16[384,1920]{1,0:T(8,128)(2,1)S(1)}, u32[]{:S(2)}, u32[]{:S(2)}) collective-permute-start(bf16[384,1920]{1,0:T(8,128)(2,1)} %shard_map.210.refs_7_.refs_16_), channel_id=1, source_target_pairs={{0,2},{1,3},{2,0},{3,1},{4,6},{5,7},{6,4},{7,5},{8,10},{9,11},{10,... | collective-permute-start | bytes 4423688 | tf_op jit(solution)/shard_map/ppermute | solution.py:80
  139.6 17.6 %collective-permute-start.20 = (bf16[384,1536]{1,0:T(8,128)(2,1)}, bf16[384,1536]{1,0:T(8,128)(2,1)S(1)}, u32[]{:S(2)}, u32[]{:S(2)}) collective-permute-start(bf16[384,1536]{1,0:T(8,128)(2,1)} %get-tuple-element.51.refs_4_.refs_19_), channel_id=1, source_target_pairs={{0,4},{1,5},{2,3},{3,2},{4,0},{5,1},{6,7},{7,6},{8,12},{9,13},{10,... | collective-permute-start | bytes 3538952 | tf_op jit(solution)/shard_map/ppermute | solution.py:80
  139.9 20.6 %collective-permute-start.21 = (bf16[384,1536]{1,0:T(8,128)(2,1)}, bf16[384,1536]{1,0:T(8,128)(2,1)}, u32[]{:S(2)}, u32[]{:S(2)}) collective-permute-start(bf16[384,1536]{1,0:T(8,128)(2,1)} %get-tuple-element.51.refs_4_.refs_19_), channel_id=1, source_target_pairs={{0,2},{1,3},{2,0},{3,1},{4,6},{5,7},{6,4},{7,5},{8,10},{9,11},{10,... | collective-permute-start | bytes 3538952 | tf_op jit(solution)/shard_map/ppermute | solution.py:80
  160.4 11.4 %collective-permute-start.24 = (bf16[384,3456]{1,0:T(8,128)(2,1)S(1)}, bf16[384,3456]{1,0:T(8,128)(2,1)S(1)}, u32[]{:S(2)}, u32[]{:S(2)}) collective-permute-start(bf16[384,3456]{1,0:T(8,128)(2,1)S(1)} %copy-done.4), channel_id=1, source_target_pairs={{0,2},{1,3},{2,0},{3,1},{4,6},{5,7},{6,4},{7,5},{8,10},{9,11},{10,... | collective-permute-start | bytes 7962632 | tf_op jit(solution)/shard_map/ppermute | solution.py:80
  170.3 62.2 %collective-permute-start.23 = (bf16[3,128,768]{2,1,0:T(8,128)(2,1)}, bf16[3,128,768]{2,1,0:T(8,128)(2,1)}, u32[]{:S(2)}, u32[]{:S(2)}) collective-permute-start(bf16[3,128,768]{2,1,0:T(8,128)(2,1)} %bitcast.77), channel_id=1, source_target_pairs={{0,1},{1,0},{2,3},{3,2},{4,5},{5,4},{6,7},{7,6},{8,9},{9,8},{10,11... | collective-permute-start | bytes 1769480 | tf_op jit(solution)/shard_map/ppermute | solution.py:80
  180.5 32.6 %collective-permute-start.25 = (bf16[384,1536]{1,0:T(8,128)(2,1)}, bf16[384,1536]{1,0:T(8,128)(2,1)S(1)}, u32[]{:S(2)}, u32[]{:S(2)}) collective-permute-start(bf16[384,1536]{1,0:T(8,128)(2,1)} %get-tuple-element.53.refs_0_), channel_id=1, source_target_pairs={{0,4},{1,5},{2,3},{3,2},{4,0},{5,1},{6,7},{7,6},{8,12},{9,13},{10,... | collective-permute-start | bytes 3538952 | tf_op jit(solution)/shard_map/ppermute | solution.py:80
  202.6 18.9 %collective-permute-start.27 = (bf16[384,4608]{1,0:T(8,128)(2,1)}, bf16[384,4608]{1,0:T(8,128)(2,1)}, u32[]{:S(2)}, u32[]{:S(2)}) collective-permute-start(bf16[384,4608]{1,0:T(8,128)(2,1)} %get-tuple-element.64.refs_3_.refs_4_), channel_id=1, source_target_pairs={{0,2},{1,3},{2,0},{3,1},{4,6},{5,7},{6,4},{7,5},{8,10},{9,11},{10,... | collective-permute-start | bytes 10616840 | tf_op jit(solution)/shard_map/ppermute | solution.py:80
  202.7 33.7 %all-to-all-start.2 = ((bf16[16,3,16,128]{3,2,1,0:T(8,128)(2,1)}), bf16[16,3,16,128]{3,2,1,0:T(8,128)(2,1)}, u32[]{:S(2)}, u32[]{:S(2)}) async-start(bf16[16,3,16,128]{3,2,1,0:T(8,128)(2,1)} %bitcast.80), calls=%async_computation.2 | async-start | bytes 393216 | tf_op jit(solution)/shard_map/all_to_all | solution.py:929
  213.3 21.5 %collective-permute-start.26 = (bf16[192,1536]{1,0:T(8,128)(2,1)S(1)}, bf16[192,1536]{1,0:T(8,128)(2,1)S(1)}, u32[]{:S(2)}, u32[]{:S(2)}) collective-permute-start(bf16[192,1536]{1,0:T(8,128)(2,1)S(1)} %fusion.10.refs_0_), channel_id=1, source_target_pairs={{0,1},{1,0},{2,6},{3,7},{4,5},{5,4},{6,2},{7,3},{8,9},{9,8},{10,14... | collective-permute-start | bytes 1769480 | tf_op jit(solution)/shard_map/ppermute | solution.py:80
  230.6 21.7 %collective-permute-start.28 = (bf16[384,1920]{1,0:T(8,128)(2,1)}, bf16[384,1920]{1,0:T(8,128)(2,1)}, u32[]{:S(2)}, u32[]{:S(2)}) collective-permute-start(bf16[384,1920]{1,0:T(8,128)(2,1)} %get-tuple-element.66.refs_0_), channel_id=1, source_target_pairs={{0,4},{1,5},{2,3},{3,2},{4,0},{5,1},{6,7},{7,6},{8,12},{9,13},{10,... | collective-permute-start | bytes 4423688 | tf_op jit(solution)/shard_map/ppermute | solution.py:80
  240.6 17.3 %all-to-all-start.3 = ((bf16[16,3,16,192]{3,2,1,0:T(8,128)(2,1)}), bf16[16,3,16,192]{3,2,1,0:T(8,128)(2,1)S(1)}, u32[]{:S(2)}, u32[]{:S(2)}) async-start(bf16[16,3,16,192]{3,2,1,0:T(8,128)(2,1)} %shard_map.218), calls=%async_computation.3 | async-start | bytes 786432 | tf_op jit(solution)/shard_map/all_to_all | solution.py:932
  246.1 53.3 %collective-permute-start.42 = (bf16[48,1536]{1,0:T(8,128)(2,1)}, bf16[48,1536]{1,0:T(8,128)(2,1)}, u32[]{:S(2)}, u32[]{:S(2)}) collective-permute-start(bf16[48,1536]{1,0:T(8,128)(2,1)} %get-tuple-element.103.refs_0_), channel_id=1, source_target_pairs={{0,8},{1,9},{2,10},{3,11},{4,12},{5,13},{6,14},{7,15},{8,0},{9,1},... | collective-permute-start | bytes 442376 | tf_op jit(solution)/shard_map/ppermute | solution.py:80
  248.0 53.0 %collective-permute-start.43 = (bf16[48,1536]{1,0:T(8,128)(2,1)}, bf16[48,1536]{1,0:T(8,128)(2,1)}, u32[]{:S(2)}, u32[]{:S(2)}) collective-permute-start(bf16[48,1536]{1,0:T(8,128)(2,1)} %get-tuple-element.102.refs_1_), channel_id=1, source_target_pairs={{0,16},{1,17},{2,18},{3,19},{4,20},{5,21},{6,22},{7,23},{8,24},{9,... | collective-permute-start | bytes 442376 | tf_op jit(solution)/shard_map/ppermute | solution.py:80
  250.3 52.4 %collective-permute-start.44 = (bf16[48,1536]{1,0:T(8,128)(2,1)S(1)}, bf16[48,1536]{1,0:T(8,128)(2,1)}, u32[]{:S(2)}, u32[]{:S(2)}) collective-permute-start(bf16[48,1536]{1,0:T(8,128)(2,1)S(1)} %get-tuple-element.101.refs_2_), channel_id=1, source_target_pairs={{0,24},{1,25},{2,26},{3,27},{4,28},{5,29},{6,30},{7,31},{8,16},{9,... | collective-permute-start | bytes 442376 | tf_op jit(solution)/shard_map/ppermute | solution.py:80
  254.0 27.1 %collective-permute-start.37 = (bf16[192,1920]{1,0:T(8,128)(2,1)S(1)}, bf16[192,1920]{1,0:T(8,128)(2,1)S(1)}, u32[]{:S(2)}, u32[]{:S(2)}) collective-permute-start(bf16[192,1920]{1,0:T(8,128)(2,1)S(1)} %fusion.6.refs_4_), channel_id=1, source_target_pairs={{0,1},{1,0},{2,6},{3,7},{4,5},{5,4},{6,2},{7,3},{8,9},{9,8},{10,14... | collective-permute-start | bytes 2211848 | tf_op jit(solution)/shard_map/ppermute | solution.py:80
  263.1 10.6 %collective-permute-start.30 = (bf16[384,2688]{1,0:T(8,128)(2,1)}, bf16[384,2688]{1,0:T(8,128)(2,1)}, u32[]{:S(2)}, u32[]{:S(2)}) collective-permute-start(bf16[384,2688]{1,0:T(8,128)(2,1)} %shard_map.219.refs_2_.refs_3_.refs_4_), channel_id=1, source_target_pairs={{0,2},{1,3},{2,0},{3,1},{4,6},{5,7},{6,4},{7,5},{8,10},{9,11},{10,... | collective-permute-start | bytes 6193160 | tf_op jit(solution)/shard_map/ppermute | solution.py:80
  273.7 43.6 %collective-permute-start.29 = (bf16[3,128,768]{2,1,0:T(8,128)(2,1)}, bf16[3,128,768]{2,1,0:T(8,128)(2,1)}, u32[]{:S(2)}, u32[]{:S(2)}) collective-permute-start(bf16[3,128,768]{2,1,0:T(8,128)(2,1)} %bitcast.75), channel_id=1, source_target_pairs={{0,1},{1,0},{2,3},{3,2},{4,5},{5,4},{6,7},{7,6},{8,9},{9,8},{10,11... | collective-permute-start | bytes 1769480 | tf_op jit(solution)/shard_map/ppermute | solution.py:80
  281.1 13.7 %collective-permute-start.31 = (bf16[400,1152]{1,0:T(8,128)(2,1)}, bf16[400,1152]{1,0:T(8,128)(2,1)S(1)}, u32[]{:S(2)}, u32[]{:S(2)}) collective-permute-start(bf16[400,1152]{1,0:T(8,128)(2,1)} %get-tuple-element.74), channel_id=1, source_target_pairs={{0,4},{1,5},{2,3},{3,2},{4,0},{5,1},{6,7},{7,6},{8,12},{9,13},{10,... | collective-permute-start | bytes 2764808 | tf_op jit(solution)/shard_map/ppermute | solution.py:80
  294.8 10.1 %collective-permute-start.38 = (bf16[48,1920]{1,0:T(8,128)(2,1)}, bf16[48,1920]{1,0:T(8,128)(2,1)S(1)}, u32[]{:S(2)}, u32[]{:S(2)}) collective-permute-start(bf16[48,1920]{1,0:T(8,128)(2,1)} %get-tuple-element.98), channel_id=1, source_target_pairs={{0,8},{1,9},{2,10},{3,11},{4,12},{5,13},{6,14},{7,15},{8,0},{9,1},... | collective-permute-start | bytes 552968 | tf_op jit(solution)/shard_map/ppermute | solution.py:80
  299.3 14.8 %collective-permute-start.39 = (bf16[48,1920]{1,0:T(8,128)(2,1)S(1)}, bf16[48,1920]{1,0:T(8,128)(2,1)S(1)}, u32[]{:S(2)}, u32[]{:S(2)}) collective-permute-start(bf16[48,1920]{1,0:T(8,128)(2,1)S(1)} %copy-done.29), channel_id=1, source_target_pairs={{0,16},{1,17},{2,18},{3,19},{4,20},{5,21},{6,22},{7,23},{8,24},{9,... | collective-permute-start | bytes 552968 | tf_op jit(solution)/shard_map/ppermute | solution.py:80
  300.9 13.2 %collective-permute-start.40 = (bf16[48,1920]{1,0:T(8,128)(2,1)S(1)}, bf16[48,1920]{1,0:T(8,128)(2,1)S(1)}, u32[]{:S(2)}, u32[]{:S(2)}) collective-permute-start(bf16[48,1920]{1,0:T(8,128)(2,1)S(1)} %copy-done.28), channel_id=1, source_target_pairs={{0,24},{1,25},{2,26},{3,27},{4,28},{5,29},{6,30},{7,31},{8,16},{9,... | collective-permute-start | bytes 552968 | tf_op jit(solution)/shard_map/ppermute | solution.py:80
  302.8 17.6 %collective-permute-start.32 = (bf16[208,1152]{1,0:T(8,128)(2,1)S(1)}, bf16[208,1152]{1,0:T(8,128)(2,1)S(1)}, u32[]{:S(2)}, u32[]{:S(2)}) collective-permute-start(bf16[208,1152]{1,0:T(8,128)(2,1)S(1)} %pad_maximum_fusion.2), channel_id=1, source_target_pairs={{0,1},{1,0},{2,6},{3,7},{4,5},{5,4},{6,2},{7,3},{8,9},{9,8},{10,14... | collective-permute-start | bytes 1437704 | tf_op jit(solution)/shard_map/ppermute | solution.py:80
  304.9 14.7 %collective-permute-start.45 = (f32[24,1536]{1,0:T(8,128)S(1)}, f32[24,1536]{1,0:T(8,128)S(1)}, u32[]{:S(2)}, u32[]{:S(2)}) collective-permute-start(f32[24,1536]{1,0:T(8,128)S(1)} %slice.396), channel_id=1, source_target_pairs={{0,2},{1,3},{2,0},{3,1},{4,6},{5,7},{6,4},{7,5},{8,10},{9,11},{10,... | collective-permute-start | bytes 442376 | tf_op jit(solution)/shard_map/ppermute | solution.py:80
  314.2 12.9 %collective-permute-start.41 = (f32[24,1920]{1,0:T(8,128)S(1)}, f32[24,1920]{1,0:T(8,128)S(1)}, u32[]{:S(2)}, u32[]{:S(2)}) collective-permute-start(f32[24,1920]{1,0:T(8,128)S(1)} %slice.393), channel_id=1, source_target_pairs={{0,2},{1,3},{2,0},{3,1},{4,6},{5,7},{6,4},{7,5},{8,10},{9,11},{10,... | collective-permute-start | bytes 552968 | tf_op jit(solution)/shard_map/ppermute | solution.py:80
  321.7 9.1 %collective-permute-start.33 = (bf16[64,1152]{1,0:T(8,128)(2,1)S(1)}, bf16[64,1152]{1,0:T(8,128)(2,1)S(1)}, u32[]{:S(2)}, u32[]{:S(2)}) collective-permute-start(bf16[64,1152]{1,0:T(8,128)(2,1)S(1)} %get-tuple-element.124), channel_id=1, source_target_pairs={{0,8},{1,9},{2,10},{3,11},{4,12},{5,13},{6,14},{7,15},{8,0},{9,1},... | collective-permute-start | bytes 442376 | tf_op jit(solution)/shard_map/ppermute | solution.py:80
  324.6 14.0 %collective-permute-start.34 = (bf16[64,1152]{1,0:T(8,128)(2,1)S(1)}, bf16[64,1152]{1,0:T(8,128)(2,1)S(1)}, u32[]{:S(2)}, u32[]{:S(2)}) collective-permute-start(bf16[64,1152]{1,0:T(8,128)(2,1)S(1)} %get-tuple-element.125), channel_id=1, source_target_pairs={{0,16},{1,17},{2,18},{3,19},{4,20},{5,21},{6,22},{7,23},{8,24},{9,... | collective-permute-start | bytes 442376 | tf_op jit(solution)/shard_map/ppermute | solution.py:80
  325.2 13.4 %collective-permute-start.35 = (bf16[64,1152]{1,0:T(8,128)(2,1)S(1)}, bf16[64,1152]{1,0:T(8,128)(2,1)S(1)}, u32[]{:S(2)}, u32[]{:S(2)}) collective-permute-start(bf16[64,1152]{1,0:T(8,128)(2,1)S(1)} %get-tuple-element.126), channel_id=1, source_target_pairs={{0,24},{1,25},{2,26},{3,27},{4,28},{5,29},{6,30},{7,31},{8,16},{9,... | collective-permute-start | bytes 442376 | tf_op jit(solution)/shard_map/ppermute | solution.py:80
  (44 other events, 355.8 us)
